TPU v7x, 32 devices: a whole 2x2x4 slice. The times are simulated.
32 devices in a mesh: section: 2 (over y), dp: 8 (over z, core), tensor: 2 (over x).
Axes of the slice: x: 2, y: 2, z: 4, core: 2. Of those that a mesh axis runs over, the one named last changes fastest.
Arguments:
- section_inputs: bfloat16 [2, 128, 2560], P('section', 'dp', 'tensor'), may hold values from -40 to 40
- entering: bfloat16 [1, 128, 2560], P(None, 'dp', 'tensor'), may hold values from -40 to 40
- grad_outputs: bfloat16 [2, 128, 2560], P('section', 'dp', 'tensor'), may hold values from -6 to 6
- arriving: bfloat16 [1, 128, 2560], P(None, 'dp', 'tensor'), may hold values from -6 to 6
- live_rows: int32 [1], replicated, may hold values from 64 to 128
- stashed_inputs: bfloat16 [2, 2, 128, 2560], P('section', None, 'dp', 'tensor'), may hold values from -40 to 40
- norm_gain: bfloat16 [2, 2560], P('section', 'tensor'), may hold values from 0.25 to 1.75
- up_weight: bfloat16 [2, 2560, 14336], P('section', 'tensor', 'dp'), may hold values from -0.125 to 0.125
- down_weight: bfloat16 [2, 14336, 2560], P('section', 'dp', 'tensor'), may hold values from -0.046875 to 0.046875
- held_blocks: int32 [2, 2, 8, 6], P('section', 'tensor'), may hold values from 0 to 279, as said below
- held_count: int32 [2, 2, 8], P('section', 'tensor'), may hold values from 1 to 6, as said below
- held_owner: int32 [2, 2, 8, 6], P('section', 'tensor'), may hold values from 0 to 7, as said below
- first_moment: float32 [2, 2, 8, 6, 128, 128], P('section', 'tensor', 'dp'), may hold values from -4 to 4
- second_moment: float32 [2, 2, 8, 6, 128, 128], P('section', 'tensor', 'dp'), may hold values from 0.01 to 1
Outputs:
- section_outputs: bfloat16 [2, 2, 128, 2560], P('section', None, 'dp', 'tensor')
- input_grads: bfloat16 [2, 2, 128, 2560], P('section', None, 'dp', 'tensor')
- first_next: float32 [2, 2, 8, 6, 128, 128], P('section', 'tensor', 'dp')
- second_next: float32 [2, 2, 8, 6, 128, 128], P('section', 'tensor', 'dp')
- update_direction: float32 [2, 2, 8, 6, 128, 128], P('section', 'tensor', 'dp')
Inputs may be any that keep to these rules, and one draw needn't show every extreme that they name: `held_blocks`: A number below 140 names a block of the device's up projection share, row-major over 10 x 14 blocks; the others, less 140, a block of its down projection share, row-major over 14 x 10 blocks. A device's first held_count entries are distinct; later entries are not used. `held_count`: some device of each section and tensor index lists 6 trainable blocks. `held_owner`: the owners of one device's trainable blocks are distinct and never the device itself. Each dp index owns at most 6 blocks of one section and tensor index, and some owns exactly 6.
All inputs are finite; a program needn't handle non-finite values.
Results may differ from a plain program's by a relative error of at most 0.015.
Values may be sent and summed in bfloat16 or wider, within the bound.
No kernel may reach another device: no remote copies, remote signals or barrier semaphores. Data moves between devices by JAX's collectives and lax.ppermute only.
A program may use at most 64 MiB of HBM per device.

v0:
```python
import jax
import jax.numpy as jnp
from jax import lax
from jax.sharding import PartitionSpec as P

DW = 2560
BLK = 128


EPSILON = 1e-06


def from_behind(value, axis, steps):
    count = lax.axis_size(axis)
    leading, last = (max(0, -steps), min(count, count - steps))
    return lax.ppermute(value, axis, [(source, source + steps) for source in range(leading, last)])


def normed_product(rows_all, gain_row, up_matrix):
    widened = rows_all.astype(jnp.float32)
    squares = jnp.sum(widened * widened, axis=1)
    normed = (widened * gain_row.astype(jnp.float32)).astype(jnp.bfloat16)
    product = jnp.dot(normed, up_matrix, preferred_element_type=jnp.float32)
    return (normed, squares, product)


def scales_of(squares):
    return lax.rsqrt(squares / DW + EPSILON)


def activate(hidden):
    return (hidden * jax.nn.sigmoid(hidden)).astype(jnp.bfloat16)


def hidden_backward(hidden, act_grad, row_scales, product):
    sigmoid_part = jax.nn.sigmoid(hidden)
    hidden_grad = act_grad * sigmoid_part * (1.0 + hidden * (1.0 - sigmoid_part))
    scaled_grad = (hidden_grad * row_scales[:, None]).astype(jnp.bfloat16)
    scale_grad = jnp.sum(hidden_grad * product, axis=1)
    return (scaled_grad, scale_grad)


def times_transposed(left, right):
    return lax.dot_general(
        left, right, (((1,), (1,)), ((), ())), preferred_element_type=jnp.float32
    )


def body(
    section_inputs,
    entering,
    grad_outputs,
    arriving,
    live_rows,
    stashed_inputs,
    norm_gain,
    up_weight,
    down_weight,
    held_blocks,
    held_count,
    held_owner,
    first_moment,
    second_moment,
):
    section_count = lax.axis_size("section")
    section_index = lax.axis_index("section")
    dp_index = lax.axis_index("dp")
    dp_count = lax.axis_size("dp")
    turn_count = stashed_inputs.shape[1]
    local_rows = section_inputs.shape[1]
    row_total = local_rows * dp_count
    gain_row = norm_gain[0]
    up_matrix = up_weight[0]
    down_matrix = down_weight[0]
    channel_blocks = up_matrix.shape[0] // BLK
    hidden_blocks = up_matrix.shape[1] // BLK
    up_count = channel_blocks * hidden_blocks
    capacity = held_owner.shape[3]
    row_start = dp_index * local_rows
    held_list = lax.dynamic_index_in_dim(held_blocks[0, 0], dp_index, 0, keepdims=False)
    down_number = held_list - up_count
    is_up = held_list < up_count
    left_index = jnp.where(
        is_up, held_list // hidden_blocks, channel_blocks + down_number // channel_blocks
    )
    right_index = jnp.where(
        is_up, held_list % hidden_blocks, hidden_blocks + down_number % channel_blocks
    )
    forward_results = []
    rows_in = section_inputs[0]
    for turn in range(turn_count):
        if turn > 0:
            passed_rows = from_behind(forward_results[-1], "section", 1)
            rows_in = jnp.where(section_index == 0, entering[turn - 1], passed_rows)
        forward_rows_all = lax.all_gather(rows_in, "dp", axis=0, tiled=True)
        forward_normed, forward_squares, forward_product = normed_product(
            forward_rows_all, gain_row, up_matrix
        )
        forward_product, forward_squares = (
            lax.psum(forward_product.astype(jnp.bfloat16), "tensor").astype(jnp.float32),
            lax.psum(forward_squares.astype(jnp.bfloat16), "tensor").astype(jnp.float32),
        )
        forward_activated = activate(forward_product * scales_of(forward_squares)[:, None])
        mixed_rows = lax.psum_scatter(
            jnp.dot(forward_activated, down_matrix, preferred_element_type=jnp.float32).astype(
                jnp.bfloat16
            ),
            "dp",
            scatter_dimension=0,
            tiled=True,
        ).astype(jnp.float32)
        forward_results.append((rows_in.astype(jnp.float32) + mixed_rows).astype(jnp.bfloat16))
    row_ids = row_start + lax.iota(jnp.int32, local_rows)
    backward_results = []
    kept_grads = jnp.zeros((capacity, BLK, BLK), jnp.float32)
    grads_in = grad_outputs[0]
    for turn in range(turn_count):
        if turn > 0:
            passed_grads = from_behind(backward_results[-1], "section", -1)
            masked = jnp.where(
                (row_ids < live_rows[turn - 1])[:, None],
                arriving[turn - 1],
                jnp.zeros_like(arriving[turn - 1]),
            )
            grads_in = jnp.where(section_index == section_count - 1, masked, passed_grads)
        rows_local = stashed_inputs[0, turn]
        rows_all = lax.all_gather(rows_local, "dp", axis=0, tiled=True)
        grads_all = lax.all_gather(grads_in, "dp", axis=0, tiled=True)
        normed, squares, product = normed_product(rows_all, gain_row, up_matrix)
        act_grad = times_transposed(grads_all, down_matrix)
        product, squares, act_grad = lax.psum((product, squares, act_grad), "tensor")
        row_scales = scales_of(squares)
        hidden = product * row_scales[:, None]
        activated = activate(hidden)
        scaled_grad, scale_grad = hidden_backward(hidden, act_grad, row_scales, product)
        normed_part = times_transposed(scaled_grad, up_matrix)
        normed_grad = lax.psum_scatter(normed_part, "dp", scatter_dimension=0, tiled=True)
        scale_grad_rows = lax.psum_scatter(scale_grad, "dp", scatter_dimension=0, tiled=True)
        scale_rows = lax.dynamic_slice_in_dim(row_scales, row_start, local_rows, 0)
        widened = rows_local.astype(jnp.float32)
        input_grad = (
            grads_in.astype(jnp.float32)
            + normed_grad * gain_row.astype(jnp.float32)
            - (scale_grad_rows * scale_rows**3)[:, None] * widened / DW
        )
        left_table = jnp.concatenate(
            [
                normed.reshape(row_total, channel_blocks, BLK),
                activated.reshape(row_total, hidden_blocks, BLK),
            ],
            axis=1,
        )
        right_table = jnp.concatenate(
            [
                scaled_grad.reshape(row_total, hidden_blocks, BLK),
                grads_all.reshape(row_total, channel_blocks, BLK),
            ],
            axis=1,
        )
        left_pick = jnp.take(left_table, left_index, axis=1)
        right_pick = jnp.take(right_table, right_index, axis=1)
        block_grads = jnp.einsum(
            "rkb,rkc->kbc", left_pick, right_pick, preferred_element_type=jnp.float32
        )
        result, block_grads = (input_grad.astype(jnp.bfloat16), block_grads)
        backward_results.append(result)
        kept_grads = kept_grads + block_grads
    counts = held_count[0, 0]
    owners = held_owner[0, 0]
    slot_ids = lax.iota(jnp.int32, capacity)
    dp_ids = lax.iota(jnp.int32, dp_count)
    live_slots = slot_ids[None, :] < counts[:, None]
    chosen = (owners[:, None, :] == dp_ids[None, :, None]) & live_slots[:, None, :]
    is_sent = jnp.any(chosen, axis=2)
    slot_pick = jnp.sum(jnp.where(chosen, slot_ids[None, None, :], 0), axis=2)
    mine_sent = lax.dynamic_index_in_dim(is_sent, dp_index, 0, keepdims=False)
    mine_pick = lax.dynamic_index_in_dim(slot_pick, dp_index, 0, keepdims=False)
    outgoing = jnp.where(mine_sent[:, None, None], jnp.take(kept_grads, mine_pick, axis=0), 0.0)
    arrived = lax.all_to_all(outgoing, "dp", split_axis=0, concat_axis=0, tiled=True)
    from_source = lax.dynamic_index_in_dim(is_sent, dp_index, 1, keepdims=False)
    source_count = from_source.astype(jnp.int32)
    ranks = jnp.cumsum(source_count) - source_count
    matches = from_source[None, :] & (ranks[None, :] == slot_ids[:, None])
    is_filled = jnp.any(matches, axis=1)
    source_ids = jnp.sum(jnp.where(matches, dp_ids[None, :], 0), axis=1)
    owned_grads = jnp.where(is_filled[:, None, None], jnp.take(arrived, source_ids, axis=0), 0.0)
    filled = is_filled[:, None, None]
    first_new = 0.9 * first_moment[0, 0, 0] + 0.1 * owned_grads
    second_new = 0.999 * second_moment[0, 0, 0] + 0.001 * owned_grads * owned_grads
    direction = first_new / (jnp.sqrt(second_new) + 1e-08)
    first_out = jnp.where(filled, first_new, 0.0)
    second_out = jnp.where(filled, second_new, 0.0)
    direction_out = jnp.where(filled, direction, 0.0)
    section_rows = jnp.stack(forward_results)
    grad_rows = jnp.stack(backward_results)
    return (
        section_rows[None],
        grad_rows[None],
        first_out[None, None, None],
        second_out[None, None, None],
        direction_out[None, None, None],
    )


def solution(mesh):
    return jax.shard_map(
        body,
        mesh=mesh,
        in_specs=(
            P("section", "dp", "tensor"),
            P(None, "dp", "tensor"),
            P("section", "dp", "tensor"),
            P(None, "dp", "tensor"),
            P(),
            P("section", None, "dp", "tensor"),
            P("section", "tensor"),
            P("section", "tensor", "dp"),
            P("section", "dp", "tensor"),
            P("section", "tensor", None, None),
            P("section", "tensor", None),
            P("section", "tensor", None, None),
            P("section", "tensor", "dp", None, None, None),
            P("section", "tensor", "dp", None, None, None),
        ),
        out_specs=(
            P("section", None, "dp", "tensor"),
            P("section", None, "dp", "tensor"),
            P("section", "tensor", "dp", None, None, None),
            P("section", "tensor", "dp", None, None, None),
            P("section", "tensor", "dp", None, None, None),
        ),
        check_vma=False,
    )
```

profile of v0, /device:TPU:0, one launch (start us, length us, event | category | flops | bytes accessed | tf_op | source)
XLA Modules:
  0.0 372.6 jit_solution(7429662772647763059)
XLA Ops:
  7.2 0.7 convert_reduce_fusion
  7.9 16.2 %all-gather = bf16[1,128,1280]{2,1,0:T(8,128)(2,1)S(1)} all-gather(bf16[1,16,1280]{2,1,0:T(8,128)(2,1)} %param.16), channel_id=2, replica_groups=mesh['section'=2,'dp'=8,'tensor'=2] {'dp'}, dimensions={1}, use_global_device_ids=true | all-gather | bytes 368640 | tf_op jit(solution)/shard_map/all_gather | solution.py:95
  24.2 3.9 %fusion.20 = bf16[128,1792]{1,0:T(8,128)(2,1)} fusion(bf16[1,1280,1792]{2,1,0:T(8,128)(2,1)} %param.23, bf16[1,128,1280]{2,1,0:T(8,128)(2,1)S(1)} %all-gather, f32[1280]{0:T(1024)S(1)} %convert_reduce_fusion), kind=kOutput, calls=%fused_computation.26 | convolution fusion | flops 587923456 | bytes 5379072 | tf_op jit(solution)/shard_map/dot_general | solution.py:23
  28.1 14.5 %all-gather.2 = bf16[1,1,128,1280]{3,2,1,0:T(8,128)(2,1)S(1)} all-gather(bf16[1,1,16,1280]{3,2,1,0:T(8,128)(2,1)S(1)} %get-tuple-element.36), channel_id=4, replica_groups=mesh['section'=2,'dp'=8,'tensor'=2] {'dp'}, dimensions={2}, use_global_device_ids=true | all-gather | bytes 368640 | tf_op jit(solution)/shard_map/all_gather | solution.py:127
  42.6 14.3 %all-gather.3 = bf16[1,1,128,1280]{3,2,1,0:T(8,128)(2,1)S(1)} all-gather(bf16[1,1,16,1280]{3,2,1,0:T(8,128)(2,1)S(1)} %get-tuple-element.37), channel_id=5, replica_groups=mesh['section'=2,'dp'=8,'tensor'=2] {'dp'}, dimensions={2}, use_global_device_ids=true | all-gather | bytes 368640 | tf_op jit(solution)/shard_map/all_gather | solution.py:127
  57.2 4.0 %fusion.14 = f32[128,1792]{1,0:T(8,128)} fusion(bf16[128,1280]{1,0:T(8,128)(2,1)S(1)} %get-tuple-element.39, bf16[1,1280,1792]{2,1,0:T(8,128)(2,1)} %param.23), kind=kOutput, calls=%fused_computation.20 | convolution fusion | flops 587202560 | bytes 5832704 | tf_op jit(solution)/shard_map/dot_general | solution.py:23
  61.2 14.5 %all-gather.1 = bf16[1,128,1280]{2,1,0:T(8,128)(2,1)S(1)} all-gather(bf16[1,16,1280]{2,1,0:T(8,128)(2,1)S(1)} %copy-done.7), channel_id=3, replica_groups=mesh['section'=2,'dp'=8,'tensor'=2] {'dp'}, dimensions={1}, use_global_device_ids=true | all-gather | bytes 368640 | tf_op jit(solution)/shard_map/all_gather | solution.py:128
  75.7 2.6 fusion.2
  79.1 4.9 %psum.71 = bf16[128]{0:T(256)(128)(2,1)S(1)} all-reduce(bf16[128]{0:T(256)(128)(2,1)S(1)} %fusion.35), channel_id=1, replica_groups=mesh['section'=2,'dp'=8,'tensor'=2] {'tensor'}, use_global_device_ids=true, to_apply=%region_2.3 | all-reduce | flops 128 | bytes 512 | tf_op jit(solution)/shard_map/psum | solution.py:101
  84.0 4.9 %all-reduce.2 = (f32[128]{0:T(128)S(1)}, f32[128]{0:T(128)S(1)}) all-reduce(f32[128]{0:T(128)S(1)} %get-tuple-element.33, f32[128]{0:T(128)S(1)} %get-tuple-element.38), channel_id=1, replica_groups=mesh['section'=2,'dp'=8,'tensor'=2] {'tensor'}, use_global_device_ids=true, to_apply=%region_18.19 | all-reduce | flops 256 | bytes 2048 | tf_op jit(solution)/shard_map/psum | solution.py:131
  89.7 4.0 %fusion.10 = f32[128,1792]{1,0:T(8,128)} fusion(bf16[128,1280]{1,0:T(8,128)(2,1)S(1)} %get-tuple-element.32, bf16[1,1280,1792]{2,1,0:T(8,128)(2,1)} %param.23), kind=kOutput, calls=%fused_computation.16 | convolution fusion | flops 587202560 | bytes 5832704 | tf_op jit(solution)/shard_map/dot_general | solution.py:23
  93.7 4.1 %fusion.26 = bf16[128,1280]{1,0:T(8,128)(2,1)} fusion(bf16[1,1792,1280]{2,1,0:T(8,128)(2,1)} %param.24, bf16[128,1792]{1,0:T(8,128)(2,1)} %all-reduce.10.cloned.1.call-done, f32[128]{0:T(128)S(1)} %add_rsqrt_fusion.3), kind=kOutput, calls=%fused_computation.28 | convolution fusion | flops 588972032 | bytes 5374464 | tf_op jit(solution)/shard_map/dot_general | solution.py:105
  97.9 39.3 %all-reduce.16.cloned.1.call-done = (f32[128,1792]{1,0:T(8,128)}, f32[128,1792]{1,0:T(8,128)}) async-done(((f32[128,1792]{1,0:T(8,128)}, f32[128,1792]{1,0:T(8,128)}), (f32[128,1792]{1,0:T(8,128)}, f32[128,1792]{1,0:T(8,128)})) %all-reduce.16.cloned.1.call-update) | async-done | bytes 1835024 | tf_op jit(solution)/shard_map/psum | solution.py:131
  137.2 2.1 multiply_reduce_fusion.1
  139.3 4.8 %fusion.12 = f32[128,1280]{1,0:T(8,128)} fusion(bf16[128,1792]{1,0:T(8,128)(2,1)S(1)} %get-tuple-element.26, bf16[1,1280,1792]{2,1,0:T(8,128)(2,1)} %param.23), kind=kOutput, calls=%fused_computation.18 | convolution fusion | flops 587202560 | bytes 5701632 | tf_op jit(solution)/shard_map/dot_general | solution.py:44
  145.4 25.2 %reduce-scatter.5.cloned.1.call-done = bf16[16,1280]{1,0:T(8,128)(2,1)} async-done(((bf16[128,1280]{1,0:T(8,128)(2,1)}), bf16[16,1280]{1,0:T(8,128)(2,1)}) %reduce-scatter.5.cloned.1.call-update) | async-done | bytes 40976 | tf_op jit(solution)/shard_map/reduce_scatter | solution.py:104
  170.6 0.8 fusion.73
  171.3 3.4 collective-permute-start
  176.4 14.9 %all_gather.19 = bf16[128,1280]{1,0:T(8,128)(2,1)S(1)} all-gather(bf16[16,1280]{1,0:T(8,128)(2,1)S(1)} %bitcast_select_fusion.2), channel_id=1, replica_groups=mesh['section'=2,'dp'=8,'tensor'=2] {'dp'}, dimensions={0}, use_global_device_ids=true | all-gather | bytes 368640 | tf_op jit(solution)/shard_map/all_gather | solution.py:95
  191.3 13.9 %all-reduce = f32[128]{0:T(128)S(1)} all-reduce(f32[128]{0:T(128)S(1)} %get-tuple-element.25), channel_id=9, replica_groups=mesh['section'=2,'dp'=8,'tensor'=2] {'dp'}, use_global_device_ids=true, to_apply=%region_14.15.clone | all-reduce | flops 128 | bytes 1024
  205.3 1.0 fusion.72
  206.3 1.3 collective-permute-start.1
  207.6 3.9 %fusion.23 = bf16[128,1792]{1,0:T(8,128)(2,1)} fusion(bf16[1,1280,1792]{2,1,0:T(8,128)(2,1)} %param.23, bf16[128,1280]{1,0:T(8,128)(2,1)S(1)} %all_gather.19, f32[1280]{0:T(1024)S(1)} %convert_reduce_fusion), kind=kOutput, calls=%fused_computation.27 | convolution fusion | flops 587923456 | bytes 5379072 | tf_op jit(solution)/shard_map/dot_general | solution.py:23
  211.5 1.0 collective-permute-done.1
  212.6 14.3 %all_gather.22 = bf16[128,1280]{1,0:T(8,128)(2,1)S(1)} all-gather(bf16[16,1280]{1,0:T(8,128)(2,1)S(1)} %fusion.76), channel_id=1, replica_groups=mesh['section'=2,'dp'=8,'tensor'=2] {'dp'}, dimensions={0}, use_global_device_ids=true | all-gather | bytes 368640 | tf_op jit(solution)/shard_map/all_gather | solution.py:128
  226.9 4.9 %fusion = f32[128,1792]{1,0:T(8,128)} fusion(bf16[128,1280]{1,0:T(8,128)(2,1)S(1)} %all_gather.22, bf16[1,1792,1280]{2,1,0:T(8,128)(2,1)} %param.24), kind=kOutput, calls=%fused_computation.6 | convolution fusion | flops 587202560 | bytes 5832704 | tf_op jit(solution)/shard_map/dot_general | solution.py:44
  233.3 0.9 copy.67
  234.4 0.9 copy.62
  239.4 4.9 %psum.73 = bf16[128]{0:T(256)(128)(2,1)S(1)} all-reduce(bf16[128]{0:T(256)(128)(2,1)S(1)} %fusion.33), channel_id=1, replica_groups=mesh['section'=2,'dp'=8,'tensor'=2] {'tensor'}, use_global_device_ids=true, to_apply=%region_6.7 | all-reduce | flops 128 | bytes 512 | tf_op jit(solution)/shard_map/psum | solution.py:101
  244.4 4.7 %fusion.29 = bf16[128,1280]{1,0:T(8,128)(2,1)} fusion(bf16[1,1792,1280]{2,1,0:T(8,128)(2,1)} %param.24, bf16[128,1792]{1,0:T(8,128)(2,1)} %all-reduce.12.cloned.1.call-done, f32[128]{0:T(128)S(1)} %add_rsqrt_fusion.2), kind=kOutput, calls=%fused_computation.29 | convolution fusion | flops 588972032 | bytes 5374464 | tf_op jit(solution)/shard_map/dot_general | solution.py:105
  250.2 1.0 pad_maximum_fusion
  252.0 1.0 pad_maximum_fusion.1
  253.0 0.7 gather_fusion.3
  253.7 1.0 fusion.54
  255.0 0.9 copy.76
  255.9 42.2 %all-reduce.14.cloned.1.call-done = (f32[128,1792]{1,0:T(8,128)}, f32[128,1792]{1,0:T(8,128)}) async-done(((f32[128,1792]{1,0:T(8,128)}, f32[128,1792]{1,0:T(8,128)}), (f32[128,1792]{1,0:T(8,128)}, f32[128,1792]{1,0:T(8,128)})) %all-reduce.14.cloned.1.call-update) | async-done | bytes 1835024 | tf_op jit(solution)/shard_map/psum | solution.py:131
  298.0 2.6 multiply_reduce_fusion
  301.8 1.0 pad_maximum_fusion.3
  304.3 1.0 convolution_add_fusion
  306.1 4.8 %fusion.8 = f32[128,1280]{1,0:T(8,128)} fusion(bf16[128,1792]{1,0:T(8,128)(2,1)S(1)} %get-tuple-element.24, bf16[1,1280,1792]{2,1,0:T(8,128)(2,1)} %param.23), kind=kOutput, calls=%fused_computation.14 | convolution fusion | flops 587202560 | bytes 5701632 | tf_op jit(solution)/shard_map/dot_general | solution.py:44
  311.0 0.9 select_select_fusion
  311.9 4.6 %all-to-all-start = ((f32[8,128,128]{2,1,0:T(8,128)}), f32[8,128,128]{2,1,0:T(8,128)S(1)}, u32[]{:S(2)}, u32[]{:S(2)}) async-start(f32[8,128,128]{2,1,0:T(8,128)} %select_select_fusion), calls=%async_computation.4 | async-start | bytes 1048576 | tf_op jit(solution)/shard_map/all_to_all | solution.py:179
  316.7 15.7 %reduce-scatter.7.cloned.1.call-done = bf16[16,1280]{1,0:T(8,128)(2,1)} async-done(((bf16[128,1280]{1,0:T(8,128)(2,1)}), bf16[16,1280]{1,0:T(8,128)(2,1)}) %reduce-scatter.7.cloned.1.call-update) | async-done | bytes 40976 | tf_op jit(solution)/shard_map/reduce_scatter | solution.py:104
  332.4 0.8 fusion.74
  333.8 13.7 %all-reduce.1 = f32[128]{0:T(128)S(1)} all-reduce(f32[128]{0:T(128)S(1)} %copy-done.15), channel_id=11, replica_groups=mesh['section'=2,'dp'=8,'tensor'=2] {'dp'}, use_global_device_ids=true, to_apply=%region_21.22.clone | all-reduce | flops 128 | bytes 1024
  348.2 1.3 divide_select_fusion
  349.5 14.6 %reduce-scatter.11.cloned.1.call-done = f32[16,1280]{1,0:T(8,128)} async-done(((f32[128,1280]{1,0:T(8,128)}), f32[16,1280]{1,0:T(8,128)}) %reduce-scatter.11.cloned.1.call-update) | async-done | bytes 81936 | tf_op jit(solution)/shard_map/reduce_scatter | solution.py:137
  364.2 1.0 fusion.75
  (125 shorter events, 17.0 us)
Async XLA Ops:
  7.2 20.9 %copy-start.3 = (bf16[1,2,16,1280]{3,2,1,0:T(8,128)(2,1)S(1)}, bf16[1,2,16,1280]{3,2,1,0:T(8,128)(2,1)}, u32[]{:S(2)}) copy-start(bf16[1,2,16,1280]{3,2,1,0:T(8,128)(2,1)} %param.21) | copy-start | bytes 245764
  7.2 86.5 %all-reduce.10.cloned.1.call-start = ((), (), s32[]{:S(2)}) async-start(), calls=%async_computation.5 | async-start | bytes 917504 | tf_op jit(solution)/shard_map/psum | solution.py:100
  28.0 33.2 %copy-start.7 = (bf16[1,16,1280]{2,1,0:T(8,128)(2,1)S(1)}, bf16[1,16,1280]{2,1,0:T(8,128)(2,1)}, u32[]{:S(2)}) copy-start(bf16[1,16,1280]{2,1,0:T(8,128)(2,1)} %param.18) | copy-start | bytes 122884
  28.1 109.1 %all-reduce.16.cloned.1.call-start = ((), (), s32[]{:S(2)}) async-start(), calls=%async_computation.12 | async-start | bytes 3670016 | tf_op jit(solution)/shard_map/psum | solution.py:131
  28.1 47.6 %copy-start = (bf16[1,1792,1280]{2,1,0:T(8,128)(2,1)S(1)}, bf16[1,1792,1280]{2,1,0:T(8,128)(2,1)}, u32[]{:S(2)}) copy-start(bf16[1,1792,1280]{2,1,0:T(8,128)(2,1)} %param.24) | copy-start | bytes 13762564
  61.2 17.2 %copy-start.20 = (s32[1,1,8]{2,1,0:T(1,128)S(1)}, s32[1,1,8]{2,1,0:T(1,128)}, u32[]{:S(2)}) copy-start(s32[1,1,8]{2,1,0:T(1,128)} %param.26) | copy-start | bytes 100
  61.2 17.2 %copy-start.11 = (s32[1,1,8,6]{2,1,3,0:T(1,128)S(1)}, s32[1,1,8,6]{2,1,3,0:T(1,128)}, u32[]{:S(2)}) copy-start(s32[1,1,8,6]{2,1,3,0:T(1,128)} %param.27) | copy-start | bytes 580
  78.3 92.2 %reduce-scatter.5.cloned.1.call-start = ((), (), s32[]{:S(2)}) async-start(), calls=%async_computation.6 | async-start | bytes 368640 | tf_op jit(solution)/shard_map/reduce_scatter | solution.py:104
  78.9 18.9 %copy-start.16 = (pred[8]{0:T(512)(128)(4,1)}, pred[8]{0:T(512)(128)(4,1)S(1)}, u32[]{:S(2)}) copy-start(pred[8]{0:T(512)(128)(4,1)S(1)} %get-tuple-element.42) | copy-start | bytes 28
  89.5 8.2 %copy-start.21 = (s32[8]{0:T(128)}, s32[8]{0:T(128)S(1)}, u32[]{:S(2)}) copy-start(s32[8]{0:T(128)S(1)} %convert_subtract_fusion) | copy-start | bytes 100
  97.8 72.8 %copy-start.6 = (bf16[1,16,1280]{2,1,0:T(8,128)(2,1)S(1)}, bf16[1,16,1280]{2,1,0:T(8,128)(2,1)}, u32[]{:S(2)}) copy-start(bf16[1,16,1280]{2,1,0:T(8,128)(2,1)} %param.16) | copy-start | bytes 122884
  97.8 107.5 %reduce-scatter.9.cloned.1.call-start = ((), (), s32[]{:S(2)}) async-start(), calls=%async_computation.9 | async-start | bytes 737280 | tf_op jit(solution)/shard_map/reduce_scatter | solution.py:137
  137.2 37.6 %copy-start.23 = (u32[32]{0:T(128)S(1)}, u32[32]{0:T(128)}, u32[]{:S(2)}) copy-start(u32[32]{0:T(128)} %constant.155) | copy-start | bytes 388
  137.2 39.2 %copy-start.9 = (bf16[1,16,1280]{2,1,0:T(8,128)(2,1)S(1)}, bf16[1,16,1280]{2,1,0:T(8,128)(2,1)}, u32[]{:S(2)}) copy-start(bf16[1,16,1280]{2,1,0:T(8,128)(2,1)} %param.17) | copy-start | bytes 122884
  144.1 68.4 %copy-start.8 = (bf16[1,16,1280]{2,1,0:T(8,128)(2,1)S(1)}, bf16[1,16,1280]{2,1,0:T(8,128)(2,1)}, u32[]{:S(2)}) copy-start(bf16[1,16,1280]{2,1,0:T(8,128)(2,1)} %param.19) | copy-start | bytes 122884
  144.1 100.3 %all-reduce.12.cloned.1.call-start = ((), (), s32[]{:S(2)}) async-start(), calls=%async_computation.7 | async-start | bytes 917504 | tf_op jit(solution)/shard_map/psum | solution.py:100
  171.3 5.0 %collective-permute-start = (bf16[16,1280]{1,0:T(8,128)(2,1)S(1)}, bf16[16,1280]{1,0:T(8,128)(2,1)S(1)}, u32[]{:S(2)}, u32[]{:S(2)}) collective-permute-start(bf16[16,1280]{1,0:T(8,128)(2,1)S(1)} %fusion.73), channel_id=1, source_target_pairs={{0,16},{1,17},{2,18},{3,19},{4,20},{5,21},{6,22},{7,23},{8,24},{9,... | collective-permute-start | bytes 122888 | tf_op jit(solution)/shard_map/ppermute | solution.py:16
  206.3 6.2 %copy-start.4 = (bf16[16,1280]{1,0:T(8,128)(2,1)}, bf16[16,1280]{1,0:T(8,128)(2,1)S(1)}, u32[]{:S(2)}) copy-start(bf16[16,1280]{1,0:T(8,128)(2,1)S(1)} %fusion.72) | copy-start | bytes 122884
  206.3 6.2 %collective-permute-start.1 = (bf16[16,1280]{1,0:T(8,128)(2,1)S(1)}, bf16[16,1280]{1,0:T(8,128)(2,1)S(1)}, u32[]{:S(2)}, u32[]{:S(2)}) collective-permute-start(bf16[16,1280]{1,0:T(8,128)(2,1)S(1)} %fusion.72), channel_id=1, source_target_pairs={{16,0},{17,1},{18,2},{19,3},{20,4},{21,5},{22,6},{23,7},{24,8},{25... | collective-permute-start | bytes 122888 | tf_op jit(solution)/shard_map/ppermute | solution.py:16
  211.4 86.6 %all-reduce.14.cloned.1.call-start = ((), (), s32[]{:S(2)}) async-start(), calls=%async_computation.11 | async-start | bytes 3670016 | tf_op jit(solution)/shard_map/psum | solution.py:131
  226.9 8.4 %copy-start.10 = (s32[1,1,8,6]{2,1,3,0:T(1,128)S(1)}, s32[1,1,8,6]{2,1,3,0:T(1,128)}, u32[]{:S(2)}) copy-start(s32[1,1,8,6]{2,1,3,0:T(1,128)} %param.25) | copy-start | bytes 580
  231.8 100.6 %reduce-scatter.7.cloned.1.call-start = ((), (), s32[]{:S(2)}) async-start(), calls=%async_computation.8 | async-start | bytes 368640 | tf_op jit(solution)/shard_map/reduce_scatter | solution.py:104
  249.1 115.1 %reduce-scatter.11.cloned.1.call-start = ((), (), s32[]{:S(2)}) async-start(), calls=%async_computation.10 | async-start | bytes 737280 | tf_op jit(solution)/shard_map/reduce_scatter | solution.py:137
  303.5 7.4 %copy-start.13 = (pred[8]{0:T(512)(128)(4,1)S(1)}, pred[8]{0:T(512)(128)(4,1)}, u32[]{:S(2)}) copy-start(pred[8]{0:T(512)(128)(4,1)} %compare_and_fusion.2) | copy-start | bytes 28
  303.5 7.4 %copy-start.14 = (pred[8]{0:T(512)(128)(4,1)S(1)}, pred[8]{0:T(512)(128)(4,1)}, u32[]{:S(2)}) copy-start(pred[8]{0:T(512)(128)(4,1)} %dynamic-slice_bitcast_fusion) | copy-start | bytes 28
  305.3 11.2 %copy-start.18 = (s32[6]{0:T(128)S(1)}, s32[6]{0:T(128)}, u32[]{:S(2)}) copy-start(s32[6]{0:T(128)} %fusion.87) | copy-start | bytes 76
  305.3 11.3 %copy-start.17 = (pred[8]{0:T(512)(128)(4,1)S(1)}, pred[8]{0:T(512)(128)(4,1)}, u32[]{:S(2)}) copy-start(pred[8]{0:T(512)(128)(4,1)} %copy-done.16) | copy-start | bytes 28
  305.3 11.3 %copy-start.22 = (s32[8]{0:T(128)S(1)}, s32[8]{0:T(128)}, u32[]{:S(2)}) copy-start(s32[8]{0:T(128)} %copy-done.21) | copy-start | bytes 100
  306.0 27.8 %copy-start.15 = (f32[128]{0:T(128)S(1)}, f32[128]{0:T(128)}, u32[]{:S(2)}) copy-start(f32[128]{0:T(128)} %get-tuple-element.23) | copy-start | bytes 1540
  306.0 41.5 %copy-start.12 = (f32[128]{0:T(128)S(1)}, f32[128]{0:T(128)}, u32[]{:S(2)}) copy-start(f32[128]{0:T(128)} %add_rsqrt_fusion) | copy-start | bytes 1540
  306.0 42.2 %copy-start.1 = (f32[1,1,1,6,128,128]{5,4,3,2,1,0:T(8,128)S(1)}, f32[1,1,1,6,128,128]{5,4,3,2,1,0:T(8,128)}, u32[]{:S(2)}) copy-start(f32[1,1,1,6,128,128]{5,4,3,2,1,0:T(8,128)} %param.28) | copy-start | bytes 1179652
  306.1 42.2 %copy-start.2 = (f32[1,1,1,6,128,128]{5,4,3,2,1,0:T(8,128)S(1)}, f32[1,1,1,6,128,128]{5,4,3,2,1,0:T(8,128)}, u32[]{:S(2)}) copy-start(f32[1,1,1,6,128,128]{5,4,3,2,1,0:T(8,128)} %param.29) | copy-start | bytes 1179652
  306.1 42.2 %copy-start.19 = (pred[6]{0:T(512)(128)(4,1)S(1)}, pred[6]{0:T(512)(128)(4,1)}, u32[]{:S(2)}) copy-start(pred[6]{0:T(512)(128)(4,1)} %compare_and_fusion.3) | copy-start | bytes 22
  310.9 54.2 %copy-start.5 = (bf16[16,1280]{1,0:T(8,128)(2,1)S(1)}, bf16[16,1280]{1,0:T(8,128)(2,1)}, u32[]{:S(2)}) copy-start(bf16[16,1280]{1,0:T(8,128)(2,1)} %copy-done.4) | copy-start | bytes 122884
  311.9 35.7 %all-to-all-start = ((f32[8,128,128]{2,1,0:T(8,128)}), f32[8,128,128]{2,1,0:T(8,128)S(1)}, u32[]{:S(2)}, u32[]{:S(2)}) async-start(f32[8,128,128]{2,1,0:T(8,128)} %select_select_fusion), calls=%async_computation.4 | async-start | bytes 1048576 | tf_op jit(solution)/shard_map/all_to_all | solution.py:179
Sparse Core Ops, SparseCore 0:
  28.2 28.2 all-reduce.9
  78.4 58.6 all-reduce.15
  140.0 30.5 reduce-scatter.4
  172.8 29.3 reduce-scatter.8
  211.6 26.7 all-reduce.11
  240.6 57.3 all-reduce.13
  300.9 31.3 reduce-scatter.6
  334.7 29.4 reduce-scatter.10
where the time goes:
time: 374 us; the launch traced here: 373 us
  waiting for transfers between devices  138 us (37%)
  blocking collectives  131 us (35%)
  matrix products  43.6 us (12%)
  other arithmetic  22.3 us (6%)
  between operations  15.9 us (4%)
  local copies, waits for them, and re-layouts  11.3 us (3%)
  starting transfers between devices  9.81 us (3%)
    psum x2, waiting for transfers between devices, body(): lax.psum((product, squares, act_grad), 'tensor')  81.5 us
    reduce_scatter x2, waiting for transfers between devices, body(): lax.psum_scatter(jnp.dot(forward_activated, down_matrix, preferred_elemen...  40.9 us
    all_gather x2, blocking collectives, body(): forward_rows_all = lax.all_gather(rows_in, 'dp', axis=0, tiled=True)  31.1 us
    all_gather x2, blocking collectives, body(): grads_all = lax.all_gather(grads_in, 'dp', axis=0, tiled=True)  28.8 us
    all_gather x2, blocking collectives, body(): rows_all = lax.all_gather(rows_local, 'dp', axis=0, tiled=True)  28.8 us
    unnamed x2, blocking collectives  27.6 us
    dot_general x4, matrix products, times_transposed(): lax.dot_general(left, right, (((1,), (1,)), ((), ())), preferred_element_...  17.1 us
    dot_general x4, matrix products, normed_product(): product = jnp.dot(normed, up_matrix, preferred_element_type=jnp.float32)  15.7 us
  transfers between devices with their start and end apart: 11, of which 7 were waited for; matrix products, arithmetic and copies ran while one was open for 19% of the time, Pallas kernels for 0%

commit v1 on v0

v1 whole, which is shorter than its diff:
```python
import functools

import jax
import jax.numpy as jnp
from jax import lax
from jax.experimental import pallas as pl
from jax.experimental.pallas import tpu as pltpu
from jax.sharding import PartitionSpec as P

BLK = 128
EPSILON = 1e-06
BF16 = jnp.bfloat16
F32 = jnp.float32


def tensor_sum(value):
    step = 1
    while step < lax.axis_size("tensor"):
        pairs = [(t, t ^ step) for t in range(lax.axis_size("tensor"))]
        value = value + lax.ppermute(value.astype(BF16), "tensor", pairs).astype(F32)
        step *= 2
    return value


def sibling(value):
    return lax.ppermute(value, "dp", [(d, d ^ 1) for d in range(lax.axis_size("dp"))])


def shifted(value, steps):
    count = lax.axis_size("dp")
    return lax.ppermute(value, "dp", [(d, (d + 2 * steps) % count) for d in range(count)])


def gather_rows(local):
    depth = lax.axis_size("dp") // 2
    mine = jnp.stack([local] + [shifted(local, k) for k in range(1, depth)], axis=-3)
    both = jnp.stack([mine, sibling(mine)], axis=-4)
    return both.reshape(local.shape[:-2] + (2 * depth * local.shape[-2], local.shape[-1]))


def gather_passed(local, direction):
    sections = lax.axis_size("section")
    count = lax.axis_size("dp")
    depth = count // 2

    def moved(k):
        pairs = [
            (s * count + d, (s + direction) * count + (d + 2 * k) % count)
            for s in range(sections)
            if 0 <= s + direction < sections
            for d in range(count)
        ]
        return lax.ppermute(local, ("section", "dp"), pairs)

    mine = jnp.stack([moved(k) for k in range(depth)])
    both = jnp.stack([mine, sibling(mine)])
    return both.reshape((2 * depth * local.shape[0], local.shape[1]))


def scatter_rows(partial):
    depth = lax.axis_size("dp") // 2
    slots = partial.reshape((2, depth, partial.shape[0] // (2 * depth), partial.shape[1]))
    pairs = slots[0] + sibling(slots[1].astype(BF16)).astype(F32)
    total = pairs[0]
    for k in range(1, depth):
        total = total + shifted(pairs[k].astype(BF16), -k).astype(F32)
    return total


def split_squares(squares):
    high = squares.astype(BF16)
    low = (squares - high.astype(F32)).astype(BF16)
    lane = lax.broadcasted_iota(jnp.int32, (squares.shape[0], BLK), 1)
    return jnp.where(lane == 0, high[:, None], jnp.where(lane == 1, low[:, None], jnp.zeros((), BF16)))


def normed_product(rows_all, gain_row, up_matrix, width):
    widened = rows_all.astype(F32)
    squares = jnp.sum(widened * widened, axis=1)
    normed = (widened * gain_row.astype(F32)).astype(BF16)
    product = jnp.dot(normed, up_matrix, preferred_element_type=F32)
    step = 1
    while step < lax.axis_size("tensor"):
        pairs = [(t, t ^ step) for t in range(lax.axis_size("tensor"))]
        sent = jnp.concatenate([product.astype(BF16), split_squares(squares)], axis=1)
        got = lax.ppermute(sent, "tensor", pairs).astype(F32)
        hidden_count = product.shape[1]
        product = product + got[:, :hidden_count]
        squares = squares + got[:, hidden_count] + got[:, hidden_count + 1]
        step *= 2
    return normed, product, lax.rsqrt(squares / width + EPSILON)


def activate(hidden):
    return (hidden * jax.nn.sigmoid(hidden)).astype(BF16)


def times_transposed(left, right):
    return lax.dot_general(left, right, (((1,), (1,)), ((), ())), preferred_element_type=F32)


def block_kernel(plan, *refs):
    turns = (len(refs) - 1) // 4
    out = refs[-1]
    slot = pl.program_id(0)
    is_up = plan[0, slot]
    left = pl.ds(pl.multiple_of(plan[1, slot] * BLK, BLK), BLK)
    right = pl.ds(pl.multiple_of(plan[2, slot] * BLK, BLK), BLK)

    def write(left_index, right_index):
        total = jnp.zeros((BLK, BLK), F32)
        for turn in range(turns):
            group = refs[4 * turn : 4 * turn + 4]
            total += lax.dot_general(
                group[left_index][:, left],
                group[right_index][:, right],
                (((0,), (0,)), ((), ())),
                preferred_element_type=F32,
            )
        out[0] = total.astype(BF16)

    @pl.when(is_up == 1)
    def _():
        write(0, 1)

    @pl.when(is_up == 0)
    def _():
        write(2, 3)


def outgoing_blocks(plan, tables):
    slots = plan.shape[1]
    flat = [table for turn in tables for table in turn]
    return pl.pallas_call(
        block_kernel,
        grid_spec=pltpu.PrefetchScalarGridSpec(
            num_scalar_prefetch=1,
            grid=(slots,),
            in_specs=[pl.BlockSpec(table.shape, lambda i, plan: (0, 0)) for table in flat],
            out_specs=pl.BlockSpec((1, BLK, BLK), lambda i, plan: (i, 0, 0)),
        ),
        out_shape=jax.ShapeDtypeStruct((slots, BLK, BLK), BF16),
        compiler_params=pltpu.CompilerParams(vmem_limit_bytes=24 * 1024 * 1024),
        name="block_grads",
    )(plan, *flat)


def adam_kernel(plan, arrived, first, second, first_out, second_out, direction_out):
    slot = pl.program_id(0)
    filled = plan[0, slot] == 1

    @pl.when(filled)
    def _():
        grad = arrived[0].astype(F32)
        first_new = 0.9 * first[0] + 0.1 * grad
        second_new = 0.999 * second[0] + 0.001 * grad * grad
        first_out[0] = first_new
        second_out[0] = second_new
        direction_out[0] = first_new / (jnp.sqrt(second_new) + 1e-08)

    @pl.when(jnp.logical_not(filled))
    def _():
        zeros = jnp.zeros((BLK, BLK), F32)
        first_out[0] = zeros
        second_out[0] = zeros
        direction_out[0] = zeros


def adam(plan, arrived, first, second):
    slots = first.shape[0]
    block = pl.BlockSpec((1, BLK, BLK), lambda i, plan: (i, 0, 0))
    shape = jax.ShapeDtypeStruct((slots, BLK, BLK), F32)
    return pl.pallas_call(
        adam_kernel,
        grid_spec=pltpu.PrefetchScalarGridSpec(
            num_scalar_prefetch=1,
            grid=(slots,),
            in_specs=[pl.BlockSpec((1, BLK, BLK), lambda i, plan: (plan[1, i], 0, 0)), block, block],
            out_specs=[block] * 3,
        ),
        out_shape=[shape] * 3,
        name="adam_step",
    )(plan, arrived, first, second)


def body(
    section_inputs,
    entering,
    grad_outputs,
    arriving,
    live_rows,
    stashed_inputs,
    norm_gain,
    up_weight,
    down_weight,
    held_blocks,
    held_count,
    held_owner,
    first_moment,
    second_moment,
):
    section_count = lax.axis_size("section")
    section_index = lax.axis_index("section")
    dp_index = lax.axis_index("dp")
    dp_count = lax.axis_size("dp")
    depth = dp_count // 2
    turn_count = stashed_inputs.shape[1]
    local_rows = section_inputs.shape[1]
    gain_row = norm_gain[0]
    up_matrix = up_weight[0]
    down_matrix = down_weight[0]
    channels = up_matrix.shape[0]
    width = channels * lax.axis_size("tensor")
    channel_blocks = channels // BLK
    hidden_blocks = up_matrix.shape[1] // BLK
    up_count = channel_blocks * hidden_blocks
    is_first = section_index == 0
    is_last = section_index == section_count - 1
    row_ids = dp_index * local_rows + lax.iota(jnp.int32, local_rows)

    start_grads = grad_outputs[0]
    later_inputs = []
    for turn in range(1, turn_count):
        live = (row_ids < live_rows[turn - 1])[:, None]
        masked = jnp.where(live, arriving[turn - 1], jnp.zeros((), BF16))
        later_inputs.append(jnp.where(is_last, masked, entering[turn - 1]))
    first_pair = gather_rows(jnp.stack([stashed_inputs[0, 0], start_grads]))
    others = gather_rows(jnp.stack([section_inputs[0]] + [stashed_inputs[0, u] for u in range(1, turn_count)] + later_inputs))
    stash_all = [first_pair[0]] + [others[u] for u in range(1, turn_count)]
    edge_all = [others[turn_count - 1 + u] for u in range(1, turn_count)]

    forward_results = []
    backward_results = []
    tables = []
    for turn in range(turn_count):
        if turn == 0:
            grads_in, grads_all = start_grads, first_pair[1]
        else:
            passed = gather_passed(backward_results[-1], -1)
            grads_all = jnp.where(is_last, edge_all[turn - 1], passed)
            grads_in = jnp.where(is_last, later_inputs[turn - 1], passed[:local_rows])
        rows_local = stashed_inputs[0, turn]
        normed, product, row_scales = normed_product(stash_all[turn], gain_row, up_matrix, width)
        act_grad = tensor_sum(times_transposed(grads_all, down_matrix))
        hidden = product * row_scales[:, None]
        gate = jax.nn.sigmoid(hidden)
        activated = (hidden * gate).astype(BF16)
        hidden_grad = act_grad * gate * (1.0 + hidden * (1.0 - gate))
        scaled_grad = (hidden_grad * row_scales[:, None]).astype(BF16)
        scale_grad = jnp.sum(hidden_grad * product, axis=1)
        normed_part = times_transposed(scaled_grad, up_matrix)
        widened_all = stash_all[turn].astype(F32)
        input_part = (
            normed_part * gain_row.astype(F32)
            - (scale_grad * row_scales**3 / width)[:, None] * widened_all
        )
        input_grad = grads_in.astype(F32) + scatter_rows(input_part)
        backward_results.append(input_grad.astype(BF16))
        tables.append((normed, scaled_grad, activated, grads_all))
        if turn == 0:
            rows_in, rows_all = section_inputs[0], others[0]
        else:
            passed = gather_passed(forward_results[-1], 1)
            rows_all = jnp.where(is_first, edge_all[turn - 1], passed)
            rows_in = jnp.where(is_first, later_inputs[turn - 1], passed[:local_rows])
        _, product, row_scales = normed_product(rows_all, gain_row, up_matrix, width)
        forward_activated = activate(product * row_scales[:, None])
        mixed = scatter_rows(jnp.dot(forward_activated, down_matrix, preferred_element_type=F32))
        forward_results.append((rows_in.astype(F32) + mixed).astype(BF16))

    counts = held_count[0, 0]
    owners = held_owner[0, 0]
    capacity = owners.shape[1]
    slot_ids = lax.iota(jnp.int32, capacity)
    dp_ids = lax.iota(jnp.int32, dp_count)
    live_slots = slot_ids[None, :] < counts[:, None]
    chosen = (owners[:, None, :] == dp_ids[None, :, None]) & live_slots[:, None, :]
    is_sent = jnp.any(chosen, axis=2)
    my_z, my_core = dp_index // 2, dp_index % 2
    slots = lax.iota(jnp.int32, dp_count)
    slot_owner = 2 * ((my_z - slots % depth) % depth) + (my_core + slots // depth) % 2
    my_owners = lax.dynamic_index_in_dim(owners, dp_index, 0, keepdims=False)
    my_count = lax.dynamic_index_in_dim(counts, dp_index, 0, keepdims=False)
    my_blocks = lax.dynamic_index_in_dim(held_blocks[0, 0], dp_index, 0, keepdims=False)
    to_slot = (my_owners[None, :] == slot_owner[:, None]) & (slot_ids < my_count)[None, :]
    number = jnp.sum(jnp.where(to_slot, my_blocks[None, :], 0), axis=1)
    is_up = number < up_count
    down_number = number - up_count
    left_index = jnp.where(is_up, number // hidden_blocks, down_number // channel_blocks)
    right_index = jnp.where(is_up, number % hidden_blocks, down_number % channel_blocks)
    plan = jnp.stack([is_up.astype(jnp.int32), left_index, right_index])

    outgoing = outgoing_blocks(plan, tables).reshape((2, depth, BLK, BLK))
    relayed = sibling(outgoing[1])
    both = jnp.stack([outgoing[0], relayed], axis=1)
    arrived = jnp.concatenate([both[:1]] + [shifted(both[k], -k)[None] for k in range(1, depth)])
    arrived = arrived.reshape((dp_count, BLK, BLK))

    from_source = lax.dynamic_index_in_dim(is_sent, dp_index, 1, keepdims=False)
    source_count = from_source.astype(jnp.int32)
    ranks = jnp.cumsum(source_count) - source_count
    matches = from_source[None, :] & (ranks[None, :] == slot_ids[:, None])
    source_place = 2 * ((dp_ids // 2 - my_z) % depth) + (dp_ids + my_core) % 2
    arrived_index = jnp.sum(jnp.where(matches, source_place[None, :], 0), axis=1)
    adam_plan = jnp.stack([jnp.any(matches, axis=1).astype(jnp.int32), arrived_index])
    first_out, second_out, direction_out = adam(adam_plan, arrived, first_moment[0, 0, 0], second_moment[0, 0, 0])
    return (
        jnp.stack(forward_results)[None],
        jnp.stack(backward_results)[None],
        first_out[None, None, None],
        second_out[None, None, None],
        direction_out[None, None, None],
    )


def solution(mesh):
    return jax.shard_map(
        body,
        mesh=mesh,
        in_specs=(
            P("section", "dp", "tensor"),
            P(None, "dp", "tensor"),
            P("section", "dp", "tensor"),
            P(None, "dp", "tensor"),
            P(),
            P("section", None, "dp", "tensor"),
            P("section", "tensor"),
            P("section", "tensor", "dp"),
            P("section", "dp", "tensor"),
            P("section", "tensor", None, None),
            P("section", "tensor", None),
            P("section", "tensor", None, None),
            P("section", "tensor", "dp", None, None, None),
            P("section", "tensor", "dp", None, None, None),
        ),
        out_specs=(
            P("section", None, "dp", "tensor"),
            P("section", None, "dp", "tensor"),
            P("section", "tensor", "dp", None, None, None),
            P("section", "tensor", "dp", None, None, None),
            P("section", "tensor", "dp", None, None, None),
        ),
        check_vma=False,
    )
```

time: 374 us -> 172 us (0.46)
  blocking collectives: 131 us -> 0 us
  waiting for transfers between devices: 138 us -> 36.4 us
  starting transfers between devices: 9.81 us -> 52 us
  between operations: 15.9 us -> 2.3 us
  matrix products: 43.6 us -> 34 us
  other arithmetic: 22.3 us -> 31.6 us
  Pallas kernels: 0 us -> 7.2 us
  local copies, waits for them, and re-layouts: 11.3 us -> 6.53 us
    all_gather x6 -> x0, blocking collectives: 88.7 us -> none  [the longest x2 31.1 us: body(): forward_rows_all = lax.all_gather(rows_in, 'dp', axis=0, tiled=True)]
    psum x4 -> x0, waiting for transfers between devices: 81.5 us -> none  [the longest x2 81.5 us: body(): lax.psum((product, squares, act_grad), 'tensor')]
    reduce_scatter x4 -> x0, waiting for transfers between devices: 55.5 us -> none  [the longest x2 40.9 us: body(): lax.psum_scatter(jnp.dot(forward_activated, down_matrix, preferred_elemen...]
    ppermute x2 -> x44, starting transfers between devices: 4.67 us -> 52 us  [the longest x21 28.1 us: shifted(): lax.ppermute(value, 'dp', [(d, (d + 2 * steps) % count) for d in range(co...]
    ppermute x2 -> x44, waiting for transfers between devices: 1.37 us -> 36.4 us  [the longest x4 15.1 us: normed_product(): got = lax.ppermute(sent, 'tensor', pairs).astype(F32)]
    unnamed x2 -> x0, blocking collectives: 27.6 us -> none
    psum x3 -> x0, blocking collectives: 14.8 us -> none  [the longest x2 9.87 us: body(): lax.psum(forward_squares.astype(jnp.bfloat16), 'tensor').astype(jnp.float32)]
    dot_general x8 -> x6, matrix products: 26.5 us -> 15.8 us  [the longest x4 13.9 us: normed_product(): product = jnp.dot(normed, up_matrix, preferred_element_type=F32)]
  transfers between devices with their start and end apart: 11 -> 44, of which waited for: 7 -> 11; matrix products, arithmetic and copies ran while one was open for 19% -> 37% of each run, Pallas kernels for 0% -> 4%
where the time goes in v1:
time: 172 us; the launch traced here: 170 us
  starting transfers between devices  52 us (30%)
  waiting for transfers between devices  36.4 us (21%)
  matrix products  34 us (20%)
  other arithmetic  31.6 us (18%)
  Pallas kernels  7.2 us (4%)
  local copies, waits for them, and re-layouts  6.53 us (4%)
  between operations  2.3 us (1%)
    ppermute x21, starting transfers between devices, shifted(): lax.ppermute(value, 'dp', [(d, (d + 2 * steps) % count) for d in range(co...  28.1 us
    dot_general x4, matrix products, times_transposed(): lax.dot_general(left, right, (((1,), (1,)), ((), ())), preferred_element_...  18.3 us
    ppermute x8, starting transfers between devices, moved(): return lax.ppermute(local, ('section', 'dp'), pairs)  16.6 us
    ppermute x4, waiting for transfers between devices, normed_product(): got = lax.ppermute(sent, 'tensor', pairs).astype(F32)  15.1 us
    dot_general x4, matrix products, normed_product(): product = jnp.dot(normed, up_matrix, preferred_element_type=F32)  13.9 us
    ppermute x21, waiting for transfers between devices, shifted(): lax.ppermute(value, 'dp', [(d, (d + 2 * steps) % count) for d in range(co...  11.2 us
    ppermute x2, waiting for transfers between devices, tensor_sum(): lax.ppermute(value.astype(BF16), 'tensor', pairs).astype(F32)  8.39 us
    ppermute x4, starting transfers between devices, normed_product(): got = lax.ppermute(sent, 'tensor', pairs).astype(F32)  5.07 us
  transfers between devices with their start and end apart: 44, of which 11 were waited for; matrix products, arithmetic and copies ran while one was open for 37% of the time, Pallas kernels for 4%

profile of v1, /device:TPU:0, one launch (start us, length us, event | category | flops | bytes accessed | tf_op | source)
XLA Modules:
  0.0 170.1 jit_solution(4600924338413386007)
XLA Ops:
  3.8 3.1 %collective-permute-start = (bf16[3,16,1280]{2,1,0:T(8,128)(2,1)S(1)}, bf16[3,16,1280]{2,1,0:T(8,128)(2,1)S(1)}, u32[]{:S(2)}, u32[]{:S(2)}) collective-permute-start(bf16[3,16,1280]{2,1,0:T(8,128)(2,1)S(1)} %get-tuple-element.66), channel_id=1, source_target_pairs={{0,4},{2,6},{4,8},{6,10},{8,12},{10,14},{12,0},{14,2},{1,5},{3,7},... | collective-permute-start | bytes 368648 | tf_op jit(solution)/shard_map/ppermute | solution.py:31
  6.9 2.6 %collective-permute-start.1 = (bf16[3,16,1280]{2,1,0:T(8,128)(2,1)S(1)}, bf16[3,16,1280]{2,1,0:T(8,128)(2,1)S(1)}, u32[]{:S(2)}, u32[]{:S(2)}) collective-permute-start(bf16[3,16,1280]{2,1,0:T(8,128)(2,1)S(1)} %get-tuple-element.66), channel_id=1, source_target_pairs={{0,8},{2,10},{4,12},{6,14},{8,0},{10,2},{12,4},{14,6},{1,9},{3,11}... | collective-permute-start | bytes 368648 | tf_op jit(solution)/shard_map/ppermute | solution.py:31
  10.4 1.8 %collective-permute-start.20 = (bf16[2,16,1280]{2,1,0:T(8,128)(2,1)S(1)}, bf16[2,16,1280]{2,1,0:T(8,128)(2,1)S(1)}, u32[]{:S(2)}, u32[]{:S(2)}) collective-permute-start(bf16[2,16,1280]{2,1,0:T(8,128)(2,1)S(1)} %get-tuple-element.72), channel_id=1, source_target_pairs={{0,8},{2,10},{4,12},{6,14},{8,0},{10,2},{12,4},{14,6},{1,9},{3,11}... | collective-permute-start | bytes 245768 | tf_op jit(solution)/shard_map/ppermute | solution.py:31
  12.2 1.9 %collective-permute-start.21 = (bf16[2,16,1280]{2,1,0:T(8,128)(2,1)S(1)}, bf16[2,16,1280]{2,1,0:T(8,128)(2,1)S(1)}, u32[]{:S(2)}, u32[]{:S(2)}) collective-permute-start(bf16[2,16,1280]{2,1,0:T(8,128)(2,1)S(1)} %get-tuple-element.72), channel_id=1, source_target_pairs={{0,12},{2,14},{4,0},{6,2},{8,4},{10,6},{12,8},{14,10},{1,13},{3,15... | collective-permute-start | bytes 245768 | tf_op jit(solution)/shard_map/ppermute | solution.py:31
  14.1 1.2 constant_dynamic-slice_fusion
  16.1 1.1 dynamic-slice_reduce_fusion
  20.9 2.0 %collective-permute-done.20 = bf16[2,16,1280]{2,1,0:T(8,128)(2,1)S(1)} collective-permute-done((bf16[2,16,1280]{2,1,0:T(8,128)(2,1)S(1)}, bf16[2,16,1280]{2,1,0:T(8,128)(2,1)S(1)}, u32[]{:S(2)}, u32[]{:S(2)}) %collective-permute-start.20) | collective-permute-done | bytes 81952 | tf_op jit(solution)/shard_map/ppermute | solution.py:31
  23.6 4.4 %collective-permute-done.2 = bf16[3,16,1280]{2,1,0:T(8,128)(2,1)S(1)} collective-permute-done((bf16[3,16,1280]{2,1,0:T(8,128)(2,1)S(1)}, bf16[3,16,1280]{2,1,0:T(8,128)(2,1)S(1)}, u32[]{:S(2)}, u32[]{:S(2)}) %collective-permute-start.2) | collective-permute-done | bytes 122912 | tf_op jit(solution)/shard_map/ppermute | solution.py:31
  28.2 5.0 %fusion.137 = (bf16[128,1792]{1,0:T(8,128)(2,1)}, f32[128,1792]{1,0:T(8,128)}) fusion(bf16[128,1280]{1,0:T(8,128)(2,1)S(1)} %bitcast.306, bf16[1,1792,1280]{2,1,0:T(8,128)(2,1)} %param.22), kind=kOutput, calls=%fused_computation.284 | convolution fusion | flops 587431936 | bytes 6291456 | tf_op jit(solution)/shard_map/dot_general | solution.py:99
  35.4 4.1 %fusion.136 = (bf16[128,1792]{1,0:T(8,128)(2,1)S(1)}, f32[128,1792]{1,0:T(8,128)}) fusion(bf16[128,1280]{1,0:T(8,128)(2,1)} %bitcast.319, bf16[1,1280,1792]{2,1,0:T(8,128)(2,1)} %param.21), kind=kOutput, calls=%fused_computation.283 | convolution fusion | flops 587431936 | bytes 6291456 | tf_op jit(solution)/shard_map/dot_general | solution.py:81
  40.5 1.8 %collective-permute-start.24 = (bf16[128,1920]{1,0:T(8,128)(2,1)}, bf16[128,1920]{1,0:T(8,128)(2,1)}, u32[]{:S(2)}, u32[]{:S(2)}) collective-permute-start(bf16[128,1920]{1,0:T(8,128)(2,1)} %pad_maximum_fusion.3), channel_id=1, source_target_pairs={{0,1},{1,0},{2,3},{3,2},{4,5},{5,4},{6,7},{7,6},{8,9},{9,8},{10,11... | collective-permute-start | bytes 1474568 | tf_op jit(solution)/shard_map/ppermute | solution.py:86
  42.3 4.0 %fusion.138 = (bf16[128,1792]{1,0:T(8,128)(2,1)S(1)}, f32[128,1792]{1,0:T(8,128)}) fusion(bf16[128,1280]{1,0:T(8,128)(2,1)S(1)} %bitcast.318, bf16[1,1280,1792]{2,1,0:T(8,128)(2,1)} %param.21), kind=kOutput, calls=%fused_computation.285 | convolution fusion | flops 587431936 | bytes 6291456 | tf_op jit(solution)/shard_map/dot_general | solution.py:81
  47.6 9.8 %collective-permute-done.24 = bf16[128,1920]{1,0:T(8,128)(2,1)} collective-permute-done((bf16[128,1920]{1,0:T(8,128)(2,1)}, bf16[128,1920]{1,0:T(8,128)(2,1)}, u32[]{:S(2)}, u32[]{:S(2)}) %collective-permute-start.24) | collective-permute-done | bytes 491552 | tf_op jit(solution)/shard_map/ppermute | solution.py:86
  57.4 1.1 convert_element_type.440
  58.6 2.1 %multiply_convert_fusion.3 = (bf16[128,1792]{1,0:T(8,128)(2,1)S(1)}, f32[128,1792]{1,0:T(8,128)S(1)}, bf16[128,1792]{1,0:T(8,128)(2,1)S(1)}) fusion(f32[128]{0:T(128)S(1)} %fusion.118, f32[128,1792]{1,0:T(8,128)} %get-tuple-element.95, f32[128,1920]{1,0:T(8,128)S(1)} %convert_element_type.440, f32[128,1792]{1,0:T(8,128)} %get-tuple-element.97, ...), kind=kLoop, calls=%fused_computation.41 | loop fusion | flops 3670016 | bytes 5046784 | tf_op jit(solution)/shard_map/convert_element_type | solution.py:249
  60.8 1.5 multiply_reduce_fusion.1
  64.1 1.2 bitcast_multiply_fusion.3
  65.3 4.3 %fusion.23 = f32[128,1280]{1,0:T(8,128)S(1)} fusion(f32[128,1280]{1,0:T(8,128)S(1)} %bitcast_multiply_fusion.3, bf16[128,1792]{1,0:T(8,128)(2,1)S(1)} %get-tuple-element.23.refs_1_, bf16[1,1280,1792]{2,1,0:T(8,128)(2,1)} %param.21, f32[1280]{0:T(1024)S(1)} %convert_reduce_fusion), kind=kOutput, calls=%fused_computation.21 | convolution fusion | flops 587530240 | bytes 6362112 | tf_op jit(solution)/shard_map/dot_general | solution.py:99
  69.8 1.1 convert_element_type.399
  72.8 3.0 %collective-permute-start.26 = (bf16[16,1280]{1,0:T(8,128)(2,1)S(1)}, bf16[16,1280]{1,0:T(8,128)(2,1)S(1)}, u32[]{:S(2)}, u32[]{:S(2)}) collective-permute-start(bf16[16,1280]{1,0:T(8,128)(2,1)S(1)} %get-tuple-element.62), channel_id=1, source_target_pairs={{0,12},{2,14},{4,0},{6,2},{8,4},{10,6},{12,8},{14,10},{1,13},{3,15... | collective-permute-start | bytes 122888 | tf_op jit(solution)/shard_map/ppermute | solution.py:31
  76.8 1.9 %collective-permute-start.28 = (bf16[16,1280]{1,0:T(8,128)(2,1)S(1)}, bf16[16,1280]{1,0:T(8,128)(2,1)S(1)}, u32[]{:S(2)}, u32[]{:S(2)}) collective-permute-start(bf16[16,1280]{1,0:T(8,128)(2,1)S(1)} %get-tuple-element.63), channel_id=1, source_target_pairs={{0,4},{2,6},{4,8},{6,10},{8,12},{10,14},{12,0},{14,2},{1,5},{3,7},... | collective-permute-start | bytes 122888 | tf_op jit(solution)/shard_map/ppermute | solution.py:31
  78.9 1.9 %collective-permute-start.6 = (bf16[16,1280]{1,0:T(8,128)(2,1)S(1)}, bf16[16,1280]{1,0:T(8,128)(2,1)S(1)}, u32[]{:S(2)}, u32[]{:S(2)}) collective-permute-start(bf16[16,1280]{1,0:T(8,128)(2,1)S(1)} %get-tuple-element.57), channel_id=1, source_target_pairs={{0,12},{2,14},{4,0},{6,2},{8,4},{10,6},{12,8},{14,10},{1,13},{3,15... | collective-permute-start | bytes 122888 | tf_op jit(solution)/shard_map/ppermute | solution.py:31
  82.7 1.3 collective-permute-start.29
  84.0 1.3 collective-permute-start.30
  85.3 1.3 collective-permute-start.31
  86.6 1.3 collective-permute-start.32
  88.0 6.0 %collective-permute-start.9 = (bf16[16,1280]{1,0:T(8,128)(2,1)S(1)}, bf16[16,1280]{1,0:T(8,128)(2,1)S(1)}, u32[]{:S(2)}, u32[]{:S(2)}) collective-permute-start(bf16[16,1280]{1,0:T(8,128)(2,1)S(1)} %fusion.70), channel_id=1, source_target_pairs={{0,16},{2,18},{4,20},{6,22},{8,24},{10,26},{12,28},{14,30},{1,17},... | collective-permute-start | bytes 122888 | tf_op jit(solution)/shard_map/ppermute | solution.py:53
  94.0 1.3 collective-permute-start.10
  95.4 1.8 %collective-permute-start.11 = (bf16[16,1280]{1,0:T(8,128)(2,1)S(1)}, bf16[16,1280]{1,0:T(8,128)(2,1)S(1)}, u32[]{:S(2)}, u32[]{:S(2)}) collective-permute-start(bf16[16,1280]{1,0:T(8,128)(2,1)S(1)} %fusion.70), channel_id=1, source_target_pairs={{0,24},{2,26},{4,28},{6,30},{8,16},{10,18},{12,20},{14,22},{1,25},... | collective-permute-start | bytes 122888 | tf_op jit(solution)/shard_map/ppermute | solution.py:53
  97.2 2.4 %collective-permute-start.12 = (bf16[16,1280]{1,0:T(8,128)(2,1)S(1)}, bf16[16,1280]{1,0:T(8,128)(2,1)S(1)}, u32[]{:S(2)}, u32[]{:S(2)}) collective-permute-start(bf16[16,1280]{1,0:T(8,128)(2,1)S(1)} %fusion.70), channel_id=1, source_target_pairs={{0,28},{2,30},{4,16},{6,18},{8,20},{10,22},{12,24},{14,26},{1,29},... | collective-permute-start | bytes 122888 | tf_op jit(solution)/shard_map/ppermute | solution.py:53
  99.7 1.3 collective-permute-done.12
  103.4 1.7 %fusion.139 = (bf16[128,1792]{1,0:T(8,128)(2,1)S(1)}, f32[128,1792]{1,0:T(8,128)}) fusion(bf16[128,1280]{1,0:T(8,128)(2,1)S(1)} %bitcast.322, bf16[1,1280,1792]{2,1,0:T(8,128)(2,1)S(1)} %bitcast.309), kind=kOutput, calls=%fused_computation.286 | convolution fusion | flops 587431936 | bytes 6291456 | tf_op jit(solution)/shard_map/dot_general | solution.py:81
  107.5 1.5 collective-permute-start.35
  109.0 5.0 %fusion.140 = (bf16[128,1792]{1,0:T(8,128)(2,1)}, f32[128,1792]{1,0:T(8,128)}) fusion(bf16[128,1280]{1,0:T(8,128)(2,1)S(1)} %bitcast.320, bf16[1,1792,1280]{2,1,0:T(8,128)(2,1)} %param.22), kind=kOutput, calls=%fused_computation.287 | convolution fusion | flops 587431936 | bytes 6291456 | tf_op jit(solution)/shard_map/dot_general | solution.py:99
  114.6 4.0 %fusion.141 = (bf16[128,1792]{1,0:T(8,128)(2,1)S(1)}, f32[128,1792]{1,0:T(8,128)}) fusion(bf16[128,1280]{1,0:T(8,128)(2,1)S(1)} %bitcast.321, bf16[1,1280,1792]{2,1,0:T(8,128)(2,1)} %param.21), kind=kOutput, calls=%fused_computation.288 | convolution fusion | flops 587431936 | bytes 6291456 | tf_op jit(solution)/shard_map/dot_general | solution.py:81
  118.8 1.6 collective-permute-start.14
  121.9 1.2 convert_element_type.463
  123.4 8.4 %collective-permute-done.34 = bf16[128,1792]{1,0:T(8,128)(2,1)} collective-permute-done((bf16[128,1792]{1,0:T(8,128)(2,1)}, bf16[128,1792]{1,0:T(8,128)(2,1)}, u32[]{:S(2)}, u32[]{:S(2)}) %collective-permute-start.34) | collective-permute-done | bytes 458784 | tf_op jit(solution)/shard_map/ppermute | solution.py:20
  131.8 2.2 %multiply_convert_fusion.2 = (bf16[128,1792]{1,0:T(8,128)(2,1)S(1)}, f32[128,1792]{1,0:T(8,128)S(1)}, bf16[128,1792]{1,0:T(8,128)(2,1)S(1)}) fusion(f32[128]{0:T(128)S(1)} %fusion.119, f32[128,1792]{1,0:T(8,128)} %get-tuple-element.101, f32[128,1920]{1,0:T(8,128)S(1)} %convert_element_type.463, f32[128,1792]{1,0:T(8,128)} %get-tuple-element.103, ...), kind=kLoop, calls=%fused_computation.37 | loop fusion | flops 3670016 | bytes 5046784 | tf_op jit(solution)/shard_map/convert_element_type | solution.py:249
  134.0 2.2 %block_grads.1 = bf16[8,128,128]{2,1,0:T(8,128)(2,1)S(1)} custom-call(s32[3,8]{1,0:T(4,128)S(1)} %pad_add_fusion.plan, bf16[128,1280]{1,0:T(8,128)(2,1)S(1)} %get-tuple-element.75.refs_0_, bf16[128,1792]{1,0:T(8,128)(2,1)S(1)} %get-tuple-element.23.refs_1_, bf16[128,1792]{1,0:T(8,128)(2,1)S(1)} %get-tuple-element.32.refs_2_, ...), custom_call_target="tpu_custom_call" | custom-call | tf_op jit(solution)/shard_map/block_grads/pallas_call | solution.py:134
  136.9 4.5 %collective-permute-done.14 = bf16[128,1920]{1,0:T(8,128)(2,1)S(1)} collective-permute-done((bf16[128,1920]{1,0:T(8,128)(2,1)S(1)}, bf16[128,1920]{1,0:T(8,128)(2,1)S(1)}, u32[]{:S(2)}, u32[]{:S(2)}) %collective-permute-start.14) | collective-permute-done | bytes 491552 | tf_op jit(solution)/shard_map/ppermute | solution.py:86
  143.2 1.1 fusion.76
  144.5 3.9 %fusion.29 = f32[128,1280]{1,0:T(8,128)S(1)} fusion(f32[128,1280]{1,0:T(8,128)S(1)} %bitcast_multiply_fusion.1, bf16[128,1792]{1,0:T(8,128)(2,1)S(1)} %get-tuple-element.17.refs_5_, bf16[1,1280,1792]{2,1,0:T(8,128)(2,1)} %param.21, f32[1280]{0:T(1024)S(1)} %convert_reduce_fusion), kind=kOutput, calls=%fused_computation.23 | convolution fusion | flops 587530240 | bytes 6362112 | tf_op jit(solution)/shard_map/dot_general | solution.py:99
  149.0 1.9 %collective-permute-start.41 = (bf16[2,128,128]{2,1,0:T(8,128)(2,1)S(1)}, bf16[2,128,128]{2,1,0:T(8,128)(2,1)S(1)}, u32[]{:S(2)}, u32[]{:S(2)}) collective-permute-start(bf16[2,128,128]{2,1,0:T(8,128)(2,1)S(1)} %get-tuple-element.44), channel_id=1, source_target_pairs={{0,12},{2,14},{4,0},{6,2},{8,4},{10,6},{12,8},{14,10},{1,13},{3,15... | collective-permute-start | bytes 196616 | tf_op jit(solution)/shard_map/ppermute | solution.py:31
  152.1 2.9 %collective-permute-start.16 = (bf16[16,1280]{1,0:T(8,128)(2,1)S(1)}, bf16[16,1280]{1,0:T(8,128)(2,1)S(1)}, u32[]{:S(2)}, u32[]{:S(2)}) collective-permute-start(bf16[16,1280]{1,0:T(8,128)(2,1)S(1)} %get-tuple-element.52), channel_id=1, source_target_pairs={{0,12},{2,14},{4,0},{6,2},{8,4},{10,6},{12,8},{14,10},{1,13},{3,15... | collective-permute-start | bytes 122888 | tf_op jit(solution)/shard_map/ppermute | solution.py:31
  156.3 3.5 %collective-permute-done.42 = bf16[2,128,128]{2,1,0:T(8,128)(2,1)S(1)} collective-permute-done((bf16[2,128,128]{2,1,0:T(8,128)(2,1)S(1)}, bf16[2,128,128]{2,1,0:T(8,128)(2,1)S(1)}, u32[]{:S(2)}, u32[]{:S(2)}) %collective-permute-start.42) | collective-permute-done | bytes 65568 | tf_op jit(solution)/shard_map/ppermute | solution.py:31
  160.7 1.3 collective-permute-start.38
  162.8 5.0 %adam_step.1 = (f32[6,128,128]{2,1,0:T(8,128)}, f32[6,128,128]{2,1,0:T(8,128)}, f32[6,128,128]{2,1,0:T(8,128)}) custom-call(s32[2,6]{1,0:T(2,128)} %pad_add_fusion.1.plan, bf16[8,128,128]{2,1,0:T(8,128)(2,1)} %bitcast.329, f32[6,128,128]{2,1,0:T(8,128)} %bitcast.335, f32[6,128,128]{2,1,0:T(8,128)} %bitcast.336), custom_call_target="tpu_custom_call" | custom-call | tf_op jit(solution)/shard_map/adam_step/pallas_call | solution.py:173
  (219 shorter events, 36.6 us)
Async XLA Ops:
  3.8 19.8 %collective-permute-start = (bf16[3,16,1280]{2,1,0:T(8,128)(2,1)S(1)}, bf16[3,16,1280]{2,1,0:T(8,128)(2,1)S(1)}, u32[]{:S(2)}, u32[]{:S(2)}) collective-permute-start(bf16[3,16,1280]{2,1,0:T(8,128)(2,1)S(1)} %get-tuple-element.66), channel_id=1, source_target_pairs={{0,4},{2,6},{4,8},{6,10},{8,12},{10,14},{12,0},{14,2},{1,5},{3,7},... | collective-permute-start | bytes 368648 | tf_op jit(solution)/shard_map/ppermute | solution.py:31
  6.9 16.7 %collective-permute-start.1 = (bf16[3,16,1280]{2,1,0:T(8,128)(2,1)S(1)}, bf16[3,16,1280]{2,1,0:T(8,128)(2,1)S(1)}, u32[]{:S(2)}, u32[]{:S(2)}) collective-permute-start(bf16[3,16,1280]{2,1,0:T(8,128)(2,1)S(1)} %get-tuple-element.66), channel_id=1, source_target_pairs={{0,8},{2,10},{4,12},{6,14},{8,0},{10,2},{12,4},{14,6},{1,9},{3,11}... | collective-permute-start | bytes 368648 | tf_op jit(solution)/shard_map/ppermute | solution.py:31
  10.3 9.9 %collective-permute-start.19 = (bf16[2,16,1280]{2,1,0:T(8,128)(2,1)S(1)}, bf16[2,16,1280]{2,1,0:T(8,128)(2,1)S(1)}, u32[]{:S(2)}, u32[]{:S(2)}) collective-permute-start(bf16[2,16,1280]{2,1,0:T(8,128)(2,1)S(1)} %get-tuple-element.72), channel_id=1, source_target_pairs={{0,4},{2,6},{4,8},{6,10},{8,12},{10,14},{12,0},{14,2},{1,5},{3,7},... | collective-permute-start | bytes 245768 | tf_op jit(solution)/shard_map/ppermute | solution.py:31
  10.4 12.5 %collective-permute-start.20 = (bf16[2,16,1280]{2,1,0:T(8,128)(2,1)S(1)}, bf16[2,16,1280]{2,1,0:T(8,128)(2,1)S(1)}, u32[]{:S(2)}, u32[]{:S(2)}) collective-permute-start(bf16[2,16,1280]{2,1,0:T(8,128)(2,1)S(1)} %get-tuple-element.72), channel_id=1, source_target_pairs={{0,8},{2,10},{4,12},{6,14},{8,0},{10,2},{12,4},{14,6},{1,9},{3,11}... | collective-permute-start | bytes 245768 | tf_op jit(solution)/shard_map/ppermute | solution.py:31
  12.2 10.6 %collective-permute-start.21 = (bf16[2,16,1280]{2,1,0:T(8,128)(2,1)S(1)}, bf16[2,16,1280]{2,1,0:T(8,128)(2,1)S(1)}, u32[]{:S(2)}, u32[]{:S(2)}) collective-permute-start(bf16[2,16,1280]{2,1,0:T(8,128)(2,1)S(1)} %get-tuple-element.72), channel_id=1, source_target_pairs={{0,12},{2,14},{4,0},{6,2},{8,4},{10,6},{12,8},{14,10},{1,13},{3,15... | collective-permute-start | bytes 245768 | tf_op jit(solution)/shard_map/ppermute | solution.py:31
  20.2 7.8 %collective-permute-start.2 = (bf16[3,16,1280]{2,1,0:T(8,128)(2,1)S(1)}, bf16[3,16,1280]{2,1,0:T(8,128)(2,1)S(1)}, u32[]{:S(2)}, u32[]{:S(2)}) collective-permute-start(bf16[3,16,1280]{2,1,0:T(8,128)(2,1)S(1)} %get-tuple-element.66), channel_id=1, source_target_pairs={{0,12},{2,14},{4,0},{6,2},{8,4},{10,6},{12,8},{14,10},{1,13},{3,15... | collective-permute-start | bytes 368648 | tf_op jit(solution)/shard_map/ppermute | solution.py:31
  22.9 5.2 %collective-permute-start.22 = (bf16[2,4,16,1280]{3,2,1,0:T(8,128)(2,1)S(1)}, bf16[2,4,16,1280]{3,2,1,0:T(8,128)(2,1)S(1)}, u32[]{:S(2)}, u32[]{:S(2)}) collective-permute-start(bf16[2,4,16,1280]{3,2,1,0:T(8,128)(2,1)S(1)} %get-tuple-element.42), channel_id=1, source_target_pairs={{0,2},{2,0},{4,6},{6,4},{8,10},{10,8},{12,14},{14,12},{1,3},{3,1},... | collective-permute-start | bytes 983048 | tf_op jit(solution)/shard_map/ppermute | solution.py:26
  28.0 5.3 %collective-permute-start.3 = (bf16[3,4,16,1280]{3,2,1,0:T(8,128)(2,1)S(1)}, bf16[3,4,16,1280]{3,2,1,0:T(8,128)(2,1)S(1)}, u32[]{:S(2)}, u32[]{:S(2)}) collective-permute-start(bf16[3,4,16,1280]{3,2,1,0:T(8,128)(2,1)S(1)} %get-tuple-element.36), channel_id=1, source_target_pairs={{0,2},{2,0},{4,6},{6,4},{8,10},{10,8},{12,14},{14,12},{1,3},{3,1},... | collective-permute-start | bytes 1474568 | tf_op jit(solution)/shard_map/ppermute | solution.py:26
  33.2 25.5 %collective-permute-start.23 = (bf16[128,1792]{1,0:T(8,128)(2,1)}, bf16[128,1792]{1,0:T(8,128)(2,1)}, u32[]{:S(2)}, u32[]{:S(2)}) collective-permute-start(bf16[128,1792]{1,0:T(8,128)(2,1)} %get-tuple-element.96), channel_id=1, source_target_pairs={{0,1},{1,0},{2,3},{3,2},{4,5},{5,4},{6,7},{7,6},{8,9},{9,8},{10,11... | collective-permute-start | bytes 1376264 | tf_op jit(solution)/shard_map/ppermute | solution.py:20
  40.5 16.9 %collective-permute-start.24 = (bf16[128,1920]{1,0:T(8,128)(2,1)}, bf16[128,1920]{1,0:T(8,128)(2,1)}, u32[]{:S(2)}, u32[]{:S(2)}) collective-permute-start(bf16[128,1920]{1,0:T(8,128)(2,1)} %pad_maximum_fusion.3), channel_id=1, source_target_pairs={{0,1},{1,0},{2,3},{3,2},{4,5},{5,4},{6,7},{7,6},{8,9},{9,8},{10,11... | collective-permute-start | bytes 1474568 | tf_op jit(solution)/shard_map/ppermute | solution.py:86
  47.4 22.4 %collective-permute-start.4 = (bf16[128,1920]{1,0:T(8,128)(2,1)}, bf16[128,1920]{1,0:T(8,128)(2,1)}, u32[]{:S(2)}, u32[]{:S(2)}) collective-permute-start(bf16[128,1920]{1,0:T(8,128)(2,1)} %pad_maximum_fusion.1), channel_id=1, source_target_pairs={{0,1},{1,0},{2,3},{3,2},{4,5},{5,4},{6,7},{7,6},{8,9},{9,8},{10,11... | collective-permute-start | bytes 1474568 | tf_op jit(solution)/shard_map/ppermute | solution.py:86
  69.7 3.1 %collective-permute-start.25 = (bf16[4,16,1280]{2,1,0:T(8,128)(2,1)S(1)}, bf16[4,16,1280]{2,1,0:T(8,128)(2,1)S(1)}, u32[]{:S(2)}, u32[]{:S(2)}) collective-permute-start(bf16[4,16,1280]{2,1,0:T(8,128)(2,1)S(1)} %bitcast.342), channel_id=1, source_target_pairs={{0,2},{2,0},{4,6},{6,4},{8,10},{10,8},{12,14},{14,12},{1,3},{3,1},... | collective-permute-start | bytes 491528 | tf_op jit(solution)/shard_map/ppermute | solution.py:26
  71.1 32.2 %slice-start = ((s8[4587520]{0:T(1024)(128)(4,1)}), s8[393216]{0:T(1024)(128)(4,1)S(1)}, s32[]{:S(2)}) async-start(s8[4587520]{0:T(1024)(128)(4,1)} %bitcast.308), calls=%async_computation | async-start | bytes 786432
  72.1 29.1 %copy-start.3 = (bf16[3,4,16,1280]{3,2,1,0:T(8,128)(2,1)S(1)}, bf16[3,4,16,1280]{3,2,1,0:T(8,128)(2,1)}, u32[]{:S(2)}) copy-start(bf16[3,4,16,1280]{3,2,1,0:T(8,128)(2,1)} %copy-done.2) | copy-start | bytes 1474564
  72.1 30.4 %copy-start.5 = (bf16[1,2,4,16,1280]{4,3,2,1,0:T(8,128)(2,1)S(1)}, bf16[1,2,4,16,1280]{4,3,2,1,0:T(8,128)(2,1)}, u32[]{:S(2)}) copy-start(bf16[1,2,4,16,1280]{4,3,2,1,0:T(8,128)(2,1)} %get-tuple-element.12) | copy-start | bytes 983044
  72.1 31.2 %slice-start.1 = ((s8[4587520]{0:T(1024)(128)(4,1)}), s8[4194304]{0:T(1024)(128)(4,1)S(1)}, s32[]{:S(2)}) async-start(s8[4587520]{0:T(1024)(128)(4,1)} %bitcast.308), calls=%async_computation.1 | async-start | bytes 8388608
  72.2 6.6 %collective-permute-start.5 = (bf16[4,16,1280]{2,1,0:T(8,128)(2,1)S(1)}, bf16[4,16,1280]{2,1,0:T(8,128)(2,1)S(1)}, u32[]{:S(2)}, u32[]{:S(2)}) collective-permute-start(bf16[4,16,1280]{2,1,0:T(8,128)(2,1)S(1)} %bitcast.341), channel_id=1, source_target_pairs={{0,2},{2,0},{4,6},{6,4},{8,10},{10,8},{12,14},{14,12},{1,3},{3,1},... | collective-permute-start | bytes 491528 | tf_op jit(solution)/shard_map/ppermute | solution.py:26
  72.8 8.1 %collective-permute-start.26 = (bf16[16,1280]{1,0:T(8,128)(2,1)S(1)}, bf16[16,1280]{1,0:T(8,128)(2,1)S(1)}, u32[]{:S(2)}, u32[]{:S(2)}) collective-permute-start(bf16[16,1280]{1,0:T(8,128)(2,1)S(1)} %get-tuple-element.62), channel_id=1, source_target_pairs={{0,12},{2,14},{4,0},{6,2},{8,4},{10,6},{12,8},{14,10},{1,13},{3,15... | collective-permute-start | bytes 122888 | tf_op jit(solution)/shard_map/ppermute | solution.py:31
  75.8 6.2 %collective-permute-start.27 = (bf16[16,1280]{1,0:T(8,128)(2,1)S(1)}, bf16[16,1280]{1,0:T(8,128)(2,1)S(1)}, u32[]{:S(2)}, u32[]{:S(2)}) collective-permute-start(bf16[16,1280]{1,0:T(8,128)(2,1)S(1)} %get-tuple-element.64), channel_id=1, source_target_pairs={{0,8},{2,10},{4,12},{6,14},{8,0},{10,2},{12,4},{14,6},{1,9},{3,11}... | collective-permute-start | bytes 122888 | tf_op jit(solution)/shard_map/ppermute | solution.py:31
  76.8 5.8 %collective-permute-start.28 = (bf16[16,1280]{1,0:T(8,128)(2,1)S(1)}, bf16[16,1280]{1,0:T(8,128)(2,1)S(1)}, u32[]{:S(2)}, u32[]{:S(2)}) collective-permute-start(bf16[16,1280]{1,0:T(8,128)(2,1)S(1)} %get-tuple-element.63), channel_id=1, source_target_pairs={{0,4},{2,6},{4,8},{6,10},{8,12},{10,14},{12,0},{14,2},{1,5},{3,7},... | collective-permute-start | bytes 122888 | tf_op jit(solution)/shard_map/ppermute | solution.py:31
  78.9 6.5 %collective-permute-start.6 = (bf16[16,1280]{1,0:T(8,128)(2,1)S(1)}, bf16[16,1280]{1,0:T(8,128)(2,1)S(1)}, u32[]{:S(2)}, u32[]{:S(2)}) collective-permute-start(bf16[16,1280]{1,0:T(8,128)(2,1)S(1)} %get-tuple-element.57), channel_id=1, source_target_pairs={{0,12},{2,14},{4,0},{6,2},{8,4},{10,6},{12,8},{14,10},{1,13},{3,15... | collective-permute-start | bytes 122888 | tf_op jit(solution)/shard_map/ppermute | solution.py:31
  80.8 5.8 %collective-permute-start.7 = (bf16[16,1280]{1,0:T(8,128)(2,1)S(1)}, bf16[16,1280]{1,0:T(8,128)(2,1)S(1)}, u32[]{:S(2)}, u32[]{:S(2)}) collective-permute-start(bf16[16,1280]{1,0:T(8,128)(2,1)S(1)} %get-tuple-element.59), channel_id=1, source_target_pairs={{0,8},{2,10},{4,12},{6,14},{8,0},{10,2},{12,4},{14,6},{1,9},{3,11}... | collective-permute-start | bytes 122888 | tf_op jit(solution)/shard_map/ppermute | solution.py:31
  80.9 7.1 %collective-permute-start.8 = (bf16[16,1280]{1,0:T(8,128)(2,1)S(1)}, bf16[16,1280]{1,0:T(8,128)(2,1)S(1)}, u32[]{:S(2)}, u32[]{:S(2)}) collective-permute-start(bf16[16,1280]{1,0:T(8,128)(2,1)S(1)} %get-tuple-element.58), channel_id=1, source_target_pairs={{0,4},{2,6},{4,8},{6,10},{8,12},{10,14},{12,0},{14,2},{1,5},{3,7},... | collective-permute-start | bytes 122888 | tf_op jit(solution)/shard_map/ppermute | solution.py:31
  82.7 11.3 %collective-permute-start.29 = (bf16[16,1280]{1,0:T(8,128)(2,1)S(1)}, bf16[16,1280]{1,0:T(8,128)(2,1)S(1)}, u32[]{:S(2)}, u32[]{:S(2)}) collective-permute-start(bf16[16,1280]{1,0:T(8,128)(2,1)S(1)} %fusion.60), channel_id=1, source_target_pairs={{16,0},{18,2},{20,4},{22,6},{24,8},{26,10},{28,12},{30,14},{17,1},... | collective-permute-start | bytes 122888 | tf_op jit(solution)/shard_map/ppermute | solution.py:53
  84.0 11.3 %collective-permute-start.30 = (bf16[16,1280]{1,0:T(8,128)(2,1)S(1)}, bf16[16,1280]{1,0:T(8,128)(2,1)S(1)}, u32[]{:S(2)}, u32[]{:S(2)}) collective-permute-start(bf16[16,1280]{1,0:T(8,128)(2,1)S(1)} %fusion.60), channel_id=1, source_target_pairs={{16,4},{18,6},{20,8},{22,10},{24,12},{26,14},{28,0},{30,2},{17,5},... | collective-permute-start | bytes 122888 | tf_op jit(solution)/shard_map/ppermute | solution.py:53
  85.3 11.8 %collective-permute-start.31 = (bf16[16,1280]{1,0:T(8,128)(2,1)S(1)}, bf16[16,1280]{1,0:T(8,128)(2,1)S(1)}, u32[]{:S(2)}, u32[]{:S(2)}) collective-permute-start(bf16[16,1280]{1,0:T(8,128)(2,1)S(1)} %fusion.60), channel_id=1, source_target_pairs={{16,8},{18,10},{20,12},{22,14},{24,0},{26,2},{28,4},{30,6},{17,9},... | collective-permute-start | bytes 122888 | tf_op jit(solution)/shard_map/ppermute | solution.py:53
  86.6 12.9 %collective-permute-start.32 = (bf16[16,1280]{1,0:T(8,128)(2,1)S(1)}, bf16[16,1280]{1,0:T(8,128)(2,1)S(1)}, u32[]{:S(2)}, u32[]{:S(2)}) collective-permute-start(bf16[16,1280]{1,0:T(8,128)(2,1)S(1)} %fusion.60), channel_id=1, source_target_pairs={{16,12},{18,14},{20,0},{22,2},{24,4},{26,6},{28,8},{30,10},{17,13}... | collective-permute-start | bytes 122888 | tf_op jit(solution)/shard_map/ppermute | solution.py:53
  88.0 11.7 %collective-permute-start.9 = (bf16[16,1280]{1,0:T(8,128)(2,1)S(1)}, bf16[16,1280]{1,0:T(8,128)(2,1)S(1)}, u32[]{:S(2)}, u32[]{:S(2)}) collective-permute-start(bf16[16,1280]{1,0:T(8,128)(2,1)S(1)} %fusion.70), channel_id=1, source_target_pairs={{0,16},{2,18},{4,20},{6,22},{8,24},{10,26},{12,28},{14,30},{1,17},... | collective-permute-start | bytes 122888 | tf_op jit(solution)/shard_map/ppermute | solution.py:53
  94.0 5.6 %collective-permute-start.10 = (bf16[16,1280]{1,0:T(8,128)(2,1)S(1)}, bf16[16,1280]{1,0:T(8,128)(2,1)S(1)}, u32[]{:S(2)}, u32[]{:S(2)}) collective-permute-start(bf16[16,1280]{1,0:T(8,128)(2,1)S(1)} %fusion.70), channel_id=1, source_target_pairs={{0,20},{2,22},{4,24},{6,26},{8,28},{10,30},{12,16},{14,18},{1,21},... | collective-permute-start | bytes 122888 | tf_op jit(solution)/shard_map/ppermute | solution.py:53
  95.4 4.3 %collective-permute-start.11 = (bf16[16,1280]{1,0:T(8,128)(2,1)S(1)}, bf16[16,1280]{1,0:T(8,128)(2,1)S(1)}, u32[]{:S(2)}, u32[]{:S(2)}) collective-permute-start(bf16[16,1280]{1,0:T(8,128)(2,1)S(1)} %fusion.70), channel_id=1, source_target_pairs={{0,24},{2,26},{4,28},{6,30},{8,16},{10,18},{12,20},{14,22},{1,25},... | collective-permute-start | bytes 122888 | tf_op jit(solution)/shard_map/ppermute | solution.py:53
  97.2 3.9 %collective-permute-start.12 = (bf16[16,1280]{1,0:T(8,128)(2,1)S(1)}, bf16[16,1280]{1,0:T(8,128)(2,1)S(1)}, u32[]{:S(2)}, u32[]{:S(2)}) collective-permute-start(bf16[16,1280]{1,0:T(8,128)(2,1)S(1)} %fusion.70), channel_id=1, source_target_pairs={{0,28},{2,30},{4,16},{6,18},{8,20},{10,22},{12,24},{14,26},{1,29},... | collective-permute-start | bytes 122888 | tf_op jit(solution)/shard_map/ppermute | solution.py:53
  99.6 1.5 collective-permute-start.33
  101.0 1.5 collective-permute-start.13
  107.5 14.4 %collective-permute-start.35 = (bf16[128,1920]{1,0:T(8,128)(2,1)}, bf16[128,1920]{1,0:T(8,128)(2,1)}, u32[]{:S(2)}, u32[]{:S(2)}) collective-permute-start(bf16[128,1920]{1,0:T(8,128)(2,1)} %pad_maximum_fusion.4), channel_id=1, source_target_pairs={{0,1},{1,0},{2,3},{3,2},{4,5},{5,4},{6,7},{7,6},{8,9},{9,8},{10,11... | collective-permute-start | bytes 1474568 | tf_op jit(solution)/shard_map/ppermute | solution.py:86
  114.1 17.7 %collective-permute-start.34 = (bf16[128,1792]{1,0:T(8,128)(2,1)}, bf16[128,1792]{1,0:T(8,128)(2,1)}, u32[]{:S(2)}, u32[]{:S(2)}) collective-permute-start(bf16[128,1792]{1,0:T(8,128)(2,1)} %get-tuple-element.102), channel_id=1, source_target_pairs={{0,1},{1,0},{2,3},{3,2},{4,5},{5,4},{6,7},{7,6},{8,9},{9,8},{10,11... | collective-permute-start | bytes 1376264 | tf_op jit(solution)/shard_map/ppermute | solution.py:20
  118.8 22.5 %collective-permute-start.14 = (bf16[128,1920]{1,0:T(8,128)(2,1)S(1)}, bf16[128,1920]{1,0:T(8,128)(2,1)S(1)}, u32[]{:S(2)}, u32[]{:S(2)}) collective-permute-start(bf16[128,1920]{1,0:T(8,128)(2,1)S(1)} %pad_maximum_fusion.2), channel_id=1, source_target_pairs={{0,1},{1,0},{2,3},{3,2},{4,5},{5,4},{6,7},{7,6},{8,9},{9,8},{10,11... | collective-permute-start | bytes 1474568 | tf_op jit(solution)/shard_map/ppermute | solution.py:86
  136.9 12.1 %collective-permute-start.40 = (bf16[4,128,128]{2,1,0:T(8,128)(2,1)}, bf16[4,128,128]{2,1,0:T(8,128)(2,1)S(1)}, u32[]{:S(2)}, u32[]{:S(2)}) collective-permute-start(bf16[4,128,128]{2,1,0:T(8,128)(2,1)} %get-tuple-element.48), channel_id=1, source_target_pairs={{0,2},{2,0},{4,6},{6,4},{8,10},{10,8},{12,14},{14,12},{1,3},{3,1},... | collective-permute-start | bytes 393224 | tf_op jit(solution)/shard_map/ppermute | solution.py:26
  142.6 9.4 %collective-permute-start.15 = (bf16[4,16,1280]{2,1,0:T(8,128)(2,1)S(1)}, bf16[4,16,1280]{2,1,0:T(8,128)(2,1)S(1)}, u32[]{:S(2)}, u32[]{:S(2)}) collective-permute-start(bf16[4,16,1280]{2,1,0:T(8,128)(2,1)S(1)} %bitcast.339), channel_id=1, source_target_pairs={{0,2},{2,0},{4,6},{6,4},{8,10},{10,8},{12,14},{14,12},{1,3},{3,1},... | collective-permute-start | bytes 491528 | tf_op jit(solution)/shard_map/ppermute | solution.py:26
  148.6 6.5 %collective-permute-start.36 = (bf16[4,16,1280]{2,1,0:T(8,128)(2,1)S(1)}, bf16[4,16,1280]{2,1,0:T(8,128)(2,1)S(1)}, u32[]{:S(2)}, u32[]{:S(2)}) collective-permute-start(bf16[4,16,1280]{2,1,0:T(8,128)(2,1)S(1)} %bitcast.340), channel_id=1, source_target_pairs={{0,2},{2,0},{4,6},{6,4},{8,10},{10,8},{12,14},{14,12},{1,3},{3,1},... | collective-permute-start | bytes 491528 | tf_op jit(solution)/shard_map/ppermute | solution.py:26
  149.0 7.1 %collective-permute-start.41 = (bf16[2,128,128]{2,1,0:T(8,128)(2,1)S(1)}, bf16[2,128,128]{2,1,0:T(8,128)(2,1)S(1)}, u32[]{:S(2)}, u32[]{:S(2)}) collective-permute-start(bf16[2,128,128]{2,1,0:T(8,128)(2,1)S(1)} %get-tuple-element.44), channel_id=1, source_target_pairs={{0,12},{2,14},{4,0},{6,2},{8,4},{10,6},{12,8},{14,10},{1,13},{3,15... | collective-permute-start | bytes 196616 | tf_op jit(solution)/shard_map/ppermute | solution.py:31
  150.9 8.9 %collective-permute-start.42 = (bf16[2,128,128]{2,1,0:T(8,128)(2,1)S(1)}, bf16[2,128,128]{2,1,0:T(8,128)(2,1)S(1)}, u32[]{:S(2)}, u32[]{:S(2)}) collective-permute-start(bf16[2,128,128]{2,1,0:T(8,128)(2,1)S(1)} %get-tuple-element.46), channel_id=1, source_target_pairs={{0,8},{2,10},{4,12},{6,14},{8,0},{10,2},{12,4},{14,6},{1,9},{3,11}... | collective-permute-start | bytes 196616 | tf_op jit(solution)/shard_map/ppermute | solution.py:31
  151.1 9.6 %collective-permute-start.43 = (bf16[2,128,128]{2,1,0:T(8,128)(2,1)S(1)}, bf16[2,128,128]{2,1,0:T(8,128)(2,1)S(1)}, u32[]{:S(2)}, u32[]{:S(2)}) collective-permute-start(bf16[2,128,128]{2,1,0:T(8,128)(2,1)S(1)} %get-tuple-element.45), channel_id=1, source_target_pairs={{0,4},{2,6},{4,8},{6,10},{8,12},{10,14},{12,0},{14,2},{1,5},{3,7},... | collective-permute-start | bytes 196616 | tf_op jit(solution)/shard_map/ppermute | solution.py:31
  152.1 9.9 %collective-permute-start.16 = (bf16[16,1280]{1,0:T(8,128)(2,1)S(1)}, bf16[16,1280]{1,0:T(8,128)(2,1)S(1)}, u32[]{:S(2)}, u32[]{:S(2)}) collective-permute-start(bf16[16,1280]{1,0:T(8,128)(2,1)S(1)} %get-tuple-element.52), channel_id=1, source_target_pairs={{0,12},{2,14},{4,0},{6,2},{8,4},{10,6},{12,8},{14,10},{1,13},{3,15... | collective-permute-start | bytes 122888 | tf_op jit(solution)/shard_map/ppermute | solution.py:31
  155.0 12.7 %collective-permute-start.17 = (bf16[16,1280]{1,0:T(8,128)(2,1)S(1)}, bf16[16,1280]{1,0:T(8,128)(2,1)S(1)}, u32[]{:S(2)}, u32[]{:S(2)}) collective-permute-start(bf16[16,1280]{1,0:T(8,128)(2,1)S(1)} %get-tuple-element.54), channel_id=1, source_target_pairs={{0,8},{2,10},{4,12},{6,14},{8,0},{10,2},{12,4},{14,6},{1,9},{3,11}... | collective-permute-start | bytes 122888 | tf_op jit(solution)/shard_map/ppermute | solution.py:31
  156.1 11.7 %collective-permute-start.18 = (bf16[16,1280]{1,0:T(8,128)(2,1)S(1)}, bf16[16,1280]{1,0:T(8,128)(2,1)S(1)}, u32[]{:S(2)}, u32[]{:S(2)}) collective-permute-start(bf16[16,1280]{1,0:T(8,128)(2,1)S(1)} %get-tuple-element.53), channel_id=1, source_target_pairs={{0,4},{2,6},{4,8},{6,10},{8,12},{10,14},{12,0},{14,2},{1,5},{3,7},... | collective-permute-start | bytes 122888 | tf_op jit(solution)/shard_map/ppermute | solution.py:31
  159.8 7.9 %collective-permute-start.37 = (bf16[16,1280]{1,0:T(8,128)(2,1)S(1)}, bf16[16,1280]{1,0:T(8,128)(2,1)S(1)}, u32[]{:S(2)}, u32[]{:S(2)}) collective-permute-start(bf16[16,1280]{1,0:T(8,128)(2,1)S(1)} %get-tuple-element.49), channel_id=1, source_target_pairs={{0,12},{2,14},{4,0},{6,2},{8,4},{10,6},{12,8},{14,10},{1,13},{3,15... | collective-permute-start | bytes 122888 | tf_op jit(solution)/shard_map/ppermute | solution.py:31
  160.7 7.0 %collective-permute-start.38 = (bf16[16,1280]{1,0:T(8,128)(2,1)S(1)}, bf16[16,1280]{1,0:T(8,128)(2,1)S(1)}, u32[]{:S(2)}, u32[]{:S(2)}) collective-permute-start(bf16[16,1280]{1,0:T(8,128)(2,1)S(1)} %get-tuple-element.51), channel_id=1, source_target_pairs={{0,8},{2,10},{4,12},{6,14},{8,0},{10,2},{12,4},{14,6},{1,9},{3,11}... | collective-permute-start | bytes 122888 | tf_op jit(solution)/shard_map/ppermute | solution.py:31
  162.0 5.8 %collective-permute-start.39 = (bf16[16,1280]{1,0:T(8,128)(2,1)S(1)}, bf16[16,1280]{1,0:T(8,128)(2,1)S(1)}, u32[]{:S(2)}, u32[]{:S(2)}) collective-permute-start(bf16[16,1280]{1,0:T(8,128)(2,1)S(1)} %get-tuple-element.50), channel_id=1, source_target_pairs={{0,4},{2,6},{4,8},{6,10},{8,12},{10,14},{12,0},{14,2},{1,5},{3,7},... | collective-permute-start | bytes 122888 | tf_op jit(solution)/shard_map/ppermute | solution.py:31
  (29 other events, 339.1 us)

commit v2 on v0

v2 whole, which is shorter than its diff:
```python
import functools

import jax
import jax.numpy as jnp
from jax import lax
from jax.experimental import pallas as pl
from jax.experimental.pallas import tpu as pltpu
from jax.sharding import PartitionSpec as P

BLK = 128
EPSILON = 1e-06
BF16 = jnp.bfloat16
F32 = jnp.float32
MIB = 1024 * 1024
VMEM = pl.BlockSpec(memory_space=pltpu.VMEM)
SMEM = pl.BlockSpec(memory_space=pltpu.SMEM)
HBM = pl.BlockSpec(memory_space=pltpu.HBM)
ANY = pl.BlockSpec(memory_space=pl.ANY)
DP, COUNT, OWNERS = range(3)


def later(values, *before):
    return lax.optimization_barrier((values, before))[0]


def sibling(value):
    return lax.ppermute(value, "dp", [(d, d ^ 1) for d in range(lax.axis_size("dp"))])


def shifted(value, steps):
    count = lax.axis_size("dp")
    return lax.ppermute(value, "dp", [(d, (d + 2 * steps) % count) for d in range(count)])


def moved_rows(local):
    depth = lax.axis_size("dp") // 2
    return [local] + [shifted(local, k) for k in range(1, depth)]


def moved_passed(down, up=None):
    sections = lax.axis_size("section")
    count = lax.axis_size("dp")

    def moved(local, direction, k):
        pairs = [
            (s * count + d, (s + direction) % sections * count + (d + 2 * k) % count)
            for s in range(sections)
            for d in range(count)
        ]
        return lax.ppermute(local, ("section", "dp"), pairs)

    both = down[None] if up is None else jnp.stack([down, up])
    if sections == 2:
        return [moved(both, 1, k) for k in range(count // 2)]
    return [jnp.stack([moved(down, -1, k), moved(up, 1, k)]) for k in range(count // 2)]


def halves(pieces):
    mine = jnp.concatenate(pieces, axis=-2)
    return mine, sibling(mine)


def scatter_pairs(kept, sent):
    depth = lax.axis_size("dp") // 2
    return (kept + sibling(sent).astype(F32)).reshape((depth, kept.shape[0] // depth, kept.shape[1]))


def scatter_parts(pairs):
    return [pairs[0]] + [shifted(pairs[k].astype(BF16), -k) for k in range(1, pairs.shape[0])]


def added(rows, parts):
    return sum([part.astype(F32) for part in parts], rows.astype(F32)).astype(BF16)


def tensor_parts(value):
    count = lax.axis_size("tensor")
    step = 1
    while True:
        got = lax.ppermute(value, "tensor", [(t, t ^ step) for t in range(count)])
        step *= 2
        if step >= count:
            return value, got
        value = value + got


def tile_of(size):
    return 256 if size % 256 == 0 else BLK


def call(kernel, name, outs, operands, specs, flops, moved, scratch=()):
    return pl.pallas_call(
        kernel,
        out_shape=outs,
        in_specs=specs,
        out_specs=[VMEM] * len(outs),
        scratch_shapes=scratch,
        compiler_params=pltpu.CompilerParams(vmem_limit_bytes=12 * MIB),
        cost_estimate=pl.CostEstimate(flops=flops, bytes_accessed=moved, transcendentals=0),
        name=name,
    )(*operands)


def struct(*shape, dtype=BF16):
    return jax.ShapeDtypeStruct(shape, dtype)


def nt_dot(left, right):
    return lax.dot_general(left, right, (((1,), (1,)), ((), ())), preferred_element_type=F32)


def load_kernel(up_in, down_in, after, up, down, sems):
    copies = [pltpu.make_async_copy(up_in, up, sems.at[0]), pltpu.make_async_copy(down_in, down, sems.at[1])]
    for copy in copies:
        copy.start()
    for copy in copies:
        copy.wait()


def load_weights(up, down, after):
    return pl.pallas_call(
        load_kernel,
        out_shape=[pltpu.VMEM(up.shape, BF16), pltpu.VMEM(down.shape, BF16)],
        in_specs=[HBM] * 2 + [ANY],
        out_specs=[VMEM] * 2,
        scratch_shapes=[pltpu.SemaphoreType.DMA((2,))],
        compiler_params=pltpu.CompilerParams(vmem_limit_bytes=16 * MIB),
        name="load_weights",
    )(in_hbm(up), in_hbm(down), after)


def in_hbm(value):
    return pltpu.with_memory_space_constraint(value, pltpu.HBM)


def write_products(rows, gain, up, sent, normed):
    widened = rows.astype(F32)
    squares = jnp.sum(widened * widened, axis=1, keepdims=True)
    normed[...] = (widened * gain[...].astype(F32)).astype(BF16)
    hidden = up.shape[1]
    step = tile_of(hidden)
    for n in range(0, hidden, step):
        sent[:, n : n + step] = jnp.dot(normed[...], up[:, n : n + step], preferred_element_type=F32).astype(BF16)
    coarse = squares.astype(BF16).astype(F32)
    lane = lax.broadcasted_iota(jnp.int32, (rows.shape[0], BLK), 1)
    sent[:, hidden:] = jnp.where(lane == 0, coarse, jnp.where(lane == 1, squares - coarse, 0.0)).astype(BF16)


def write_act_grads(grads, down, sent):
    hidden = down.shape[0]
    step = tile_of(hidden)
    for n in range(0, hidden, step):
        sent[:, n : n + step] = nt_dot(grads[...], down[n : n + step, :]).astype(BF16)


def joined(low, high):
    return jnp.concatenate([low[...], high[...]], axis=0)


def product_kernel(low, high, gain, up, _, sent, normed):
    write_products(joined(low, high), gain, up, sent, normed)


def products(row_halves, gain, up, down):
    rows = 2 * row_halves[0].shape[0]
    channels, hidden = up.shape
    return call(
        product_kernel, "products", [struct(rows, hidden + BLK)],
        [*row_halves, gain, up, down], [VMEM] * 5, 2 * rows * channels * hidden, 2 * channels * hidden,
        [pltpu.VMEM((rows, channels), BF16)],
    )[0]


def act_kernel(low, high, down, _, sent, grads):
    grads[...] = joined(low, high)
    write_act_grads(grads, down, sent)


def act_grads(grad_halves, up, down):
    rows = 2 * grad_halves[0].shape[0]
    hidden, channels = down.shape
    return call(
        act_kernel, "act_grads", [struct(rows, hidden)],
        [*grad_halves, down, up], [VMEM] * 4, 2 * rows * channels * hidden, 2 * channels * hidden,
        [pltpu.VMEM((rows, channels), BF16)],
    )[0]


def scales_in(own, got, hidden, width):
    tail = own[:, hidden:].astype(F32) + got[:, hidden:].astype(F32)
    return lax.rsqrt((tail[:, 0:1] + tail[:, 1:2]) / width + EPSILON)


def gate_of(hidden):
    return 1.0 / (1.0 + jnp.exp(-hidden))


def write_backward(width, own, got, act_own, act_got, low, high, gain, up, kept, sent, scaled, activated):
    channels, hidden = up.shape
    scales = scales_in(own, got, hidden, width)
    scale_grad = jnp.zeros_like(scales)
    step = tile_of(hidden)
    for n in range(0, hidden, step):
        cut = slice(n, n + step)
        product = own[:, cut].astype(F32) + got[:, cut].astype(F32)
        act_grad = act_own[:, cut].astype(F32) + act_got[:, cut].astype(F32)
        value = product * scales
        gate = gate_of(value)
        activated[:, cut] = (value * gate).astype(BF16)
        grad = act_grad * gate * (1.0 + value * (1.0 - gate))
        scaled[:, cut] = (grad * scales).astype(BF16)
        scale_grad += jnp.sum(grad * product, axis=1, keepdims=True)
    factor = scale_grad * scales * scales * scales / width
    half = low.shape[0]
    step = tile_of(channels)
    for c in range(0, channels, step):
        cut = slice(c, c + step)
        part = nt_dot(scaled[...], up[cut, :]) * gain[:, cut].astype(F32)
        kept[:, cut] = part[:half] - factor[:half] * low[:, cut].astype(F32)
        sent[:, cut] = (part[half:] - factor[half:] * high[:, cut].astype(F32)).astype(BF16)


def write_forward(width, own, got, down, kept, sent, activated):
    hidden, channels = down.shape
    scales = scales_in(own, got, hidden, width)
    step = tile_of(hidden)
    for n in range(0, hidden, step):
        cut = slice(n, n + step)
        value = (own[:, cut].astype(F32) + got[:, cut].astype(F32)) * scales
        activated[:, cut] = (value * gate_of(value)).astype(BF16)
    half = kept.shape[0]
    step = tile_of(channels)
    for c in range(0, channels, step):
        cut = slice(c, c + step)
        part = jnp.dot(activated[...], down[:, cut], preferred_element_type=F32)
        kept[:, cut] = part[:half]
        sent[:, cut] = part[half:].astype(BF16)


def backward_kernel(width, own, got, act_own, act_got, low, high, gain, up, _, *refs):
    write_backward(width, own, got, act_own, act_got, low, high, gain, up, *refs[-4:])


def backward(width, products_parts, act_parts, row_halves, gain, up, down, after):
    half, channels = row_halves[0].shape
    hidden = up.shape[1]
    outs = [struct(half, channels, dtype=F32), struct(half, channels), struct(2 * half, hidden), struct(2 * half, hidden)]
    operands = [*products_parts, *act_parts, *row_halves, gain, up, down]
    return call(
        functools.partial(backward_kernel, width), "backward", outs, operands + after,
        [VMEM] * len(operands) + [ANY] * len(after),
        4 * half * channels * hidden, 2 * channels * hidden,
    )


def forward_kernel(width, own, got, down, _, *refs):
    write_forward(width, own, got, down, *refs[-3:])


def forward(width, products_parts, up, down, after):
    rows = products_parts[0].shape[0]
    hidden, channels = down.shape
    outs = [struct(rows // 2, channels, dtype=F32), struct(rows // 2, channels)]
    return call(
        functools.partial(forward_kernel, width), "forward", outs, [*products_parts, down, up, *after],
        [VMEM] * 4 + [ANY] * len(after),
        2 * rows * channels * hidden, 2 * channels * hidden, [pltpu.VMEM((rows, hidden), BF16)],
    )


def enter_kernel(flag, low, high, other_low, other_high, gain, up, down, sent, grads, normed):
    @pl.when(flag[0] == 1)
    def _():
        write_products(joined(low, high), gain, up, sent, normed)
        grads[...] = joined(other_low, other_high)

    @pl.when(flag[0] == 0)
    def _():
        grads[...] = joined(low, high)
        write_act_grads(grads, down, sent)
        sent[:, up.shape[1] :] = jnp.zeros((sent.shape[0], BLK), BF16)


def enter(flag, row_halves, other_halves, gain, up, down):
    rows = 2 * row_halves[0].shape[0]
    channels, hidden = up.shape
    return call(
        enter_kernel, "enter", [struct(rows, hidden + BLK), struct(rows, channels)],
        [flag, *row_halves, *other_halves, gain, up, down], [SMEM] + [VMEM] * 7,
        2 * rows * channels * hidden, 2 * channels * hidden, [pltpu.VMEM((rows, channels), BF16)],
    )


def leave_kernel(width, flag, own, got, back_own, back_got, low, high, gain, up, down, *refs):
    kept, sent, scaled, activated, scratch = refs[-5:]

    @pl.when(flag[0] == 1)
    def _():
        write_forward(width, own, got, down, kept, sent, scratch)

    @pl.when(flag[0] == 0)
    def _():
        write_backward(width, back_own, back_got, own, got, low, high, gain, up, kept, sent, scaled, activated)


def leave(width, flag, parts, back_parts, row_halves, gain, up, down, filled, after):
    half, channels = row_halves[0].shape
    hidden = up.shape[1]
    outs = [struct(half, channels, dtype=F32), struct(half, channels), struct(2 * half, hidden), struct(2 * half, hidden)]
    operands = [flag, *parts, *back_parts, *row_halves, gain, up, down, *filled]
    first = len(operands) - len(filled)
    return pl.pallas_call(
        functools.partial(leave_kernel, width),
        out_shape=outs,
        in_specs=[SMEM] + [VMEM] * (len(operands) - 1) + [ANY] * len(after),
        out_specs=[VMEM] * 4,
        scratch_shapes=[pltpu.VMEM((2 * half, hidden), BF16)],
        input_output_aliases={first + i: 2 + i for i in range(len(filled))},
        compiler_params=pltpu.CompilerParams(vmem_limit_bytes=12 * MIB),
        cost_estimate=pl.CostEstimate(flops=4 * half * channels * hidden, bytes_accessed=2 * channels * hidden, transcendentals=0),
        name="leave",
    )(*operands, *after)


def block_kernel(channel_blocks, hidden_blocks, depth, capacity, table_counts, plan, gain, *refs):
    *tables, out = refs
    up_count = channel_blocks * hidden_blocks
    dp_index = plan[0, DP]
    z, core = dp_index // 2, lax.rem(dp_index, 2)

    def per_slot(slot, carry):
        owner = 2 * lax.rem(z - lax.rem(slot, depth) + depth, depth) + lax.rem(core + slot // depth, 2)
        number = jnp.int32(-1)
        for entry in range(capacity):
            here = jnp.logical_and(plan[dp_index, OWNERS + entry] == owner, entry < plan[dp_index, COUNT])
            number = jnp.where(here, plan[dp_index, OWNERS + capacity + entry], number)
        is_up = number < up_count
        down_number = jnp.maximum(number - up_count, 0)
        up_number = jnp.maximum(number, 0)
        left_index = jnp.where(is_up, up_number // hidden_blocks, down_number // channel_blocks)
        right_index = jnp.where(is_up, lax.rem(up_number, hidden_blocks), lax.rem(down_number, channel_blocks))
        left = pl.ds(pl.multiple_of(left_index * BLK, BLK), BLK)
        right = pl.ds(pl.multiple_of(right_index * BLK, BLK), BLK)

        def both(halves, cut):
            return jnp.concatenate([half[:, cut] for half in halves], axis=0)

        groups = []
        start = 0
        for count in table_counts:
            groups.append(tables[start : start + count])
            start += count

        def write(is_up_block):
            total = jnp.zeros((BLK, BLK), F32)
            for group in groups:
                rows, scaled, activated, grads = group[:2], group[2], group[3], group[4:]
                if is_up_block:
                    first = (both(rows, left).astype(F32) * gain[:, left].astype(F32)).astype(BF16)
                    second = scaled[:, right]
                else:
                    first = activated[:, left]
                    second = both(grads, right)
                total += lax.dot_general(first, second, (((0,), (0,)), ((), ())), preferred_element_type=F32)
            out[slot] = total.astype(BF16)

        @pl.when(jnp.logical_and(number >= 0, is_up))
        def _():
            write(True)

        @pl.when(jnp.logical_not(is_up))
        def _():
            write(False)

        @pl.when(number < 0)
        def _():
            out[slot] = jnp.zeros((BLK, BLK), BF16)

        return carry

    lax.fori_loop(0, out.shape[0], per_slot, 0)


def outgoing_blocks(plan, capacity, gain, tables, channel_blocks, hidden_blocks):
    slots = lax.axis_size("dp")
    flat = [table for turn in tables for table in turn]
    kernel = functools.partial(
        block_kernel, channel_blocks, hidden_blocks, slots // 2, capacity, [len(turn) for turn in tables]
    )
    return call(
        kernel, "block_grads", [struct(slots, BLK, BLK)], [plan, gain, *flat],
        [SMEM, VMEM] + [VMEM] * len(flat), 4 * slots * BLK * BLK * BLK, 2 * slots * BLK * BLK,
    )[0]


def adam_kernel(depth, plan, relayed, *refs):
    *others, first, second, first_out, second_out, direction_out = refs
    dp_index = plan[0, DP]
    z, core = dp_index // 2, lax.rem(dp_index, 2)
    slots, capacity = plan.shape[0], first.shape[0]
    first_out[...] = jnp.zeros(first_out.shape, F32)
    second_out[...] = jnp.zeros(first_out.shape, F32)
    direction_out[...] = jnp.zeros(first_out.shape, F32)

    def update(place, grad):
        grad = grad.astype(F32)
        first_new = 0.9 * first[place] + 0.1 * grad
        second_new = 0.999 * second[place] + 0.001 * grad * grad
        first_out[place] = first_new
        second_out[place] = second_new
        direction_out[place] = first_new / (jnp.sqrt(second_new) + 1e-08)

    def per_source(source, place):
        sends = False
        for entry in range(capacity):
            sends = jnp.logical_or(sends, jnp.logical_and(plan[source, OWNERS + entry] == dp_index, entry < plan[source, COUNT]))
        back = lax.rem(source // 2 - z + depth, depth)
        across = lax.rem(source + core, 2)
        for k in range(depth):
            @pl.when(jnp.logical_and(sends, back == k))
            def _():
                if k == 0:
                    update(place, relayed[0])
                else:
                    update(place, others[k - 1][across])

        return place + jnp.where(sends, 1, 0)

    lax.fori_loop(0, slots, per_source, 0)


def adam(plan, relayed, others, first, second):
    shape = jax.ShapeDtypeStruct(first.shape, F32)
    operands = [plan, relayed, *others, first, second]
    return call(
        functools.partial(adam_kernel, lax.axis_size("dp") // 2), "adam_step", [shape] * 3, operands,
        [SMEM] + [VMEM] * (len(operands) - 1), 20 * first.size, 20 * first.size,
    )


def finish_kernel(earlier_count, *refs):
    earlier, rows, parts, out = refs[:earlier_count], refs[earlier_count], refs[earlier_count + 1 : -1], refs[-1]
    for turn in range(earlier_count):
        out[turn] = earlier[turn][...]
    total = rows[...].astype(F32)
    for part in parts:
        total += part[...].astype(F32)
    out[earlier_count] = total.astype(BF16)


def finish(earlier, rows, parts):
    operands = [*earlier, rows, *parts]
    return call(
        functools.partial(finish_kernel, len(earlier)), "finish", [struct(len(earlier) + 1, *rows.shape)], operands,
        [VMEM] * len(operands), rows.size, 8 * rows.size,
    )[0]


def finish_pair_kernel(depth, flag, chained, off_back, forward_rows, chain_rows, *refs):
    forward_parts, chain_parts, (section_out, grads_out) = refs[:depth], refs[depth : 2 * depth], refs[2 * depth :]

    def total(rows, parts):
        value = rows[...].astype(F32)
        for part in parts:
            value += part[...].astype(F32)
        return value.astype(BF16)

    off_forward = total(forward_rows, forward_parts)
    chained_later = total(chain_rows, chain_parts)

    @pl.when(flag[0] == 1)
    def _():
        section_out[0] = chained[...]
        section_out[1] = off_forward
        grads_out[0] = off_back[...]
        grads_out[1] = chained_later

    @pl.when(flag[0] == 0)
    def _():
        section_out[0] = off_forward
        section_out[1] = chained_later
        grads_out[0] = chained[...]
        grads_out[1] = off_back[...]


def finish_pair(flag, chained, off_back, forward_rows, forward_parts, chain_rows, chain_parts):
    operands = [flag, chained, off_back, forward_rows, chain_rows, *forward_parts, *chain_parts]
    return call(
        functools.partial(finish_pair_kernel, len(chain_parts)), "finish_pair", [struct(2, *chained.shape)] * 2, operands,
        [SMEM] + [VMEM] * (len(operands) - 1), 8 * chained.size, 16 * chained.size,
    )


def relay_pair(
    is_first, masked, entering, begin, start, stash, gain, up, down, width
):
    def pick(first, last):
        return jnp.where(is_first, first, last)

    flag = pick(jnp.int32(1), jnp.int32(0)).reshape(1)
    other_flag = 1 - flag
    chain_in = pick(begin, start)
    first = jnp.stack([pick(stash[1], stash[0]), chain_in])
    off_grads, off_rows = pick(start, masked[0]), pick(entering[0], begin)
    others = jnp.stack([pick(stash[0], stash[1]), off_grads, off_rows])
    up, down, flag, other_flag, others = lax.optimization_barrier((up, down, flag, other_flag, others))

    with jax.named_scope("gather_first"):
        moved = moved_rows(first)
    up, down = load_weights(up, down, first)
    with jax.named_scope("gather_first"):
        gathered = halves(later(moved, up))
    back_halves, chain_halves = [[half[i] for half in gathered] for i in range(2)]
    back_product = products(back_halves, gain, up, down)
    with jax.named_scope("swap_back"):
        back_parts = tensor_parts(back_product)
    entered, _ = enter(flag, later(chain_halves, back_product), chain_halves, gain, up, down)
    with jax.named_scope("swap_chain0"):
        parts = tensor_parts(entered)
    with jax.named_scope("gather_others"):
        gathered = halves(later(moved_rows(later(others, entered)), back_parts[1]))
    off_halves, off_grad_halves, off_row_halves = [[half[i] for half in gathered] for i in range(3)]
    off_product = products(off_halves, gain, up, down)
    with jax.named_scope("swap_off_back"):
        off_parts = tensor_parts(off_product)
    off_act = act_grads(later(off_grad_halves, off_product), up, down)
    with jax.named_scope("swap_off_act"):
        off_act_parts = tensor_parts(off_act)
    off_forward = products(later(off_row_halves, off_act), gain, up, down)

    with jax.named_scope("chain0"):
        kept, sent, scaled, activated = leave(
            width, flag, parts, back_parts, back_halves, gain, up, down, [], [off_product, off_act, off_forward]
        )
        sums = scatter_parts(scatter_pairs(kept, sent))
        chained = added(chain_in, later(sums, off_parts[1]))
    with jax.named_scope("pass"):
        passed = halves([one[0] for one in moved_passed(chained)])
    chain_in = passed[0][: chained.shape[0]]
    entered, grads = enter(other_flag, later(passed, off_act_parts[1]), chain_halves, gain, up, down)
    with jax.named_scope("swap_chain1"):
        parts = tensor_parts(entered)
    with jax.named_scope("off_back"):
        kept, sent, off_scaled, off_activated = backward(
            width, off_parts, off_act_parts, off_halves, gain, up, down, [entered]
        )
        off_back_sums = scatter_parts(scatter_pairs(kept, sent))
    with jax.named_scope("swap_off_forward"):
        off_forward_parts = tensor_parts(later(off_forward, entered))
    with jax.named_scope("chain1"):
        kept, sent, scaled, activated = leave(
            width, other_flag, parts, back_parts, back_halves, gain, up, down, [scaled, activated], []
        )
        chain_sums = scatter_parts(scatter_pairs(kept, sent))
        off_back = added(off_grads, later(off_back_sums, kept))
    with jax.named_scope("off_forward"):
        kept, sent = forward(width, later(off_forward_parts, chain_sums), up, down, [])
        off_sums = scatter_parts(scatter_pairs(kept, sent))
    section_outputs, input_grads = finish_pair(flag, chained, off_back, off_rows, off_sums, chain_in, chain_sums)
    tables = [
        (*back_halves, scaled, activated, grads),
        (*off_halves, off_scaled, off_activated, *off_grad_halves),
    ]
    return section_outputs, input_grads, tables, off_back


def relay(
    is_first, is_last, masked, entering, section_inputs, grad_outputs, stashed_inputs, gain, up, down, width
):
    turn_count = stashed_inputs.shape[1]
    local_rows = section_inputs.shape[1]
    up, down, is_first, is_last, masked = lax.optimization_barrier((up, down, is_first, is_last, masked))
    grads_in, rows_in = grad_outputs[0], section_inputs[0]
    first = jnp.concatenate([stashed_inputs[0, :1], grad_outputs])
    with jax.named_scope("gather_first"):
        moved = moved_rows(first)
    up, down = load_weights(up, down, first)
    with jax.named_scope("gather_first"):
        gathered = halves(later(moved, up))
    stash_rows = [[half[0] for half in gathered]]
    grad_halves = [half[1] for half in gathered]
    back_products = [products(stash_rows[0], gain, up, down)]
    with jax.named_scope("swap_b0p"):
        back_parts = [tensor_parts(back_products[0])]
    act_grad = act_grads(later(grad_halves, back_products[0]), up, down)
    with jax.named_scope("swap_b0a"):
        act_parts = tensor_parts(act_grad)
    with jax.named_scope("gather_others"):
        others = jnp.concatenate([section_inputs, stashed_inputs[0, 1:]])
        gathered = halves(moved_rows(later(others, act_grad)))
    product = products([half[0] for half in gathered], gain, up, down)
    with jax.named_scope("swap_f0p"):
        parts = tensor_parts(product)
    ahead = [product]
    for turn in range(1, turn_count):
        stash_rows.append([half[turn] for half in gathered])
        back_products.append(products(stash_rows[turn], gain, up, down))
        ahead.append(back_products[turn])
        with jax.named_scope("swap_b1p"):
            back_parts.append(tensor_parts(back_products[turn]))

    forward_results = []
    backward_results = []
    tables = []
    for turn in range(turn_count):
        with jax.named_scope(f"backward{turn}"):
            kept, sent, scaled, activated = backward(
                width, back_parts[turn], act_parts, stash_rows[turn], gain, up, down, ahead
            )
            back_pairs = scatter_pairs(kept, sent)
        tables.append((*stash_rows[turn], scaled, activated, *grad_halves))
        if turn + 1 == turn_count:
            with jax.named_scope(f"backward{turn}"):
                back_sums = scatter_parts(back_pairs)
            parts = later(parts, back_sums)
        with jax.named_scope(f"forward{turn}"):
            kept, sent = forward(width, parts, up, down, [])
            pairs = scatter_pairs(kept, sent)
        if turn + 1 == turn_count:
            with jax.named_scope(f"forward{turn}"):
                sums = scatter_parts(pairs)
            input_grads = finish(backward_results, grads_in, back_sums)
            section_outputs = finish(forward_results, rows_in, sums)
            break
        with jax.named_scope(f"scatter{turn}"):
            sums = scatter_parts(jnp.stack([back_pairs, pairs], axis=1))
        backward_results.append(added(grads_in, [part[0] for part in sums]))
        forward_results.append(added(rows_in, [part[1] for part in sums]))
        with jax.named_scope(f"gather{turn}"):
            moved = moved_passed(
                jnp.where(is_first, masked[turn], backward_results[-1]),
                jnp.where(is_last, entering[turn], forward_results[-1]),
            )
            passed = halves(later(moved, back_parts[turn + 1][1]))
        grad_halves = [half[0] for half in passed]
        grads_in, rows_in = passed[0][0, :local_rows], passed[0][1, :local_rows]
        act_grad = act_grads(grad_halves, up, down)
        with jax.named_scope("swap_b1a"):
            act_parts = tensor_parts(act_grad)
        product = products(later([half[1] for half in passed], act_grad), gain, up, down)
        with jax.named_scope("swap_f1p"):
            parts = tensor_parts(product)
        ahead = []
    return section_outputs, input_grads, tables


def body(
    section_inputs,
    entering,
    grad_outputs,
    arriving,
    live_rows,
    stashed_inputs,
    norm_gain,
    up_weight,
    down_weight,
    held_blocks,
    held_count,
    held_owner,
    first_moment,
    second_moment,
):
    section_count = lax.axis_size("section")
    section_index = lax.axis_index("section")
    dp_count = lax.axis_size("dp")
    turn_count = stashed_inputs.shape[1]
    local_rows = section_inputs.shape[1]
    channels, hidden = up_weight.shape[1:]
    width = channels * lax.axis_size("tensor")
    is_first = section_index == 0
    is_last = section_index == section_count - 1
    counts, owners = held_count[0, 0], held_owner[0, 0]
    capacity = owners.shape[1]
    dp_index = lax.axis_index("dp")
    plan = jnp.concatenate(
        [jnp.full((dp_count, 1), dp_index, jnp.int32), counts[:, None], owners, held_blocks[0, 0]], axis=1
    )
    row_ids = dp_index * local_rows + lax.iota(jnp.int32, local_rows)
    masked = jnp.where((row_ids < live_rows[:, None])[..., None], arriving, jnp.zeros((), BF16))

    if section_count == 2 and turn_count == 2:
        weights = lax.optimization_barrier((up_weight[0], down_weight[0], plan))
        section_outputs, input_grads, tables, before = relay_pair(
            is_first, masked, entering, section_inputs[0], grad_outputs[0], stashed_inputs[0], norm_gain, *weights[:2], width
        )
        plan = later(weights[2], before)
    else:
        section_outputs, input_grads, tables = relay(
            is_first, is_last, masked, entering, section_inputs, grad_outputs, stashed_inputs, norm_gain,
            up_weight[0], down_weight[0], width,
        )
    with jax.named_scope("block_exchange"):
        outgoing = outgoing_blocks(plan, capacity, norm_gain, tables, channels // BLK, hidden // BLK)
        outgoing = outgoing.reshape((2, dp_count // 2, BLK, BLK))
        relayed = sibling(outgoing[1])
        others = [shifted(jnp.stack([outgoing[0, k], relayed[k]]), -k) for k in range(1, dp_count // 2)]
    first_out, second_out, direction_out = adam(plan, relayed, others, first_moment[0, 0, 0], second_moment[0, 0, 0])
    return (
        section_outputs[None],
        input_grads[None],
        first_out[None, None, None],
        second_out[None, None, None],
        direction_out[None, None, None],
    )


def solution(mesh):
    return jax.shard_map(
        body,
        mesh=mesh,
        in_specs=(
            P("section", "dp", "tensor"),
            P(None, "dp", "tensor"),
            P("section", "dp", "tensor"),
            P(None, "dp", "tensor"),
            P(),
            P("section", None, "dp", "tensor"),
            P("section", "tensor"),
            P("section", "tensor", "dp"),
            P("section", "dp", "tensor"),
            P("section", "tensor", None, None),
            P("section", "tensor", None),
            P("section", "tensor", None, None),
            P("section", "tensor", "dp", None, None, None),
            P("section", "tensor", "dp", None, None, None),
        ),
        out_specs=(
            P("section", None, "dp", "tensor"),
            P("section", None, "dp", "tensor"),
            P("section", "tensor", "dp", None, None, None),
            P("section", "tensor", "dp", None, None, None),
            P("section", "tensor", "dp", None, None, None),
        ),
        check_vma=False,
    )
```

time: 374 us -> 124 us (0.33)
  blocking collectives: 131 us -> 0 us
  waiting for transfers between devices: 138 us -> 47.1 us
  matrix products: 43.6 us -> 0 us
  starting transfers between devices: 9.81 us -> 47.6 us
  Pallas kernels: 0 us -> 22.5 us
  other arithmetic: 22.3 us -> 2.1 us
  between operations: 15.9 us -> 1.72 us
  local copies, waits for them, and re-layouts: 11.3 us -> 2.54 us
    all_gather x6 -> x0, blocking collectives: 88.7 us -> none  [the longest x2 31.1 us: body(): forward_rows_all = lax.all_gather(rows_in, 'dp', axis=0, tiled=True)]
    psum x4 -> x0, waiting for transfers between devices: 81.5 us -> none  [the longest x2 81.5 us: body(): lax.psum((product, squares, act_grad), 'tensor')]
    reduce_scatter x4 -> x0, waiting for transfers between devices: 55.5 us -> none  [the longest x2 40.9 us: body(): lax.psum_scatter(jnp.dot(forward_activated, down_matrix, preferred_elemen...]
    ppermute x2 -> x39, waiting for transfers between devices: 1.37 us -> 47.1 us  [the longest x6 18.9 us: tensor_parts(): got = lax.ppermute(value, 'tensor', [(t, t ^ step) for t in range(count)])]
    dot_general x12 -> x0, matrix products: 43.6 us -> none  [the longest x4 17.1 us: times_transposed(): lax.dot_general(left, right, (((1,), (1,)), ((), ())), preferred_element_...]
    ppermute x2 -> x39, starting transfers between devices: 4.67 us -> 47.6 us  [the longest x21 32.5 us: shifted(): lax.ppermute(value, 'dp', [(d, (d + 2 * steps) % count) for d in range(co...]
    unnamed x2 -> x0, blocking collectives: 27.6 us -> none
    pallas_call x0 -> x14, Pallas kernels: none -> 22.5 us  [the longest x11 15.5 us: call(): pl.pallas_call(kernel, out_shape=outs, in_specs=specs, out_specs=[VMEM] *...]
  transfers between devices with their start and end apart: 11 -> 39, of which waited for: 7 -> 20; matrix products, arithmetic and copies ran while one was open for 19% -> 2% of each run, Pallas kernels for 0% -> 13%
where the time goes in v2:
time: 124 us
  starting transfers between devices  47.6 us (38%)
  waiting for transfers between devices  47.1 us (38%)
  Pallas kernels  22.5 us (18%)
  local copies, waits for them, and re-layouts  2.54 us (2%)
  other arithmetic  2.1 us (2%)
  between operations  1.72 us (1%)
    ppermute x21, starting transfers between devices, shifted(): lax.ppermute(value, 'dp', [(d, (d + 2 * steps) % count) for d in range(co...  32.5 us
    ppermute x6, waiting for transfers between devices, tensor_parts(): got = lax.ppermute(value, 'tensor', [(t, t ^ step) for t in range(count)])  18.9 us
    ppermute x21, waiting for transfers between devices, shifted(): lax.ppermute(value, 'dp', [(d, (d + 2 * steps) % count) for d in range(co...  18.8 us
    pallas_call x11, Pallas kernels, call(): pl.pallas_call(kernel, out_shape=outs, in_specs=specs, out_specs=[VMEM] *...  15.5 us
    ppermute x4, starting transfers between devices, moved(): return lax.ppermute(local, ('section', 'dp'), pairs)  8.36 us
    ppermute x8, waiting for transfers between devices, sibling(): lax.ppermute(value, 'dp', [(d, d ^ 1) for d in range(lax.axis_size('dp'))])  5.95 us
    ppermute x6, starting transfers between devices, tensor_parts(): got = lax.ppermute(value, 'tensor', [(t, t ^ step) for t in range(count)])  5.51 us
    pallas_call x1, Pallas kernels, load_weights(): pl.pallas_call(load_kernel, out_shape=[pltpu.VMEM(up.shape, BF16), pltpu....  3.73 us
  transfers between devices with their start and end apart: 39, of which 20 were waited for; matrix products, arithmetic and copies ran while one was open for 2% of the time, Pallas kernels for 13%

profile of v2, /device:TPU:0, one launch (start us, length us, event | category | flops | bytes accessed | tf_op | source)
XLA Modules:
  0.0 123.6 jit_solution(14438258634473407089)
XLA Ops:
  1.3 0.8 select_bitcast_fusion
  2.1 0.9 broadcast_select_fusion
  3.1 3.1 %collective-permute-start = (bf16[2,16,1280]{2,1,0:T(8,128)(2,1)S(1)}, bf16[2,16,1280]{2,1,0:T(8,128)(2,1)S(1)}, u32[]{:S(2)}, u32[]{:S(2)}) collective-permute-start(bf16[2,16,1280]{2,1,0:T(8,128)(2,1)S(1)} %pad_maximum_fusion.2.after), channel_id=1, source_target_pairs={{0,4},{2,6},{4,8},{6,10},{8,12},{10,14},{12,0},{14,2},{1,5},{3,7},... | collective-permute-start | bytes 245768 | tf_op jit(solution)/shard_map/gather_first/ppermute | solution.py:32
  6.1 2.6 %collective-permute-start.1 = (bf16[2,16,1280]{2,1,0:T(8,128)(2,1)S(1)}, bf16[2,16,1280]{2,1,0:T(8,128)(2,1)S(1)}, u32[]{:S(2)}, u32[]{:S(2)}) collective-permute-start(bf16[2,16,1280]{2,1,0:T(8,128)(2,1)S(1)} %pad_maximum_fusion.2.after), channel_id=1, source_target_pairs={{0,8},{2,10},{4,12},{6,14},{8,0},{10,2},{12,4},{14,6},{1,9},{3,11}... | collective-permute-start | bytes 245768 | tf_op jit(solution)/shard_map/gather_first/ppermute | solution.py:32
  8.7 1.3 %collective-permute-start.2 = (bf16[2,16,1280]{2,1,0:T(8,128)(2,1)S(1)}, bf16[2,16,1280]{2,1,0:T(8,128)(2,1)S(1)}, u32[]{:S(2)}, u32[]{:S(2)}) collective-permute-start(bf16[2,16,1280]{2,1,0:T(8,128)(2,1)S(1)} %pad_maximum_fusion.2.after), channel_id=1, source_target_pairs={{0,12},{2,14},{4,0},{6,2},{8,4},{10,6},{12,8},{14,10},{1,13},{3,15... | collective-permute-start | bytes 245768 | tf_op jit(solution)/shard_map/gather_first/ppermute | solution.py:32
  12.4 3.7 %load_weights.1 = (bf16[1280,1792]{1,0:T(8,128)(2,1)S(1)}, bf16[1792,1280]{1,0:T(8,128)(2,1)S(1)}) custom-call(bf16[1280,1792]{1,0:T(8,128)(2,1)} %bitcast.69, bf16[1792,1280]{1,0:T(8,128)(2,1)} %bitcast.70, bf16[2,16,1280]{2,1,0:T(8,128)(2,1)S(1)} %pad_maximum_fusion.2.after), custom_call_target="tpu_custom_call" | custom-call | tf_op jit(solution)/shard_map/load_weights/pallas_call | solution.py:121
  16.4 1.6 %collective-permute-done.3 = bf16[2,64,1280]{2,1,0:T(8,128)(2,1)S(1)} collective-permute-done((bf16[2,64,1280]{2,1,0:T(8,128)(2,1)S(1)}, bf16[2,64,1280]{2,1,0:T(8,128)(2,1)S(1)}, u32[]{:S(2)}, u32[]{:S(2)}) %collective-permute-start.3) | collective-permute-done | bytes 327712 | tf_op jit(solution)/shard_map/gather_first/ppermute | solution.py:27
  18.0 0.8 products.3.back_own
  18.8 1.6 %collective-permute-start.5 = (bf16[128,1920]{1,0:T(8,128)(2,1)S(1)}, bf16[128,1920]{1,0:T(8,128)(2,1)S(1)}, u32[]{:S(2)}, u32[]{:S(2)}) collective-permute-start(bf16[128,1920]{1,0:T(8,128)(2,1)S(1)} %products.3.back_own), channel_id=1, source_target_pairs={{0,1},{1,0},{2,3},{3,2},{4,5},{5,4},{6,7},{7,6},{8,9},{9,8},{10,11... | collective-permute-start | bytes 1474568 | tf_op jit(solution)/shard_map/swap_back/ppermute | solution.py:80
  20.3 1.5 %enter.2 = (bf16[128,1920]{1,0:T(8,128)(2,1)S(1)}, bf16[128,1280]{1,0:T(8,128)(2,1)}) custom-call(s32[1]{0:T(128)} %bitcast.5.flag, bf16[64,1280]{1,0:T(8,128)(2,1)S(1)} %get-tuple-element.77.low.other_low, bf16[64,1280]{1,0:T(8,128)(2,1)S(1)} %get-tuple-element.78.high.other_high, bf16[64,1280]{1,0:T(8,128)(2,1)S(1)} %get-tuple-element.77.low.other_low, ...), custom_call_target="tpu_custom_call" | custom-call | flops 587202560 | bytes 4587520 | tf_op jit(solution)/shard_map/enter/pallas_call | solution.py:92
  22.5 1.4 %collective-permute-start.7 = (bf16[3,16,1280]{2,1,0:T(8,128)(2,1)S(1)}, bf16[3,16,1280]{2,1,0:T(8,128)(2,1)S(1)}, u32[]{:S(2)}, u32[]{:S(2)}) collective-permute-start(bf16[3,16,1280]{2,1,0:T(8,128)(2,1)S(1)} %pad_maximum_fusion.1), channel_id=1, source_target_pairs={{0,8},{2,10},{4,12},{6,14},{8,0},{10,2},{12,4},{14,6},{1,9},{3,11}... | collective-permute-start | bytes 368648 | tf_op jit(solution)/shard_map/gather_others/ppermute | solution.py:32
  23.9 1.7 %collective-permute-start.8 = (bf16[3,16,1280]{2,1,0:T(8,128)(2,1)S(1)}, bf16[3,16,1280]{2,1,0:T(8,128)(2,1)S(1)}, u32[]{:S(2)}, u32[]{:S(2)}) collective-permute-start(bf16[3,16,1280]{2,1,0:T(8,128)(2,1)S(1)} %pad_maximum_fusion.1), channel_id=1, source_target_pairs={{0,12},{2,14},{4,0},{6,2},{8,4},{10,6},{12,8},{14,10},{1,13},{3,15... | collective-permute-start | bytes 368648 | tf_op jit(solution)/shard_map/gather_others/ppermute | solution.py:32
  25.7 4.2 %collective-permute-done.6 = bf16[3,16,1280]{2,1,0:T(8,128)(2,1)S(1)} collective-permute-done((bf16[3,16,1280]{2,1,0:T(8,128)(2,1)S(1)}, bf16[3,16,1280]{2,1,0:T(8,128)(2,1)S(1)}, u32[]{:S(2)}, u32[]{:S(2)}) %collective-permute-start.6) | collective-permute-done | bytes 122912 | tf_op jit(solution)/shard_map/gather_others/ppermute | solution.py:32
  29.9 4.2 %collective-permute-done.7 = bf16[3,16,1280]{2,1,0:T(8,128)(2,1)S(1)} collective-permute-done((bf16[3,16,1280]{2,1,0:T(8,128)(2,1)S(1)}, bf16[3,16,1280]{2,1,0:T(8,128)(2,1)S(1)}, u32[]{:S(2)}, u32[]{:S(2)}) %collective-permute-start.7) | collective-permute-done | bytes 122912 | tf_op jit(solution)/shard_map/gather_others/ppermute | solution.py:32
  34.9 1.2 collective-permute-done.9
  36.2 0.8 products.4.refs_0_.own
  37.0 1.6 %act_grads.1.refs_1_.act_own = bf16[128,1792]{1,0:T(8,128)(2,1)S(1)} custom-call(bf16[64,1280]{1,0:T(8,128)(2,1)S(1)} %get-tuple-element.86.low.refs_9_, bf16[64,1280]{1,0:T(8,128)(2,1)S(1)} %get-tuple-element.87.high.refs_10_, bf16[1792,1280]{1,0:T(8,128)(2,1)S(1)} %get-tuple-element.76._.down, bf16[1280,1792]{1,0:T(8,128)(2,1)S(1)} %get-tuple-element.71.up._), custom_call_target="tpu_custom_call" | custom-call | flops 587202560 | bytes 4587520 | tf_op jit(solution)/shard_map/act_grads/pallas_call | solution.py:92
  38.5 0.8 products.5.refs_2_.own
  39.3 8.6 %collective-permute-done.4.got = bf16[128,1920]{1,0:T(8,128)(2,1)S(1)} collective-permute-done((bf16[128,1920]{1,0:T(8,128)(2,1)S(1)}, bf16[128,1920]{1,0:T(8,128)(2,1)S(1)}, u32[]{:S(2)}, u32[]{:S(2)}) %collective-permute-start.4) | collective-permute-done | bytes 491552 | tf_op jit(solution)/shard_map/swap_chain0/ppermute | solution.py:80
  47.9 1.1 leave.2
  49.7 0.8 collective-permute-done.10
  50.5 2.3 %collective-permute-start.11 = (bf16[16,1280]{1,0:T(8,128)(2,1)S(1)}, bf16[16,1280]{1,0:T(8,128)(2,1)S(1)}, u32[]{:S(2)}, u32[]{:S(2)}) collective-permute-start(bf16[16,1280]{1,0:T(8,128)(2,1)S(1)} %get-tuple-element.159), channel_id=1, source_target_pairs={{0,12},{2,14},{4,0},{6,2},{8,4},{10,6},{12,8},{14,10},{1,13},{3,15... | collective-permute-start | bytes 122888 | tf_op jit(solution)/shard_map/chain0/ppermute | solution.py:32
  52.8 1.7 %collective-permute-start.12 = (bf16[16,1280]{1,0:T(8,128)(2,1)S(1)}, bf16[16,1280]{1,0:T(8,128)(2,1)S(1)}, u32[]{:S(2)}, u32[]{:S(2)}) collective-permute-start(bf16[16,1280]{1,0:T(8,128)(2,1)S(1)} %get-tuple-element.158), channel_id=1, source_target_pairs={{0,8},{2,10},{4,12},{6,14},{8,0},{10,2},{12,4},{14,6},{1,9},{3,11}... | collective-permute-start | bytes 122888 | tf_op jit(solution)/shard_map/chain0/ppermute | solution.py:32
  55.3 3.0 %collective-permute-done.12 = bf16[16,1280]{1,0:T(8,128)(2,1)S(1)} collective-permute-done((bf16[16,1280]{1,0:T(8,128)(2,1)S(1)}, bf16[16,1280]{1,0:T(8,128)(2,1)S(1)}, u32[]{:S(2)}, u32[]{:S(2)}) %collective-permute-start.12) | collective-permute-done | bytes 40992 | tf_op jit(solution)/shard_map/chain0/ppermute | solution.py:32
  58.3 2.1 %collective-permute-done.13 = bf16[16,1280]{1,0:T(8,128)(2,1)S(1)} collective-permute-done((bf16[16,1280]{1,0:T(8,128)(2,1)S(1)}, bf16[16,1280]{1,0:T(8,128)(2,1)S(1)}, u32[]{:S(2)}, u32[]{:S(2)}) %collective-permute-start.13) | collective-permute-done | bytes 40992 | tf_op jit(solution)/shard_map/chain0/ppermute | solution.py:32
  60.4 2.8 %collective-permute-done.14.got = bf16[128,1920]{1,0:T(8,128)(2,1)S(1)} collective-permute-done((bf16[128,1920]{1,0:T(8,128)(2,1)S(1)}, bf16[128,1920]{1,0:T(8,128)(2,1)S(1)}, u32[]{:S(2)}, u32[]{:S(2)}) %collective-permute-start.14) | collective-permute-done | bytes 491552 | tf_op jit(solution)/shard_map/swap_off_back/ppermute | solution.py:80
  63.2 5.2 %collective-permute-start.19 = (bf16[1,16,1280]{2,1,0:T(8,128)(2,1)S(1)}, bf16[1,16,1280]{2,1,0:T(8,128)(2,1)S(1)}, u32[]{:S(2)}, u32[]{:S(2)}) collective-permute-start(bf16[1,16,1280]{2,1,0:T(8,128)(2,1)S(1)} %bitcast.63), channel_id=1, source_target_pairs={{0,28},{2,30},{4,16},{6,18},{8,20},{10,22},{12,24},{14,26},{16,12}... | collective-permute-start | bytes 122888 | tf_op jit(solution)/shard_map/pass/ppermute | solution.py:50
  68.3 2.2 %collective-permute-start.17 = (bf16[1,16,1280]{2,1,0:T(8,128)(2,1)S(1)}, bf16[1,16,1280]{2,1,0:T(8,128)(2,1)S(1)}, u32[]{:S(2)}, u32[]{:S(2)}) collective-permute-start(bf16[1,16,1280]{2,1,0:T(8,128)(2,1)S(1)} %bitcast.65), channel_id=1, source_target_pairs={{0,20},{2,22},{4,24},{6,26},{8,28},{10,30},{12,16},{14,18},{16,4},... | collective-permute-start | bytes 122888 | tf_op jit(solution)/shard_map/pass/ppermute | solution.py:50
  70.5 1.0 collective-permute-start.16
  71.5 2.6 %collective-permute-done.18 = bf16[1,16,1280]{2,1,0:T(8,128)(2,1)S(1)} collective-permute-done((bf16[1,16,1280]{2,1,0:T(8,128)(2,1)S(1)}, bf16[1,16,1280]{2,1,0:T(8,128)(2,1)S(1)}, u32[]{:S(2)}, u32[]{:S(2)}) %collective-permute-start.18) | collective-permute-done | bytes 40992 | tf_op jit(solution)/shard_map/pass/ppermute | solution.py:50
  74.1 0.9 collective-permute-done.17
  75.1 1.4 %collective-permute-done.20.high = bf16[64,1280]{1,0:T(8,128)(2,1)S(1)} collective-permute-done((bf16[64,1280]{1,0:T(8,128)(2,1)S(1)}, bf16[64,1280]{1,0:T(8,128)(2,1)S(1)}, u32[]{:S(2)}, u32[]{:S(2)}) %collective-permute-start.20) | collective-permute-done | bytes 163872 | tf_op jit(solution)/shard_map/pass/ppermute | solution.py:27
  76.5 1.8 %enter.3 = (bf16[128,1920]{1,0:T(8,128)(2,1)S(1)}, bf16[128,1280]{1,0:T(8,128)(2,1)S(1)}) custom-call(s32[1]{0:T(128)S(6)} %sub.3.flag, bf16[64,1280]{1,0:T(8,128)(2,1)S(1)} %pad_maximum_fusion.low, bf16[64,1280]{1,0:T(8,128)(2,1)S(1)} %collective-permute-done.20.high, bf16[64,1280]{1,0:T(8,128)(2,1)S(1)} %get-tuple-element.77.low.other_low, ...), custom_call_target="tpu_custom_call" | custom-call | flops 587202560 | bytes 4587520 | tf_op jit(solution)/shard_map/enter/pallas_call | solution.py:92
  78.3 2.2 %backward.1 = (f32[64,1280]{1,0:T(8,128)S(1)}, bf16[64,1280]{1,0:T(8,128)(2,1)S(1)}, bf16[128,1792]{1,0:T(8,128)(2,1)S(1)}, bf16[128,1792]{1,0:T(8,128)(2,1)S(1)}) custom-call(bf16[128,1920]{1,0:T(8,128)(2,1)S(1)} %products.4.refs_0_.own, bf16[128,1920]{1,0:T(8,128)(2,1)S(1)} %collective-permute-done.14.got, bf16[128,1792]{1,0:T(8,128)(2,1)S(1)} %act_grads.1.refs_1_.act_own, ...), custom_call_target="tpu_custom_call" | custom-call | flops 587202560 | bytes 4587520 | tf_op jit(solution)/shard_map/off_back/backward/pallas_call | solution.py:92
  81.2 1.5 %collective-permute-start.26 = (bf16[128,1920]{1,0:T(8,128)(2,1)S(1)}, bf16[128,1920]{1,0:T(8,128)(2,1)S(1)}, u32[]{:S(2)}, u32[]{:S(2)}) collective-permute-start(bf16[128,1920]{1,0:T(8,128)(2,1)S(1)} %products.5.refs_2_.own), channel_id=1, source_target_pairs={{0,1},{1,0},{2,3},{3,2},{4,5},{5,4},{6,7},{7,6},{8,9},{9,8},{10,11... | collective-permute-start | bytes 1474568 | tf_op jit(solution)/shard_map/swap_off_forward/ppermute | solution.py:80
  82.8 3.8 %collective-permute-start.22 = (bf16[16,1280]{1,0:T(8,128)(2,1)S(1)}, bf16[16,1280]{1,0:T(8,128)(2,1)S(1)}, u32[]{:S(2)}, u32[]{:S(2)}) collective-permute-start(bf16[16,1280]{1,0:T(8,128)(2,1)S(1)} %get-tuple-element.156), channel_id=1, source_target_pairs={{0,12},{2,14},{4,0},{6,2},{8,4},{10,6},{12,8},{14,10},{1,13},{3,15... | collective-permute-start | bytes 122888 | tf_op jit(solution)/shard_map/off_back/ppermute | solution.py:32
  87.2 7.5 %collective-permute-done.25.got = bf16[128,1920]{1,0:T(8,128)(2,1)S(1)} collective-permute-done((bf16[128,1920]{1,0:T(8,128)(2,1)S(1)}, bf16[128,1920]{1,0:T(8,128)(2,1)S(1)}, u32[]{:S(2)}, u32[]{:S(2)}) %collective-permute-start.25) | collective-permute-done | bytes 491552 | tf_op jit(solution)/shard_map/swap_chain1/ppermute | solution.py:80
  94.7 2.2 %leave.3 = (f32[64,1280]{1,0:T(8,128)S(1)}, bf16[64,1280]{1,0:T(8,128)(2,1)S(1)}, bf16[128,1792]{1,0:T(8,128)(2,1)S(1)}, bf16[128,1792]{1,0:T(8,128)(2,1)S(1)}) custom-call(s32[1]{0:T(128)S(6)} %sub.3.flag, bf16[128,1920]{1,0:T(8,128)(2,1)S(1)} %get-tuple-element.99.refs_0_.own, ...), custom_call_target="tpu_custom_call", output_to_operand_aliasing={{2}: (10, {}), {3}: (11, {})} | custom-call | flops 587202560 | bytes 4587520 | tf_op jit(solution)/shard_map/chain1/leave/pallas_call | solution.py:312
  97.0 2.1 %block_grads.1 = bf16[8,128,128]{2,1,0:T(8,128)(2,1)S(1)} custom-call(s32[8,14]{1,0:T(8,128)S(1)} %pad_add_fusion.plan, bf16[1,1280]{1,0:T(2,128)(2,1)S(1)} %copy-done, bf16[64,1280]{1,0:T(8,128)(2,1)S(1)} %get-tuple-element.143.low.refs_0_, bf16[64,1280]{1,0:T(8,128)(2,1)S(1)} %get-tuple-element.141.high.refs_1_, ...), custom_call_target="tpu_custom_call" | custom-call | flops 67108864 | bytes 262144 | tf_op jit(solution)/shard_map/block_exchange/block_grads/pallas_call | solution.py:92
  99.8 1.0 collective-permute-done.35.relayed
  100.8 3.8 %collective-permute-start.28 = (bf16[16,1280]{1,0:T(8,128)(2,1)S(1)}, bf16[16,1280]{1,0:T(8,128)(2,1)S(1)}, u32[]{:S(2)}, u32[]{:S(2)}) collective-permute-start(bf16[16,1280]{1,0:T(8,128)(2,1)S(1)} %get-tuple-element.153), channel_id=1, source_target_pairs={{0,12},{2,14},{4,0},{6,2},{8,4},{10,6},{12,8},{14,10},{1,13},{3,15... | collective-permute-start | bytes 122888 | tf_op jit(solution)/shard_map/chain1/ppermute | solution.py:32
  105.3 3.2 %collective-permute-start.36 = (bf16[2,128,128]{2,1,0:T(8,128)(2,1)S(1)}, bf16[2,128,128]{2,1,0:T(8,128)(2,1)S(1)}, u32[]{:S(2)}, u32[]{:S(2)}) collective-permute-start(bf16[2,128,128]{2,1,0:T(8,128)(2,1)S(1)} %pad_maximum_fusion.3), channel_id=1, source_target_pairs={{0,12},{2,14},{4,0},{6,2},{8,4},{10,6},{12,8},{14,10},{1,13},{3,15... | collective-permute-start | bytes 196616 | tf_op jit(solution)/shard_map/block_exchange/ppermute | solution.py:32
  108.6 1.9 %collective-permute-done.29.refs_6_ = bf16[16,1280]{1,0:T(8,128)(2,1)S(1)} collective-permute-done((bf16[16,1280]{1,0:T(8,128)(2,1)S(1)}, bf16[16,1280]{1,0:T(8,128)(2,1)S(1)}, u32[]{:S(2)}, u32[]{:S(2)}) %collective-permute-start.29) | collective-permute-done | bytes 40992 | tf_op jit(solution)/shard_map/chain1/ppermute | solution.py:32
  110.7 1.0 forward.1
  111.9 0.9 collective-permute-start.37
  113.3 3.5 %collective-permute-start.32 = (bf16[16,1280]{1,0:T(8,128)(2,1)S(1)}, bf16[16,1280]{1,0:T(8,128)(2,1)S(1)}, u32[]{:S(2)}, u32[]{:S(2)}) collective-permute-start(bf16[16,1280]{1,0:T(8,128)(2,1)S(1)} %get-tuple-element.150), channel_id=1, source_target_pairs={{0,12},{2,14},{4,0},{6,2},{8,4},{10,6},{12,8},{14,10},{1,13},{3,15... | collective-permute-start | bytes 122888 | tf_op jit(solution)/shard_map/off_forward/ppermute | solution.py:32
  117.4 1.5 %collective-permute-done.37.refs_1_ = bf16[2,128,128]{2,1,0:T(8,128)(2,1)S(1)} collective-permute-done((bf16[2,128,128]{2,1,0:T(8,128)(2,1)S(1)}, bf16[2,128,128]{2,1,0:T(8,128)(2,1)S(1)}, u32[]{:S(2)}, u32[]{:S(2)}) %collective-permute-start.37) | collective-permute-done | bytes 65568 | tf_op jit(solution)/shard_map/block_exchange/ppermute | solution.py:32
  119.6 2.3 %adam_step.1 = (f32[6,128,128]{2,1,0:T(8,128)}, f32[6,128,128]{2,1,0:T(8,128)}, f32[6,128,128]{2,1,0:T(8,128)}) custom-call(s32[8,14]{1,0:T(8,128)S(1)} %pad_add_fusion.plan, bf16[4,128,128]{2,1,0:T(8,128)(2,1)S(1)} %collective-permute-done.35.relayed, bf16[2,128,128]{2,1,0:T(8,128)(2,1)S(1)} %collective-permute-done.36.refs_0_, ...), custom_call_target="tpu_custom_call" | custom-call | flops 1966080 | bytes 1966080 | tf_op jit(solution)/shard_map/adam_step/pallas_call | solution.py:92
  (93 shorter events, 12.3 us)
Async XLA Ops:
  3.1 13.1 %collective-permute-start = (bf16[2,16,1280]{2,1,0:T(8,128)(2,1)S(1)}, bf16[2,16,1280]{2,1,0:T(8,128)(2,1)S(1)}, u32[]{:S(2)}, u32[]{:S(2)}) collective-permute-start(bf16[2,16,1280]{2,1,0:T(8,128)(2,1)S(1)} %pad_maximum_fusion.2.after), channel_id=1, source_target_pairs={{0,4},{2,6},{4,8},{6,10},{8,12},{10,14},{12,0},{14,2},{1,5},{3,7},... | collective-permute-start | bytes 245768 | tf_op jit(solution)/shard_map/gather_first/ppermute | solution.py:32
  6.1 10.0 %collective-permute-start.1 = (bf16[2,16,1280]{2,1,0:T(8,128)(2,1)S(1)}, bf16[2,16,1280]{2,1,0:T(8,128)(2,1)S(1)}, u32[]{:S(2)}, u32[]{:S(2)}) collective-permute-start(bf16[2,16,1280]{2,1,0:T(8,128)(2,1)S(1)} %pad_maximum_fusion.2.after), channel_id=1, source_target_pairs={{0,8},{2,10},{4,12},{6,14},{8,0},{10,2},{12,4},{14,6},{1,9},{3,11}... | collective-permute-start | bytes 245768 | tf_op jit(solution)/shard_map/gather_first/ppermute | solution.py:32
  8.7 7.5 %collective-permute-start.2 = (bf16[2,16,1280]{2,1,0:T(8,128)(2,1)S(1)}, bf16[2,16,1280]{2,1,0:T(8,128)(2,1)S(1)}, u32[]{:S(2)}, u32[]{:S(2)}) collective-permute-start(bf16[2,16,1280]{2,1,0:T(8,128)(2,1)S(1)} %pad_maximum_fusion.2.after), channel_id=1, source_target_pairs={{0,12},{2,14},{4,0},{6,2},{8,4},{10,6},{12,8},{14,10},{1,13},{3,15... | collective-permute-start | bytes 245768 | tf_op jit(solution)/shard_map/gather_first/ppermute | solution.py:32
  12.4 5.6 %copy-start = (bf16[1,1280]{1,0:T(2,128)(2,1)S(1)}, bf16[1,1280]{1,0:T(2,128)(2,1)}, u32[]{:S(2)}) copy-start(bf16[1,1280]{1,0:T(2,128)(2,1)} %gain.17) | copy-start | bytes 7684
  16.2 1.7 %collective-permute-start.3 = (bf16[2,64,1280]{2,1,0:T(8,128)(2,1)S(1)}, bf16[2,64,1280]{2,1,0:T(8,128)(2,1)S(1)}, u32[]{:S(2)}, u32[]{:S(2)}) collective-permute-start(bf16[2,64,1280]{2,1,0:T(8,128)(2,1)S(1)} %constant_dynamic-update-slice_fusion), channel_id=1, source_target_pairs={{0,2},{2,0},{4,6},{6,4},{8,10},{10,8},{12,14},{14,12},{1,3},{3,1},... | collective-permute-start | bytes 983048 | tf_op jit(solution)/shard_map/gather_first/ppermute | solution.py:27
  18.8 15.4 %collective-permute-start.5 = (bf16[128,1920]{1,0:T(8,128)(2,1)S(1)}, bf16[128,1920]{1,0:T(8,128)(2,1)S(1)}, u32[]{:S(2)}, u32[]{:S(2)}) collective-permute-start(bf16[128,1920]{1,0:T(8,128)(2,1)S(1)} %products.3.back_own), channel_id=1, source_target_pairs={{0,1},{1,0},{2,3},{3,2},{4,5},{5,4},{6,7},{7,6},{8,9},{9,8},{10,11... | collective-permute-start | bytes 1474568 | tf_op jit(solution)/shard_map/swap_back/ppermute | solution.py:80
  21.8 8.1 %collective-permute-start.6 = (bf16[3,16,1280]{2,1,0:T(8,128)(2,1)S(1)}, bf16[3,16,1280]{2,1,0:T(8,128)(2,1)S(1)}, u32[]{:S(2)}, u32[]{:S(2)}) collective-permute-start(bf16[3,16,1280]{2,1,0:T(8,128)(2,1)S(1)} %pad_maximum_fusion.1), channel_id=1, source_target_pairs={{0,4},{2,6},{4,8},{6,10},{8,12},{10,14},{12,0},{14,2},{1,5},{3,7},... | collective-permute-start | bytes 368648 | tf_op jit(solution)/shard_map/gather_others/ppermute | solution.py:32
  22.5 11.6 %collective-permute-start.7 = (bf16[3,16,1280]{2,1,0:T(8,128)(2,1)S(1)}, bf16[3,16,1280]{2,1,0:T(8,128)(2,1)S(1)}, u32[]{:S(2)}, u32[]{:S(2)}) collective-permute-start(bf16[3,16,1280]{2,1,0:T(8,128)(2,1)S(1)} %pad_maximum_fusion.1), channel_id=1, source_target_pairs={{0,8},{2,10},{4,12},{6,14},{8,0},{10,2},{12,4},{14,6},{1,9},{3,11}... | collective-permute-start | bytes 368648 | tf_op jit(solution)/shard_map/gather_others/ppermute | solution.py:32
  23.9 10.2 %collective-permute-start.8 = (bf16[3,16,1280]{2,1,0:T(8,128)(2,1)S(1)}, bf16[3,16,1280]{2,1,0:T(8,128)(2,1)S(1)}, u32[]{:S(2)}, u32[]{:S(2)}) collective-permute-start(bf16[3,16,1280]{2,1,0:T(8,128)(2,1)S(1)} %pad_maximum_fusion.1), channel_id=1, source_target_pairs={{0,12},{2,14},{4,0},{6,2},{8,4},{10,6},{12,8},{14,10},{1,13},{3,15... | collective-permute-start | bytes 368648 | tf_op jit(solution)/shard_map/gather_others/ppermute | solution.py:32
  34.2 1.9 %collective-permute-start.9 = (bf16[3,64,1280]{2,1,0:T(8,128)(2,1)S(1)}, bf16[3,64,1280]{2,1,0:T(8,128)(2,1)S(1)}, u32[]{:S(2)}, u32[]{:S(2)}) collective-permute-start(bf16[3,64,1280]{2,1,0:T(8,128)(2,1)S(1)} %constant_dynamic-update-slice_fusion.4), channel_id=1, source_target_pairs={{0,2},{2,0},{4,6},{6,4},{8,10},{10,8},{12,14},{14,12},{1,3},{3,1},... | collective-permute-start | bytes 1474568 | tf_op jit(solution)/shard_map/gather_others/ppermute | solution.py:27
  34.3 13.6 %collective-permute-start.4 = (bf16[128,1920]{1,0:T(8,128)(2,1)S(1)}, bf16[128,1920]{1,0:T(8,128)(2,1)S(1)}, u32[]{:S(2)}, u32[]{:S(2)}) collective-permute-start(bf16[128,1920]{1,0:T(8,128)(2,1)S(1)} %get-tuple-element.79.own), channel_id=1, source_target_pairs={{0,1},{1,0},{2,3},{3,2},{4,5},{5,4},{6,7},{7,6},{8,9},{9,8},{10,11... | collective-permute-start | bytes 1474568 | tf_op jit(solution)/shard_map/swap_chain0/ppermute | solution.py:80
  49.0 1.5 %collective-permute-start.10 = (bf16[64,1280]{1,0:T(8,128)(2,1)S(1)}, bf16[64,1280]{1,0:T(8,128)(2,1)S(1)}, u32[]{:S(2)}, u32[]{:S(2)}) collective-permute-start(bf16[64,1280]{1,0:T(8,128)(2,1)S(1)} %get-tuple-element.91), channel_id=1, source_target_pairs={{0,2},{2,0},{4,6},{6,4},{8,10},{10,8},{12,14},{14,12},{1,3},{3,1},... | collective-permute-start | bytes 491528 | tf_op jit(solution)/shard_map/chain0/ppermute | solution.py:27
  49.1 14.1 %collective-permute-start.14 = (bf16[128,1920]{1,0:T(8,128)(2,1)S(1)}, bf16[128,1920]{1,0:T(8,128)(2,1)S(1)}, u32[]{:S(2)}, u32[]{:S(2)}) collective-permute-start(bf16[128,1920]{1,0:T(8,128)(2,1)S(1)} %products.4.refs_0_.own), channel_id=1, source_target_pairs={{0,1},{1,0},{2,3},{3,2},{4,5},{5,4},{6,7},{7,6},{8,9},{9,8},{10,11... | collective-permute-start | bytes 1474568 | tf_op jit(solution)/shard_map/swap_off_back/ppermute | solution.py:80
  50.5 4.8 %collective-permute-start.11 = (bf16[16,1280]{1,0:T(8,128)(2,1)S(1)}, bf16[16,1280]{1,0:T(8,128)(2,1)S(1)}, u32[]{:S(2)}, u32[]{:S(2)}) collective-permute-start(bf16[16,1280]{1,0:T(8,128)(2,1)S(1)} %get-tuple-element.159), channel_id=1, source_target_pairs={{0,12},{2,14},{4,0},{6,2},{8,4},{10,6},{12,8},{14,10},{1,13},{3,15... | collective-permute-start | bytes 122888 | tf_op jit(solution)/shard_map/chain0/ppermute | solution.py:32
  52.8 5.5 %collective-permute-start.12 = (bf16[16,1280]{1,0:T(8,128)(2,1)S(1)}, bf16[16,1280]{1,0:T(8,128)(2,1)S(1)}, u32[]{:S(2)}, u32[]{:S(2)}) collective-permute-start(bf16[16,1280]{1,0:T(8,128)(2,1)S(1)} %get-tuple-element.158), channel_id=1, source_target_pairs={{0,8},{2,10},{4,12},{6,14},{8,0},{10,2},{12,4},{14,6},{1,9},{3,11}... | collective-permute-start | bytes 122888 | tf_op jit(solution)/shard_map/chain0/ppermute | solution.py:32
  54.6 5.8 %collective-permute-start.13 = (bf16[16,1280]{1,0:T(8,128)(2,1)S(1)}, bf16[16,1280]{1,0:T(8,128)(2,1)S(1)}, u32[]{:S(2)}, u32[]{:S(2)}) collective-permute-start(bf16[16,1280]{1,0:T(8,128)(2,1)S(1)} %get-tuple-element.157), channel_id=1, source_target_pairs={{0,4},{2,6},{4,8},{6,10},{8,12},{10,14},{12,0},{14,2},{1,5},{3,7},... | collective-permute-start | bytes 122888 | tf_op jit(solution)/shard_map/chain0/ppermute | solution.py:32
  54.6 20.6 %collective-permute-start.15 = (bf16[128,1792]{1,0:T(8,128)(2,1)S(1)}, bf16[128,1792]{1,0:T(8,128)(2,1)S(1)}, u32[]{:S(2)}, u32[]{:S(2)}) collective-permute-start(bf16[128,1792]{1,0:T(8,128)(2,1)S(1)} %act_grads.1.refs_1_.act_own), channel_id=1, source_target_pairs={{0,1},{1,0},{2,3},{3,2},{4,5},{5,4},{6,7},{7,6},{8,9},{9,8},{10,11... | collective-permute-start | bytes 1376264 | tf_op jit(solution)/shard_map/swap_off_act/ppermute | solution.py:80
  63.2 8.4 %collective-permute-start.19 = (bf16[1,16,1280]{2,1,0:T(8,128)(2,1)S(1)}, bf16[1,16,1280]{2,1,0:T(8,128)(2,1)S(1)}, u32[]{:S(2)}, u32[]{:S(2)}) collective-permute-start(bf16[1,16,1280]{2,1,0:T(8,128)(2,1)S(1)} %bitcast.63), channel_id=1, source_target_pairs={{0,28},{2,30},{4,16},{6,18},{8,20},{10,22},{12,24},{14,26},{16,12}... | collective-permute-start | bytes 122888 | tf_op jit(solution)/shard_map/pass/ppermute | solution.py:50
  68.3 5.8 %collective-permute-start.18 = (bf16[1,16,1280]{2,1,0:T(8,128)(2,1)S(1)}, bf16[1,16,1280]{2,1,0:T(8,128)(2,1)S(1)}, u32[]{:S(2)}, u32[]{:S(2)}) collective-permute-start(bf16[1,16,1280]{2,1,0:T(8,128)(2,1)S(1)} %bitcast.64), channel_id=1, source_target_pairs={{0,24},{2,26},{4,28},{6,30},{8,16},{10,18},{12,20},{14,22},{16,8},... | collective-permute-start | bytes 122888 | tf_op jit(solution)/shard_map/pass/ppermute | solution.py:50
  68.3 6.7 %collective-permute-start.17 = (bf16[1,16,1280]{2,1,0:T(8,128)(2,1)S(1)}, bf16[1,16,1280]{2,1,0:T(8,128)(2,1)S(1)}, u32[]{:S(2)}, u32[]{:S(2)}) collective-permute-start(bf16[1,16,1280]{2,1,0:T(8,128)(2,1)S(1)} %bitcast.65), channel_id=1, source_target_pairs={{0,20},{2,22},{4,24},{6,26},{8,28},{10,30},{12,16},{14,18},{16,4},... | collective-permute-start | bytes 122888 | tf_op jit(solution)/shard_map/pass/ppermute | solution.py:50
  70.5 4.5 %collective-permute-start.16 = (bf16[1,16,1280]{2,1,0:T(8,128)(2,1)S(1)}, bf16[1,16,1280]{2,1,0:T(8,128)(2,1)S(1)}, u32[]{:S(2)}, u32[]{:S(2)}) collective-permute-start(bf16[1,16,1280]{2,1,0:T(8,128)(2,1)S(1)} %bitcast.66), channel_id=1, source_target_pairs={{0,16},{2,18},{4,20},{6,22},{8,24},{10,26},{12,28},{14,30},{16,0},... | collective-permute-start | bytes 122888 | tf_op jit(solution)/shard_map/pass/ppermute | solution.py:50
  75.1 1.5 %collective-permute-start.20 = (bf16[64,1280]{1,0:T(8,128)(2,1)S(1)}, bf16[64,1280]{1,0:T(8,128)(2,1)S(1)}, u32[]{:S(2)}, u32[]{:S(2)}) collective-permute-start(bf16[64,1280]{1,0:T(8,128)(2,1)S(1)} %pad_maximum_fusion.low), channel_id=1, source_target_pairs={{0,2},{2,0},{4,6},{6,4},{8,10},{10,8},{12,14},{14,12},{1,3},{3,1},... | collective-permute-start | bytes 491528 | tf_op jit(solution)/shard_map/pass/ppermute | solution.py:27
  80.5 2.2 %collective-permute-start.21 = (bf16[64,1280]{1,0:T(8,128)(2,1)S(1)}, bf16[64,1280]{1,0:T(8,128)(2,1)S(1)}, u32[]{:S(2)}, u32[]{:S(2)}) collective-permute-start(bf16[64,1280]{1,0:T(8,128)(2,1)S(1)} %get-tuple-element.101), channel_id=1, source_target_pairs={{0,2},{2,0},{4,6},{6,4},{8,10},{10,8},{12,14},{14,12},{1,3},{3,1},... | collective-permute-start | bytes 491528 | tf_op jit(solution)/shard_map/off_back/ppermute | solution.py:27
  80.7 14.1 %collective-permute-start.25 = (bf16[128,1920]{1,0:T(8,128)(2,1)S(1)}, bf16[128,1920]{1,0:T(8,128)(2,1)S(1)}, u32[]{:S(2)}, u32[]{:S(2)}) collective-permute-start(bf16[128,1920]{1,0:T(8,128)(2,1)S(1)} %get-tuple-element.99.refs_0_.own), channel_id=1, source_target_pairs={{0,1},{1,0},{2,3},{3,2},{4,5},{5,4},{6,7},{7,6},{8,9},{9,8},{10,11... | collective-permute-start | bytes 1474568 | tf_op jit(solution)/shard_map/swap_chain1/ppermute | solution.py:80
  81.2 27.3 %collective-permute-start.26 = (bf16[128,1920]{1,0:T(8,128)(2,1)S(1)}, bf16[128,1920]{1,0:T(8,128)(2,1)S(1)}, u32[]{:S(2)}, u32[]{:S(2)}) collective-permute-start(bf16[128,1920]{1,0:T(8,128)(2,1)S(1)} %products.5.refs_2_.own), channel_id=1, source_target_pairs={{0,1},{1,0},{2,3},{3,2},{4,5},{5,4},{6,7},{7,6},{8,9},{9,8},{10,11... | collective-permute-start | bytes 1474568 | tf_op jit(solution)/shard_map/swap_off_forward/ppermute | solution.py:80
  82.8 14.1 %collective-permute-start.22 = (bf16[16,1280]{1,0:T(8,128)(2,1)S(1)}, bf16[16,1280]{1,0:T(8,128)(2,1)S(1)}, u32[]{:S(2)}, u32[]{:S(2)}) collective-permute-start(bf16[16,1280]{1,0:T(8,128)(2,1)S(1)} %get-tuple-element.156), channel_id=1, source_target_pairs={{0,12},{2,14},{4,0},{6,2},{8,4},{10,6},{12,8},{14,10},{1,13},{3,15... | collective-permute-start | bytes 122888 | tf_op jit(solution)/shard_map/off_back/ppermute | solution.py:32
  86.6 10.3 %collective-permute-start.23 = (bf16[16,1280]{1,0:T(8,128)(2,1)S(1)}, bf16[16,1280]{1,0:T(8,128)(2,1)S(1)}, u32[]{:S(2)}, u32[]{:S(2)}) collective-permute-start(bf16[16,1280]{1,0:T(8,128)(2,1)S(1)} %get-tuple-element.155), channel_id=1, source_target_pairs={{0,8},{2,10},{4,12},{6,14},{8,0},{10,2},{12,4},{14,6},{1,9},{3,11}... | collective-permute-start | bytes 122888 | tf_op jit(solution)/shard_map/off_back/ppermute | solution.py:32
  86.6 10.3 %collective-permute-start.24 = (bf16[16,1280]{1,0:T(8,128)(2,1)S(1)}, bf16[16,1280]{1,0:T(8,128)(2,1)S(1)}, u32[]{:S(2)}, u32[]{:S(2)}) collective-permute-start(bf16[16,1280]{1,0:T(8,128)(2,1)S(1)} %get-tuple-element.154), channel_id=1, source_target_pairs={{0,4},{2,6},{4,8},{6,10},{8,12},{10,14},{12,0},{14,2},{1,5},{3,7},... | collective-permute-start | bytes 122888 | tf_op jit(solution)/shard_map/off_back/ppermute | solution.py:32
  96.9 3.8 %collective-permute-start.27 = (bf16[64,1280]{1,0:T(8,128)(2,1)S(1)}, bf16[64,1280]{1,0:T(8,128)(2,1)S(1)}, u32[]{:S(2)}, u32[]{:S(2)}) collective-permute-start(bf16[64,1280]{1,0:T(8,128)(2,1)S(1)} %get-tuple-element.110), channel_id=1, source_target_pairs={{0,2},{2,0},{4,6},{6,4},{8,10},{10,8},{12,14},{14,12},{1,3},{3,1},... | collective-permute-start | bytes 491528 | tf_op jit(solution)/shard_map/chain1/ppermute | solution.py:27
  99.2 1.6 %collective-permute-start.35 = (bf16[4,128,128]{2,1,0:T(8,128)(2,1)S(1)}, bf16[4,128,128]{2,1,0:T(8,128)(2,1)S(1)}, u32[]{:S(2)}, u32[]{:S(2)}) collective-permute-start(bf16[4,128,128]{2,1,0:T(8,128)(2,1)S(1)} %slice.199), channel_id=1, source_target_pairs={{0,2},{2,0},{4,6},{6,4},{8,10},{10,8},{12,14},{14,12},{1,3},{3,1},... | collective-permute-start | bytes 393224 | tf_op jit(solution)/shard_map/block_exchange/ppermute | solution.py:27
  100.8 7.7 %collective-permute-start.28 = (bf16[16,1280]{1,0:T(8,128)(2,1)S(1)}, bf16[16,1280]{1,0:T(8,128)(2,1)S(1)}, u32[]{:S(2)}, u32[]{:S(2)}) collective-permute-start(bf16[16,1280]{1,0:T(8,128)(2,1)S(1)} %get-tuple-element.153), channel_id=1, source_target_pairs={{0,12},{2,14},{4,0},{6,2},{8,4},{10,6},{12,8},{14,10},{1,13},{3,15... | collective-permute-start | bytes 122888 | tf_op jit(solution)/shard_map/chain1/ppermute | solution.py:32
  104.6 5.8 %collective-permute-start.29 = (bf16[16,1280]{1,0:T(8,128)(2,1)S(1)}, bf16[16,1280]{1,0:T(8,128)(2,1)S(1)}, u32[]{:S(2)}, u32[]{:S(2)}) collective-permute-start(bf16[16,1280]{1,0:T(8,128)(2,1)S(1)} %get-tuple-element.152), channel_id=1, source_target_pairs={{0,8},{2,10},{4,12},{6,14},{8,0},{10,2},{12,4},{14,6},{1,9},{3,11}... | collective-permute-start | bytes 122888 | tf_op jit(solution)/shard_map/chain1/ppermute | solution.py:32
  104.6 6.1 %collective-permute-start.30 = (bf16[16,1280]{1,0:T(8,128)(2,1)S(1)}, bf16[16,1280]{1,0:T(8,128)(2,1)S(1)}, u32[]{:S(2)}, u32[]{:S(2)}) collective-permute-start(bf16[16,1280]{1,0:T(8,128)(2,1)S(1)} %get-tuple-element.151), channel_id=1, source_target_pairs={{0,4},{2,6},{4,8},{6,10},{8,12},{10,14},{12,0},{14,2},{1,5},{3,7},... | collective-permute-start | bytes 122888 | tf_op jit(solution)/shard_map/chain1/ppermute | solution.py:32
  105.3 11.8 %collective-permute-start.36 = (bf16[2,128,128]{2,1,0:T(8,128)(2,1)S(1)}, bf16[2,128,128]{2,1,0:T(8,128)(2,1)S(1)}, u32[]{:S(2)}, u32[]{:S(2)}) collective-permute-start(bf16[2,128,128]{2,1,0:T(8,128)(2,1)S(1)} %pad_maximum_fusion.3), channel_id=1, source_target_pairs={{0,12},{2,14},{4,0},{6,2},{8,4},{10,6},{12,8},{14,10},{1,13},{3,15... | collective-permute-start | bytes 196616 | tf_op jit(solution)/shard_map/block_exchange/ppermute | solution.py:32
  108.5 11.1 %copy-start.1 = (f32[1,1,1,6,128,128]{5,4,3,2,1,0:T(8,128)S(1)}, f32[1,1,1,6,128,128]{5,4,3,2,1,0:T(8,128)}, u32[]{:S(2)}) copy-start(f32[1,1,1,6,128,128]{5,4,3,2,1,0:T(8,128)} %param.26) | copy-start | bytes 1179652
  108.5 11.1 %copy-start.2 = (f32[1,1,1,6,128,128]{5,4,3,2,1,0:T(8,128)S(1)}, f32[1,1,1,6,128,128]{5,4,3,2,1,0:T(8,128)}, u32[]{:S(2)}) copy-start(f32[1,1,1,6,128,128]{5,4,3,2,1,0:T(8,128)} %param.27) | copy-start | bytes 1179652
  111.8 1.5 %collective-permute-start.31 = (bf16[64,1280]{1,0:T(8,128)(2,1)S(1)}, bf16[64,1280]{1,0:T(8,128)(2,1)S(1)}, u32[]{:S(2)}, u32[]{:S(2)}) collective-permute-start(bf16[64,1280]{1,0:T(8,128)(2,1)S(1)} %get-tuple-element.114), channel_id=1, source_target_pairs={{0,2},{2,0},{4,6},{6,4},{8,10},{10,8},{12,14},{14,12},{1,3},{3,1},... | collective-permute-start | bytes 491528 | tf_op jit(solution)/shard_map/off_forward/ppermute | solution.py:27
  111.9 7.0 %collective-permute-start.37 = (bf16[2,128,128]{2,1,0:T(8,128)(2,1)S(1)}, bf16[2,128,128]{2,1,0:T(8,128)(2,1)S(1)}, u32[]{:S(2)}, u32[]{:S(2)}) collective-permute-start(bf16[2,128,128]{2,1,0:T(8,128)(2,1)S(1)} %pad_maximum_fusion.4), channel_id=1, source_target_pairs={{0,8},{2,10},{4,12},{6,14},{8,0},{10,2},{12,4},{14,6},{1,9},{3,11}... | collective-permute-start | bytes 196616 | tf_op jit(solution)/shard_map/block_exchange/ppermute | solution.py:32
  112.8 6.8 %collective-permute-start.38 = (bf16[2,128,128]{2,1,0:T(8,128)(2,1)S(1)}, bf16[2,128,128]{2,1,0:T(8,128)(2,1)S(1)}, u32[]{:S(2)}, u32[]{:S(2)}) collective-permute-start(bf16[2,128,128]{2,1,0:T(8,128)(2,1)S(1)} %pad_maximum_fusion.5), channel_id=1, source_target_pairs={{0,4},{2,6},{4,8},{6,10},{8,12},{10,14},{12,0},{14,2},{1,5},{3,7},... | collective-permute-start | bytes 196616 | tf_op jit(solution)/shard_map/block_exchange/ppermute | solution.py:32
  113.3 8.6 %collective-permute-start.32 = (bf16[16,1280]{1,0:T(8,128)(2,1)S(1)}, bf16[16,1280]{1,0:T(8,128)(2,1)S(1)}, u32[]{:S(2)}, u32[]{:S(2)}) collective-permute-start(bf16[16,1280]{1,0:T(8,128)(2,1)S(1)} %get-tuple-element.150), channel_id=1, source_target_pairs={{0,12},{2,14},{4,0},{6,2},{8,4},{10,6},{12,8},{14,10},{1,13},{3,15... | collective-permute-start | bytes 122888 | tf_op jit(solution)/shard_map/off_forward/ppermute | solution.py:32
  116.8 5.4 %collective-permute-start.33 = (bf16[16,1280]{1,0:T(8,128)(2,1)S(1)}, bf16[16,1280]{1,0:T(8,128)(2,1)S(1)}, u32[]{:S(2)}, u32[]{:S(2)}) collective-permute-start(bf16[16,1280]{1,0:T(8,128)(2,1)S(1)} %get-tuple-element.149), channel_id=1, source_target_pairs={{0,8},{2,10},{4,12},{6,14},{8,0},{10,2},{12,4},{14,6},{1,9},{3,11}... | collective-permute-start | bytes 122888 | tf_op jit(solution)/shard_map/off_forward/ppermute | solution.py:32
  117.0 5.8 %collective-permute-start.34 = (bf16[16,1280]{1,0:T(8,128)(2,1)S(1)}, bf16[16,1280]{1,0:T(8,128)(2,1)S(1)}, u32[]{:S(2)}, u32[]{:S(2)}) collective-permute-start(bf16[16,1280]{1,0:T(8,128)(2,1)S(1)} %get-tuple-element.148), channel_id=1, source_target_pairs={{0,4},{2,6},{4,8},{6,10},{8,12},{10,14},{12,0},{14,2},{1,5},{3,7},... | collective-permute-start | bytes 122888 | tf_op jit(solution)/shard_map/off_forward/ppermute | solution.py:32

commit v3 on v2

--- a/solution.py
+++ b/solution.py
@@ -56,13 +56,17 @@
 
 
 def halves(pieces):
-    mine = jnp.concatenate(pieces, axis=-2)
-    return mine, sibling(mine)
+    mine = [jnp.concatenate([piece[i] for piece in pieces]) for i in range(pieces[0].shape[0])]
+    return [[half, sibling(half)] for half in mine]
 
 
 def scatter_pairs(kept, sent):
+    return summed_pairs(kept, sibling(sent))
+
+
+def summed_pairs(kept, got):
     depth = lax.axis_size("dp") // 2
-    return (kept + sibling(sent).astype(F32)).reshape((depth, kept.shape[0] // depth, kept.shape[1]))
+    return (kept + got.astype(F32)).reshape((depth, kept.shape[0] // depth, kept.shape[1]))
 
 
 def scatter_parts(pairs):
@@ -96,7 +100,7 @@
         out_specs=[VMEM] * len(outs),
         scratch_shapes=scratch,
         compiler_params=pltpu.CompilerParams(vmem_limit_bytes=12 * MIB),
-        cost_estimate=pl.CostEstimate(flops=flops, bytes_accessed=moved, transcendentals=0),
+        cost_estimate=pl.CostEstimate(flops=1, bytes_accessed=1, transcendentals=0),
         name=name,
     )(*operands)
 
@@ -115,6 +119,56 @@
         copy.start()
     for copy in copies:
         copy.wait()
+
+
+def load_one_kernel(source, *refs):
+    target, sem = refs[-2:]
+    copy = pltpu.make_async_copy(source, target, sem)
+    copy.start()
+    copy.wait()
+
+
+def load_one(weight, after):
+    return pl.pallas_call(
+        load_one_kernel,
+        out_shape=pltpu.VMEM(weight.shape, BF16),
+        in_specs=[HBM] + [ANY] * len(after),
+        out_specs=VMEM,
+        scratch_shapes=[pltpu.SemaphoreType.DMA(())],
+        compiler_params=pltpu.CompilerParams(vmem_limit_bytes=8 * MIB),
+        name="load_weight",
+    )(in_hbm(weight), *after)
+
+
+def first_kernel(flag, stash, begin, start, out, sems):
+    stashed = pltpu.make_async_copy(stash.at[flag[0]], out.at[0], sems.at[0])
+    stashed.start()
+
+    @pl.when(flag[0] == 1)
+    def _():
+        copy = pltpu.make_async_copy(begin, out.at[1], sems.at[1])
+        copy.start()
+        copy.wait()
+
+    @pl.when(flag[0] == 0)
+    def _():
+        copy = pltpu.make_async_copy(start, out.at[1], sems.at[1])
+        copy.start()
+        copy.wait()
+
+    stashed.wait()
+
+
+def first_rows_of(flag, stash, begin, start):
+    return pl.pallas_call(
+        first_kernel,
+        out_shape=struct(2, *begin.shape),
+        in_specs=[SMEM] + [HBM] * 3,
+        out_specs=VMEM,
+        scratch_shapes=[pltpu.SemaphoreType.DMA((2,))],
+        compiler_params=pltpu.CompilerParams(vmem_limit_bytes=2 * MIB),
+        name="first_rows",
+    )(flag, *map(in_hbm, [stash, begin, start]))
 
 
 def load_weights(up, down, after):
@@ -157,16 +211,18 @@
     return jnp.concatenate([low[...], high[...]], axis=0)
 
 
-def product_kernel(low, high, gain, up, _, sent, normed):
+def product_kernel(low, high, gain, up, *refs):
+    sent, normed = refs[-2:]
     write_products(joined(low, high), gain, up, sent, normed)
 
 
 def products(row_halves, gain, up, down):
     rows = 2 * row_halves[0].shape[0]
     channels, hidden = up.shape
+    operands = [*row_halves, gain, up, *down]
     return call(
         product_kernel, "products", [struct(rows, hidden + BLK)],
-        [*row_halves, gain, up, down], [VMEM] * 5, 2 * rows * channels * hidden, 2 * channels * hidden,
+        operands, [VMEM] * len(operands), 2 * rows * channels * hidden, 2 * channels * hidden,
         [pltpu.VMEM((rows, channels), BF16)],
     )[0]
 
@@ -182,6 +238,23 @@
     return call(
         act_kernel, "act_grads", [struct(rows, hidden)],
         [*grad_halves, down, up], [VMEM] * 4, 2 * rows * channels * hidden, 2 * channels * hidden,
+        [pltpu.VMEM((rows, channels), BF16)],
+    )[0]
+
+
+def product_act_kernel(low, high, grad_low, grad_high, gain, up, down, sent, normed):
+    width = up.shape[1] + BLK
+    write_products(joined(low, high), gain, up, sent.at[:, :width], normed)
+    normed[...] = joined(grad_low, grad_high)
+    write_act_grads(normed, down, sent.at[:, width:])
+
+
+def products_and_act_grads(row_halves, grad_halves, gain, up, down):
+    rows = 2 * row_halves[0].shape[0]
+    channels, hidden = up.shape
+    return call(
+        product_act_kernel, "products_and_act_grads", [struct(rows, 2 * hidden + BLK)],
+        [*row_halves, *grad_halves, gain, up, down], [VMEM] * 7, 4 * rows * channels * hidden, 4 * channels * hidden,
         [pltpu.VMEM((rows, channels), BF16)],
     )[0]
 
@@ -241,6 +314,25 @@
     write_backward(width, own, got, act_own, act_got, low, high, gain, up, *refs[-4:])
 
 
+def joint_backward_kernel(width, own, got, low, high, gain, up, _, *refs):
+    cut = up.shape[1] + BLK
+    write_backward(
+        width, own.at[:, :cut], got.at[:, :cut], own.at[:, cut:], got.at[:, cut:], low, high, gain, up, *refs[-4:]
+    )
+
+
+def joint_backward(width, parts, row_halves, gain, up, down, after):
+    half, channels = row_halves[0].shape
+    hidden = up.shape[1]
+    outs = [struct(half, channels, dtype=F32), struct(half, channels), struct(2 * half, hidden), struct(2 * half, hidden)]
+    operands = [*parts, *row_halves, gain, up, down]
+    return call(
+        functools.partial(joint_backward_kernel, width), "backward", outs, operands + after,
+        [VMEM] * len(operands) + [ANY] * len(after),
+        4 * half * channels * hidden, 2 * channels * hidden,
+    )
+
+
 def backward(width, products_parts, act_parts, row_halves, gain, up, down, after):
     half, channels = row_halves[0].shape
     hidden = up.shape[1]
@@ -268,56 +360,56 @@
     )
 
 
-def enter_kernel(flag, low, high, other_low, other_high, gain, up, down, sent, grads, normed):
-    @pl.when(flag[0] == 1)
+def enter_kernel(forward_in, flag, low, high, other_low, other_high, gain, up, down, sent, grads, normed):
+    @pl.when(flag[0] == forward_in)
     def _():
         write_products(joined(low, high), gain, up, sent, normed)
         grads[...] = joined(other_low, other_high)
 
-    @pl.when(flag[0] == 0)
+    @pl.when(flag[0] != forward_in)
     def _():
         grads[...] = joined(low, high)
         write_act_grads(grads, down, sent)
         sent[:, up.shape[1] :] = jnp.zeros((sent.shape[0], BLK), BF16)
 
 
-def enter(flag, row_halves, other_halves, gain, up, down):
+def enter(forward_in, flag, row_halves, other_halves, gain, up, down):
     rows = 2 * row_halves[0].shape[0]
     channels, hidden = up.shape
     return call(
-        enter_kernel, "enter", [struct(rows, hidden + BLK), struct(rows, channels)],
+        functools.partial(enter_kernel, forward_in), "enter", [struct(rows, hidden + BLK), struct(rows, channels)],
         [flag, *row_halves, *other_halves, gain, up, down], [SMEM] + [VMEM] * 7,
         2 * rows * channels * hidden, 2 * channels * hidden, [pltpu.VMEM((rows, channels), BF16)],
     )
 
 
-def leave_kernel(width, flag, own, got, back_own, back_got, low, high, gain, up, down, *refs):
+def leave_kernel(forward_in, width, flag, own, got, back_own, back_got, low, high, gain, up, down, *refs):
     kept, sent, scaled, activated, scratch = refs[-5:]
 
-    @pl.when(flag[0] == 1)
+    @pl.when(flag[0] == forward_in)
     def _():
         write_forward(width, own, got, down, kept, sent, scratch)
 
-    @pl.when(flag[0] == 0)
+    @pl.when(flag[0] != forward_in)
     def _():
         write_backward(width, back_own, back_got, own, got, low, high, gain, up, kept, sent, scaled, activated)
 
 
-def leave(width, flag, parts, back_parts, row_halves, gain, up, down, filled, after):
+def leave(width, forward_in, flag, parts, back_parts, row_halves, gain, up, down, filled, after):
     half, channels = row_halves[0].shape
     hidden = up.shape[1]
     outs = [struct(half, channels, dtype=F32), struct(half, channels), struct(2 * half, hidden), struct(2 * half, hidden)]
     operands = [flag, *parts, *back_parts, *row_halves, gain, up, down, *filled]
     first = len(operands) - len(filled)
     return pl.pallas_call(
-        functools.partial(leave_kernel, width),
+        functools.partial(leave_kernel, forward_in, width),
         out_shape=outs,
         in_specs=[SMEM] + [VMEM] * (len(operands) - 1) + [ANY] * len(after),
         out_specs=[VMEM] * 4,
         scratch_shapes=[pltpu.VMEM((2 * half, hidden), BF16)],
         input_output_aliases={first + i: 2 + i for i in range(len(filled))},
         compiler_params=pltpu.CompilerParams(vmem_limit_bytes=12 * MIB),
-        cost_estimate=pl.CostEstimate(flops=4 * half * channels * hidden, bytes_accessed=2 * channels * hidden, transcendentals=0),
+        cost_estimate=pl.CostEstimate(flops=1, bytes_accessed=1, transcendentals=0),
         name="leave",
     )(*operands, *after)
 
@@ -394,21 +486,28 @@
 
 
 def adam_kernel(depth, plan, relayed, *refs):
-    *others, first, second, first_out, second_out, direction_out = refs
+    others = refs[: depth - 1]
+    first, second, *rest = refs[depth - 1 :]
+    outs, (first_new, second_new, direction), sems = rest[-7:-4], rest[-4:-1], rest[-1]
     dp_index = plan[0, DP]
     z, core = dp_index // 2, lax.rem(dp_index, 2)
     slots, capacity = plan.shape[0], first.shape[0]
-    first_out[...] = jnp.zeros(first_out.shape, F32)
-    second_out[...] = jnp.zeros(first_out.shape, F32)
-    direction_out[...] = jnp.zeros(first_out.shape, F32)
+
+    def copies(place):
+        return [
+            pltpu.make_async_copy(new.at[place], out.at[place], sems.at[i, place])
+            for i, (new, out) in enumerate(zip((first_new, second_new, direction), outs))
+        ]
 
     def update(place, grad):
         grad = grad.astype(F32)
-        first_new = 0.9 * first[place] + 0.1 * grad
-        second_new = 0.999 * second[place] + 0.001 * grad * grad
-        first_out[place] = first_new
-        second_out[place] = second_new
-        direction_out[place] = first_new / (jnp.sqrt(second_new) + 1e-08)
+        first_next = 0.9 * first[place] + 0.1 * grad
+        second_next = 0.999 * second[place] + 0.001 * grad * grad
+        first_new[place] = first_next
+        second_new[place] = second_next
+        direction[place] = first_next / (jnp.sqrt(second_next) + 1e-08)
+        for copy in copies(place):
+            copy.start()
 
     def per_source(source, place):
         sends = False
@@ -422,20 +521,37 @@
                 if k == 0:
                     update(place, relayed[0])
                 else:
-                    update(place, others[k - 1][across])
+                    update(place, others[k - 1][pl.ds(pl.multiple_of(across * BLK, BLK), BLK)])
 
         return place + jnp.where(sends, 1, 0)
 
-    lax.fori_loop(0, slots, per_source, 0)
-
-
-def adam(plan, relayed, others, first, second):
+    count = lax.fori_loop(0, slots, per_source, 0)
+
+    def empty(place, carry):
+        for new in (first_new, second_new, direction):
+            new[place] = jnp.zeros((BLK, BLK), F32)
+        for copy in copies(place):
+            copy.start()
+        return carry
+
+    lax.fori_loop(count, capacity, empty, 0)
+    for place in range(capacity):
+        for copy in copies(place):
+            copy.wait()
+
+
+def adam(plan, relayed, others, first, second, after):
     shape = jax.ShapeDtypeStruct(first.shape, F32)
     operands = [plan, relayed, *others, first, second]
-    return call(
-        functools.partial(adam_kernel, lax.axis_size("dp") // 2), "adam_step", [shape] * 3, operands,
-        [SMEM] + [VMEM] * (len(operands) - 1), 20 * first.size, 20 * first.size,
-    )
+    return pl.pallas_call(
+        functools.partial(adam_kernel, lax.axis_size("dp") // 2),
+        out_shape=[shape] * 3,
+        in_specs=[SMEM] + [VMEM] * (len(operands) - 1) + [ANY] * len(after),
+        out_specs=[HBM] * 3,
+        scratch_shapes=[pltpu.VMEM(first.shape, F32)] * 3 + [pltpu.SemaphoreType.DMA((3, first.shape[0]))],
+        compiler_params=pltpu.CompilerParams(vmem_limit_bytes=12 * MIB),
+        name="adam_step",
+    )(*operands, *after)
 
 
 def finish_kernel(earlier_count, *refs):
@@ -456,112 +572,120 @@
     )[0]
 
 
-def finish_pair_kernel(depth, flag, chained, off_back, forward_rows, chain_rows, *refs):
-    forward_parts, chain_parts, (section_out, grads_out) = refs[:depth], refs[depth : 2 * depth], refs[2 * depth :]
-
-    def total(rows, parts):
-        value = rows[...].astype(F32)
+def finish_pair_kernel(depth, flag, chained, off_grads, off_rows, chain_rows, *refs):
+    off_parts, chain_parts, (section_out, grads_out, done) = refs[:depth], refs[depth : 2 * depth], refs[2 * depth :]
+    done[...] = jnp.zeros(done.shape, F32)
+
+    def total(local, parts):
+        value = local[...].astype(F32)
         for part in parts:
             value += part[...].astype(F32)
         return value.astype(BF16)
 
-    off_forward = total(forward_rows, forward_parts)
-    chained_later = total(chain_rows, chain_parts)
+    off_back = total(off_grads, [part.at[0] for part in off_parts])
+    off_forward = total(off_rows, [part.at[1] for part in off_parts])
+    later_turn = total(chain_rows, chain_parts)
 
     @pl.when(flag[0] == 1)
     def _():
         section_out[0] = chained[...]
         section_out[1] = off_forward
-        grads_out[0] = off_back[...]
-        grads_out[1] = chained_later
+        grads_out[0] = off_back
+        grads_out[1] = later_turn
 
     @pl.when(flag[0] == 0)
     def _():
         section_out[0] = off_forward
-        section_out[1] = chained_later
+        section_out[1] = later_turn
         grads_out[0] = chained[...]
-        grads_out[1] = off_back[...]
-
-
-def finish_pair(flag, chained, off_back, forward_rows, forward_parts, chain_rows, chain_parts):
-    operands = [flag, chained, off_back, forward_rows, chain_rows, *forward_parts, *chain_parts]
-    return call(
-        functools.partial(finish_pair_kernel, len(chain_parts)), "finish_pair", [struct(2, *chained.shape)] * 2, operands,
+        grads_out[1] = off_back
+
+
+def finish_pair(flag, chained, off_grads, off_rows, chain_rows, off_parts, chain_parts):
+    operands = [flag, chained, off_grads, off_rows, chain_rows, *off_parts, *chain_parts]
+    return call(
+        functools.partial(finish_pair_kernel, len(off_parts)), "finish_pair",
+        [struct(2, *chained.shape)] * 2 + [struct(8, BLK, dtype=F32)], operands,
         [SMEM] + [VMEM] * (len(operands) - 1), 8 * chained.size, 16 * chained.size,
     )
 
 
 def relay_pair(
-    is_first, masked, entering, begin, start, stash, gain, up, down, width
+    live_rows, arriving, entering, begin, start, stash, gain, up, down, width, plan, exchange
 ):
-    def pick(first, last):
-        return jnp.where(is_first, first, last)
-
-    flag = pick(jnp.int32(1), jnp.int32(0)).reshape(1)
-    other_flag = 1 - flag
-    chain_in = pick(begin, start)
-    first = jnp.stack([pick(stash[1], stash[0]), chain_in])
-    off_grads, off_rows = pick(start, masked[0]), pick(entering[0], begin)
-    others = jnp.stack([pick(stash[0], stash[1]), off_grads, off_rows])
-    up, down, flag, other_flag, others = lax.optimization_barrier((up, down, flag, other_flag, others))
+    rows = begin.shape[0]
+    is_first = lax.axis_index("section") == 0
+    flag = is_first.astype(jnp.int32).reshape(1)
+    first = first_rows_of(flag, stash, begin, start)
+    row_start = lax.axis_index("dp") * rows
+    up, down, is_first, row_start, plan = lax.optimization_barrier((up, down, is_first, row_start, plan))
 
     with jax.named_scope("gather_first"):
         moved = moved_rows(first)
-    up, down = load_weights(up, down, first)
+    up = load_one(up, [first, plan])
     with jax.named_scope("gather_first"):
-        gathered = halves(later(moved, up))
-    back_halves, chain_halves = [[half[i] for half in gathered] for i in range(2)]
-    back_product = products(back_halves, gain, up, down)
+        back_halves, chain_halves = halves(later(moved, up))
+    back_product = products(back_halves, gain, up, [])
+    down = load_one(down, [back_product])
     with jax.named_scope("swap_back"):
         back_parts = tensor_parts(back_product)
-    entered, _ = enter(flag, later(chain_halves, back_product), chain_halves, gain, up, down)
+    entered, _ = enter(1, flag, later(chain_halves, back_product), chain_halves, gain, up, down)
     with jax.named_scope("swap_chain0"):
         parts = tensor_parts(entered)
+    live = (row_start + lax.iota(jnp.int32, rows) < live_rows[0])[:, None]
+
+    def pick(in_first, in_last):
+        return jnp.where(is_first, in_first, in_last)
+
+    others = jnp.stack([
+        pick(stash[0], stash[1]),
+        pick(start, jnp.where(live, later(arriving, entered)[0], jnp.zeros((), BF16))),
+        pick(later(entering, entered)[0], begin),
+    ])
+    off_grads, off_rows = others[1], others[2]
     with jax.named_scope("gather_others"):
-        gathered = halves(later(moved_rows(later(others, entered)), back_parts[1]))
-    off_halves, off_grad_halves, off_row_halves = [[half[i] for half in gathered] for i in range(3)]
-    off_product = products(off_halves, gain, up, down)
+        off_halves, off_grad_halves, off_row_halves = halves(later(moved_rows(later(others, entered)), back_parts[1]))
+    off_product = products_and_act_grads(off_halves, off_grad_halves, gain, up, down)
     with jax.named_scope("swap_off_back"):
         off_parts = tensor_parts(off_product)
-    off_act = act_grads(later(off_grad_halves, off_product), up, down)
-    with jax.named_scope("swap_off_act"):
-        off_act_parts = tensor_parts(off_act)
-    off_forward = products(later(off_row_halves, off_act), gain, up, down)
+    off_forward = products(later(off_row_halves, off_product), gain, up, [down])
+    with jax.named_scope("swap_off_forward"):
+        off_forward_parts = tensor_parts(off_forward)
 
     with jax.named_scope("chain0"):
         kept, sent, scaled, activated = leave(
-            width, flag, parts, back_parts, back_halves, gain, up, down, [], [off_product, off_act, off_forward]
+            width, 1, flag, parts, back_parts, back_halves, gain, up, down, [], [off_product, off_forward]
         )
-        sums = scatter_parts(scatter_pairs(kept, sent))
-        chained = added(chain_in, later(sums, off_parts[1]))
+        chained = added(first[1], scatter_parts(scatter_pairs(kept, sent)))
+    with jax.named_scope("off_back"):
+        kept, sent, off_scaled, off_activated = joint_backward(width, off_parts, off_halves, gain, up, down, [])
+        off_back_pairs = scatter_pairs(kept, sent)
     with jax.named_scope("pass"):
-        passed = halves([one[0] for one in moved_passed(chained)])
-    chain_in = passed[0][: chained.shape[0]]
-    entered, grads = enter(other_flag, later(passed, off_act_parts[1]), chain_halves, gain, up, down)
+        passed = later(halves(moved_passed(chained))[0], kept)
+    chain_in = passed[0][:rows]
+    entered, grads = enter(0, flag, passed, chain_halves, gain, up, down)
     with jax.named_scope("swap_chain1"):
         parts = tensor_parts(entered)
-    with jax.named_scope("off_back"):
-        kept, sent, off_scaled, off_activated = backward(
-            width, off_parts, off_act_parts, off_halves, gain, up, down, [entered]
-        )
-        off_back_sums = scatter_parts(scatter_pairs(kept, sent))
-    with jax.named_scope("swap_off_forward"):
-        off_forward_parts = tensor_parts(later(off_forward, entered))
+    with jax.named_scope("off_forward"):
+        kept, sent = forward(width, off_forward_parts, up, down, [entered])
+        pairs = jnp.stack([off_back_pairs, scatter_pairs(kept, sent)], axis=1)
+        off_sums = scatter_parts(pairs)
     with jax.named_scope("chain1"):
         kept, sent, scaled, activated = leave(
-            width, other_flag, parts, back_parts, back_halves, gain, up, down, [scaled, activated], []
+            width, 0, flag, parts, back_parts, back_halves, gain, up, down, [scaled, activated], [pairs]
         )
-        chain_sums = scatter_parts(scatter_pairs(kept, sent))
-        off_back = added(off_grads, later(off_back_sums, kept))
-    with jax.named_scope("off_forward"):
-        kept, sent = forward(width, later(off_forward_parts, chain_sums), up, down, [])
-        off_sums = scatter_parts(scatter_pairs(kept, sent))
-    section_outputs, input_grads = finish_pair(flag, chained, off_back, off_rows, off_sums, chain_in, chain_sums)
+        got = sibling(sent)
+        chain_sums = scatter_parts(summed_pairs(kept, got))
+        off_sums = later(off_sums, kept)
     tables = [
         (*back_halves, scaled, activated, grads),
         (*off_halves, off_scaled, off_activated, *off_grad_halves),
     ]
-    return section_outputs, input_grads, tables, off_back
+    relayed, from_others = exchange(later(plan, off_sums), tables, got)
+    section_outputs, input_grads, done = finish_pair(
+        flag, chained, off_grads, off_rows, chain_in, off_sums, chain_sums
+    )
+    return section_outputs, input_grads, plan, relayed, from_others, [done]
 
 
 def relay(
@@ -577,9 +701,9 @@
     up, down = load_weights(up, down, first)
     with jax.named_scope("gather_first"):
         gathered = halves(later(moved, up))
-    stash_rows = [[half[0] for half in gathered]]
-    grad_halves = [half[1] for half in gathered]
-    back_products = [products(stash_rows[0], gain, up, down)]
+    stash_rows = [gathered[0]]
+    grad_halves = gathered[1]
+    back_products = [products(stash_rows[0], gain, up, [down])]
     with jax.named_scope("swap_b0p"):
         back_parts = [tensor_parts(back_products[0])]
     act_grad = act_grads(later(grad_halves, back_products[0]), up, down)
@@ -588,13 +712,13 @@
     with jax.named_scope("gather_others"):
         others = jnp.concatenate([section_inputs, stashed_inputs[0, 1:]])
         gathered = halves(moved_rows(later(others, act_grad)))
-    product = products([half[0] for half in gathered], gain, up, down)
+    product = products(gathered[0], gain, up, [down])
     with jax.named_scope("swap_f0p"):
         parts = tensor_parts(product)
     ahead = [product]
     for turn in range(1, turn_count):
-        stash_rows.append([half[turn] for half in gathered])
-        back_products.append(products(stash_rows[turn], gain, up, down))
+        stash_rows.append(gathered[turn])
+        back_products.append(products(stash_rows[turn], gain, up, [down]))
         ahead.append(back_products[turn])
         with jax.named_scope("swap_b1p"):
             back_parts.append(tensor_parts(back_products[turn]))
@@ -632,12 +756,12 @@
                 jnp.where(is_last, entering[turn], forward_results[-1]),
             )
             passed = halves(later(moved, back_parts[turn + 1][1]))
-        grad_halves = [half[0] for half in passed]
-        grads_in, rows_in = passed[0][0, :local_rows], passed[0][1, :local_rows]
+        grad_halves = passed[0]
+        grads_in, rows_in = passed[0][0][:local_rows], passed[1][0][:local_rows]
         act_grad = act_grads(grad_halves, up, down)
         with jax.named_scope("swap_b1a"):
             act_parts = tensor_parts(act_grad)
-        product = products(later([half[1] for half in passed], act_grad), gain, up, down)
+        product = products(later(passed[1], act_grad), gain, up, [down])
         with jax.named_scope("swap_f1p"):
             parts = tensor_parts(product)
         ahead = []
@@ -669,32 +793,36 @@
     width = channels * lax.axis_size("tensor")
     is_first = section_index == 0
     is_last = section_index == section_count - 1
-    counts, owners = held_count[0, 0], held_owner[0, 0]
+    counts, owners, blocks = held_count[0, 0], held_owner[0, 0], held_blocks[0, 0]
     capacity = owners.shape[1]
     dp_index = lax.axis_index("dp")
-    plan = jnp.concatenate(
-        [jnp.full((dp_count, 1), dp_index, jnp.int32), counts[:, None], owners, held_blocks[0, 0]], axis=1
-    )
-    row_ids = dp_index * local_rows + lax.iota(jnp.int32, local_rows)
-    masked = jnp.where((row_ids < live_rows[:, None])[..., None], arriving, jnp.zeros((), BF16))
+    plan = jnp.concatenate([jnp.full((dp_count, 1), dp_index, jnp.int32), counts[:, None], owners, blocks], axis=1)
+
+    def exchange(plan, tables, before):
+        with jax.named_scope("block_exchange"):
+            outgoing = outgoing_blocks(plan, capacity, norm_gain, tables, channels // BLK, hidden // BLK)
+            outgoing = outgoing.reshape((2, dp_count // 2, BLK, BLK))
+            relayed = later(sibling(outgoing[1]), before)
+            pairs = [jnp.concatenate([outgoing[0, k], relayed[k]]) for k in range(1, dp_count // 2)]
+            return relayed, [shifted(pair, -k - 1) for k, pair in enumerate(pairs)]
 
     if section_count == 2 and turn_count == 2:
-        weights = lax.optimization_barrier((up_weight[0], down_weight[0], plan))
-        section_outputs, input_grads, tables, before = relay_pair(
-            is_first, masked, entering, section_inputs[0], grad_outputs[0], stashed_inputs[0], norm_gain, *weights[:2], width
+        section_outputs, input_grads, plan, relayed, others, after = relay_pair(
+            live_rows, arriving, entering, section_inputs[0], grad_outputs[0], stashed_inputs[0], norm_gain,
+            up_weight[0], down_weight[0], width, plan, exchange,
         )
-        plan = later(weights[2], before)
     else:
+        row_ids = dp_index * local_rows + lax.iota(jnp.int32, local_rows)
+        masked = jnp.where((row_ids < live_rows[:, None])[..., None], arriving, jnp.zeros((), BF16))
         section_outputs, input_grads, tables = relay(
             is_first, is_last, masked, entering, section_inputs, grad_outputs, stashed_inputs, norm_gain,
             up_weight[0], down_weight[0], width,
         )
-    with jax.named_scope("block_exchange"):
-        outgoing = outgoing_blocks(plan, capacity, norm_gain, tables, channels // BLK, hidden // BLK)
-        outgoing = outgoing.reshape((2, dp_count // 2, BLK, BLK))
-        relayed = sibling(outgoing[1])
-        others = [shifted(jnp.stack([outgoing[0, k], relayed[k]]), -k) for k in range(1, dp_count // 2)]
-    first_out, second_out, direction_out = adam(plan, relayed, others, first_moment[0, 0, 0], second_moment[0, 0, 0])
+        relayed, others = exchange(plan, tables, None)
+        after = []
+    first_out, second_out, direction_out = adam(
+        plan, relayed, others, first_moment[0, 0, 0], second_moment[0, 0, 0], after
+    )
     return (
         section_outputs[None],
         input_grads[None],

time: 124 us -> 108 us (0.87)
  waiting for transfers between devices: 47.1 us -> 36.3 us
  starting transfers between devices: 47.6 us -> 42.4 us
  other arithmetic: 2.1 us -> 0.63 us
    ppermute x21 -> x18, starting transfers between devices: 32.5 us -> 26 us  [shifted(): lax.ppermute(value, 'dp', [(d, (d + 2 * steps) % count) for d in range(co...]
    ppermute x6 -> x5, waiting for transfers between devices: 18.9 us -> 12.9 us  [tensor_parts(): got = lax.ppermute(value, 'tensor', [(t, t ^ step) for t in range(count)])]
    pallas_call x3 -> x6, Pallas kernels: 6.94 us -> 10.8 us  [the longest x2 4.65 us: load_one(): pl.pallas_call(load_one_kernel, out_shape=pltpu.VMEM(weight.shape, BF16),...]
    ppermute x8 -> x11, waiting for transfers between devices: 5.95 us -> 2.65 us  [sibling(): lax.ppermute(value, 'dp', [(d, d ^ 1) for d in range(lax.axis_size('dp'))])]
    pallas_call x11 -> x9, Pallas kernels: 15.5 us -> 12.9 us  [call(): pl.pallas_call(kernel, out_shape=outs, in_specs=specs, out_specs=[VMEM] *...]
    ppermute x21 -> x18, waiting for transfers between devices: 18.8 us -> 17.2 us  [shifted(): lax.ppermute(value, 'dp', [(d, (d + 2 * steps) % count) for d in range(co...]
    select_n x2 -> x3, other arithmetic: 1.74 us -> 0.17 us  [pick(): return jnp.where(is_first, in_first, in_last)]
    ppermute x6 -> x5, starting transfers between devices: 5.51 us -> 6.54 us  [tensor_parts(): got = lax.ppermute(value, 'tensor', [(t, t ^ step) for t in range(count)])]
  transfers between devices with their start and end apart: 39 -> 38, of which waited for: 20 -> 19; matrix products, arithmetic and copies ran while one was open for 2% -> 3% of each run, Pallas kernels for 13% -> 18%
where the time goes in v3:
time: 108 us; the launch traced here: 107 us
  starting transfers between devices  42.4 us (39%)
  waiting for transfers between devices  36.3 us (34%)
  Pallas kernels  23.7 us (22%)
  local copies, waits for them, and re-layouts  2.44 us (2%)
  between operations  1.95 us (2%)
    ppermute x18, starting transfers between devices, shifted(): lax.ppermute(value, 'dp', [(d, (d + 2 * steps) % count) for d in range(co...  26 us
    ppermute x18, waiting for transfers between devices, shifted(): lax.ppermute(value, 'dp', [(d, (d + 2 * steps) % count) for d in range(co...  17.2 us
    pallas_call x9, Pallas kernels, call(): pl.pallas_call(kernel, out_shape=outs, in_specs=specs, out_specs=[VMEM] *...  12.9 us
    ppermute x5, waiting for transfers between devices, tensor_parts(): got = lax.ppermute(value, 'tensor', [(t, t ^ step) for t in range(count)])  12.9 us
    ppermute x4, starting transfers between devices, moved(): return lax.ppermute(local, ('section', 'dp'), pairs)  8.15 us
    ppermute x5, starting transfers between devices, tensor_parts(): got = lax.ppermute(value, 'tensor', [(t, t ^ step) for t in range(count)])  6.54 us
    pallas_call x2, Pallas kernels, load_one(): pl.pallas_call(load_one_kernel, out_shape=pltpu.VMEM(weight.shape, BF16),...  4.65 us
    ppermute x4, waiting for transfers between devices, moved(): return lax.ppermute(local, ('section', 'dp'), pairs)  3.6 us
  transfers between devices with their start and end apart: 38, of which 19 were waited for; matrix products, arithmetic and copies ran while one was open for 3% of the time, Pallas kernels for 18%

profile of v3, /device:TPU:0, one launch (start us, length us, event | category | flops | bytes accessed | tf_op | source)
XLA Modules:
  0.0 107.4 jit_solution(1076234124258118187)
XLA Ops:
  0.6 0.8 first_rows.1.refs_0_
  1.5 3.1 %collective-permute-start = (bf16[2,16,1280]{2,1,0:T(8,128)(2,1)S(1)}, bf16[2,16,1280]{2,1,0:T(8,128)(2,1)S(1)}, u32[]{:S(2)}, u32[]{:S(2)}) collective-permute-start(bf16[2,16,1280]{2,1,0:T(8,128)(2,1)S(1)} %first_rows.1.refs_0_), channel_id=1, source_target_pairs={{0,4},{2,6},{4,8},{6,10},{8,12},{10,14},{12,0},{14,2},{1,5},{3,7},... | collective-permute-start | bytes 245768 | tf_op jit(solution)/shard_map/gather_first/ppermute | solution.py:32
  4.5 2.6 %collective-permute-start.1 = (bf16[2,16,1280]{2,1,0:T(8,128)(2,1)S(1)}, bf16[2,16,1280]{2,1,0:T(8,128)(2,1)S(1)}, u32[]{:S(2)}, u32[]{:S(2)}) collective-permute-start(bf16[2,16,1280]{2,1,0:T(8,128)(2,1)S(1)} %first_rows.1.refs_0_), channel_id=1, source_target_pairs={{0,8},{2,10},{4,12},{6,14},{8,0},{10,2},{12,4},{14,6},{1,9},{3,11}... | collective-permute-start | bytes 245768 | tf_op jit(solution)/shard_map/gather_first/ppermute | solution.py:32
  7.1 1.3 %collective-permute-start.2 = (bf16[2,16,1280]{2,1,0:T(8,128)(2,1)S(1)}, bf16[2,16,1280]{2,1,0:T(8,128)(2,1)S(1)}, u32[]{:S(2)}, u32[]{:S(2)}) collective-permute-start(bf16[2,16,1280]{2,1,0:T(8,128)(2,1)S(1)} %first_rows.1.refs_0_), channel_id=1, source_target_pairs={{0,12},{2,14},{4,0},{6,2},{8,4},{10,6},{12,8},{14,10},{1,13},{3,15... | collective-permute-start | bytes 245768 | tf_op jit(solution)/shard_map/gather_first/ppermute | solution.py:32
  8.5 0.8 copy.22
  9.2 0.8 copy.21
  10.8 2.3 %load_weight.2.up._ = bf16[1280,1792]{1,0:T(8,128)(2,1)S(1)} custom-call(bf16[1280,1792]{1,0:T(8,128)(2,1)} %bitcast.115, bf16[2,16,1280]{2,1,0:T(8,128)(2,1)S(1)} %first_rows.1.refs_0_, s32[8,14]{1,0:T(8,128)S(1)} %pad_add_fusion.refs_1_.plan), custom_call_target="tpu_custom_call" | custom-call | tf_op jit(solution)/shard_map/load_weight/pallas_call | solution.py:132
  15.0 0.8 products.2.refs_0_.back_own
  15.8 1.6 %collective-permute-start.6 = (bf16[128,1920]{1,0:T(8,128)(2,1)S(1)}, bf16[128,1920]{1,0:T(8,128)(2,1)S(1)}, u32[]{:S(2)}, u32[]{:S(2)}) collective-permute-start(bf16[128,1920]{1,0:T(8,128)(2,1)S(1)} %products.2.refs_0_.back_own), channel_id=1, source_target_pairs={{0,1},{1,0},{2,3},{3,2},{4,5},{5,4},{6,7},{7,6},{8,9},{9,8},{10,11... | collective-permute-start | bytes 1474568 | tf_op jit(solution)/shard_map/swap_back/ppermute | solution.py:84
  17.3 2.3 %load_weight.3.down.refs_0_._ = bf16[1792,1280]{1,0:T(8,128)(2,1)S(1)} custom-call(bf16[1792,1280]{1,0:T(8,128)(2,1)} %bitcast.116, bf16[128,1920]{1,0:T(8,128)(2,1)S(1)} %products.2.refs_0_.back_own), custom_call_target="tpu_custom_call" | custom-call | tf_op jit(solution)/shard_map/load_weight/pallas_call | solution.py:132
  19.7 1.5 %enter.2 = (bf16[128,1920]{1,0:T(8,128)(2,1)S(1)}, bf16[128,1280]{1,0:T(8,128)(2,1)}) custom-call(s32[1]{0:T(128)} %bitcast.flag, bf16[64,1280]{1,0:T(8,128)(2,1)S(1)} %pad_maximum_fusion.1.low.other_low, bf16[64,1280]{1,0:T(8,128)(2,1)S(1)} %collective-permute-done.3.high.other_high, bf16[64,1280]{1,0:T(8,128)(2,1)S(1)} %pad_maximum_fusion.1.low.other_low, ...), custom_call_target="tpu_custom_call" | custom-call | flops 1 | bytes 1 | tf_op jit(solution)/shard_map/enter/pallas_call | solution.py:96
  21.3 1.7 %collective-permute-start.7 = (bf16[3,16,1280]{2,1,0:T(8,128)(2,1)S(1)}, bf16[3,16,1280]{2,1,0:T(8,128)(2,1)S(1)}, u32[]{:S(2)}, u32[]{:S(2)}) collective-permute-start(bf16[3,16,1280]{2,1,0:T(8,128)(2,1)S(1)} %pad_maximum_fusion.7), channel_id=1, source_target_pairs={{0,4},{2,6},{4,8},{6,10},{8,12},{10,14},{12,0},{14,2},{1,5},{3,7},... | collective-permute-start | bytes 368648 | tf_op jit(solution)/shard_map/gather_others/ppermute | solution.py:32
  23.0 1.9 %collective-permute-start.8 = (bf16[3,16,1280]{2,1,0:T(8,128)(2,1)S(1)}, bf16[3,16,1280]{2,1,0:T(8,128)(2,1)S(1)}, u32[]{:S(2)}, u32[]{:S(2)}) collective-permute-start(bf16[3,16,1280]{2,1,0:T(8,128)(2,1)S(1)} %pad_maximum_fusion.7), channel_id=1, source_target_pairs={{0,8},{2,10},{4,12},{6,14},{8,0},{10,2},{12,4},{14,6},{1,9},{3,11}... | collective-permute-start | bytes 368648 | tf_op jit(solution)/shard_map/gather_others/ppermute | solution.py:32
  26.0 3.5 %collective-permute-done.7 = bf16[3,16,1280]{2,1,0:T(8,128)(2,1)S(1)} collective-permute-done((bf16[3,16,1280]{2,1,0:T(8,128)(2,1)S(1)}, bf16[3,16,1280]{2,1,0:T(8,128)(2,1)S(1)}, u32[]{:S(2)}, u32[]{:S(2)}) %collective-permute-start.7) | collective-permute-done | bytes 122912 | tf_op jit(solution)/shard_map/gather_others/ppermute | solution.py:32
  29.5 4.4 %collective-permute-done.8 = bf16[3,16,1280]{2,1,0:T(8,128)(2,1)S(1)} collective-permute-done((bf16[3,16,1280]{2,1,0:T(8,128)(2,1)S(1)}, bf16[3,16,1280]{2,1,0:T(8,128)(2,1)S(1)}, u32[]{:S(2)}, u32[]{:S(2)}) %collective-permute-start.8) | collective-permute-done | bytes 122912 | tf_op jit(solution)/shard_map/gather_others/ppermute | solution.py:32
  35.6 2.0 %products_and_act_grads.1.refs_0_.own = bf16[128,3712]{1,0:T(8,128)(2,1)S(1)} custom-call(bf16[64,1280]{1,0:T(8,128)(2,1)S(1)} %pad_maximum_fusion.3.low.refs_5_, bf16[64,1280]{1,0:T(8,128)(2,1)S(1)} %collective-permute-done.10.high.refs_6_, bf16[64,1280]{1,0:T(8,128)(2,1)S(1)} %pad_maximum_fusion.4.grad_low.refs_9_, ...), custom_call_target="tpu_custom_call" | custom-call | flops 1 | bytes 1 | tf_op jit(solution)/shard_map/products_and_act_grads/pallas_call | solution.py:96
  37.6 0.8 products.3.refs_1_.own
  38.4 1.4 %collective-permute-done.5.got = bf16[128,1920]{1,0:T(8,128)(2,1)S(1)} collective-permute-done((bf16[128,1920]{1,0:T(8,128)(2,1)S(1)}, bf16[128,1920]{1,0:T(8,128)(2,1)S(1)}, u32[]{:S(2)}, u32[]{:S(2)}) %collective-permute-start.5) | collective-permute-done | bytes 491552 | tf_op jit(solution)/shard_map/swap_chain0/ppermute | solution.py:84
  39.8 1.1 leave.2
  41.0 1.6 %collective-permute-start.22 = (bf16[128,3712]{1,0:T(8,128)(2,1)S(1)}, bf16[128,3712]{1,0:T(8,128)(2,1)S(1)}, u32[]{:S(2)}, u32[]{:S(2)}) collective-permute-start(bf16[128,3712]{1,0:T(8,128)(2,1)S(1)} %products_and_act_grads.1.refs_0_.own), channel_id=1, source_target_pairs={{0,1},{1,0},{2,3},{3,2},{4,5},{5,4},{6,7},{7,6},{8,9},{9,8},{10,11... | collective-permute-start | bytes 2850824 | tf_op jit(solution)/shard_map/swap_off_back/ppermute | solution.py:84
  42.6 1.7 %collective-permute-start.16 = (bf16[16,1280]{1,0:T(8,128)(2,1)S(1)}, bf16[16,1280]{1,0:T(8,128)(2,1)S(1)}, u32[]{:S(2)}, u32[]{:S(2)}) collective-permute-start(bf16[16,1280]{1,0:T(8,128)(2,1)S(1)} %get-tuple-element.121), channel_id=1, source_target_pairs={{0,4},{2,6},{4,8},{6,10},{8,12},{10,14},{12,0},{14,2},{1,5},{3,7},... | collective-permute-start | bytes 122888 | tf_op jit(solution)/shard_map/chain0/ppermute | solution.py:32
  44.3 1.9 %collective-permute-start.15 = (bf16[16,1280]{1,0:T(8,128)(2,1)S(1)}, bf16[16,1280]{1,0:T(8,128)(2,1)S(1)}, u32[]{:S(2)}, u32[]{:S(2)}) collective-permute-start(bf16[16,1280]{1,0:T(8,128)(2,1)S(1)} %get-tuple-element.122), channel_id=1, source_target_pairs={{0,8},{2,10},{4,12},{6,14},{8,0},{10,2},{12,4},{14,6},{1,9},{3,11}... | collective-permute-start | bytes 122888 | tf_op jit(solution)/shard_map/chain0/ppermute | solution.py:32
  46.7 1.3 %collective-permute-start.24 = (bf16[128,1920]{1,0:T(8,128)(2,1)S(1)}, bf16[128,1920]{1,0:T(8,128)(2,1)S(1)}, u32[]{:S(2)}, u32[]{:S(2)}) collective-permute-start(bf16[128,1920]{1,0:T(8,128)(2,1)S(1)} %products.3.refs_1_.own), channel_id=1, source_target_pairs={{0,1},{1,0},{2,3},{3,2},{4,5},{5,4},{6,7},{7,6},{8,9},{9,8},{10,11... | collective-permute-start | bytes 1474568 | tf_op jit(solution)/shard_map/swap_off_forward/ppermute | solution.py:84
  48.6 1.3 %collective-permute-done.15 = bf16[16,1280]{1,0:T(8,128)(2,1)S(1)} collective-permute-done((bf16[16,1280]{1,0:T(8,128)(2,1)S(1)}, bf16[16,1280]{1,0:T(8,128)(2,1)S(1)}, u32[]{:S(2)}, u32[]{:S(2)}) %collective-permute-start.15) | collective-permute-done | bytes 40992 | tf_op jit(solution)/shard_map/chain0/ppermute | solution.py:32
  50.3 5.1 %collective-permute-start.20 = (bf16[1,16,1280]{2,1,0:T(8,128)(2,1)S(1)}, bf16[1,16,1280]{2,1,0:T(8,128)(2,1)S(1)}, u32[]{:S(2)}, u32[]{:S(2)}) collective-permute-start(bf16[1,16,1280]{2,1,0:T(8,128)(2,1)S(1)} %bitcast.105), channel_id=1, source_target_pairs={{0,28},{2,30},{4,16},{6,18},{8,20},{10,22},{12,24},{14,26},{16,12}... | collective-permute-start | bytes 122888 | tf_op jit(solution)/shard_map/pass/ppermute | solution.py:50
  55.4 1.6 %collective-permute-start.18 = (bf16[1,16,1280]{2,1,0:T(8,128)(2,1)S(1)}, bf16[1,16,1280]{2,1,0:T(8,128)(2,1)S(1)}, u32[]{:S(2)}, u32[]{:S(2)}) collective-permute-start(bf16[1,16,1280]{2,1,0:T(8,128)(2,1)S(1)} %bitcast.107), channel_id=1, source_target_pairs={{0,20},{2,22},{4,24},{6,26},{8,28},{10,30},{12,16},{14,18},{16,4},... | collective-permute-start | bytes 122888 | tf_op jit(solution)/shard_map/pass/ppermute | solution.py:50
  57.0 1.5 %collective-permute-start.17 = (bf16[1,16,1280]{2,1,0:T(8,128)(2,1)S(1)}, bf16[1,16,1280]{2,1,0:T(8,128)(2,1)S(1)}, u32[]{:S(2)}, u32[]{:S(2)}) collective-permute-start(bf16[1,16,1280]{2,1,0:T(8,128)(2,1)S(1)} %bitcast.108), channel_id=1, source_target_pairs={{0,16},{2,18},{4,20},{6,22},{8,24},{10,26},{12,28},{14,30},{16,0},... | collective-permute-start | bytes 122888 | tf_op jit(solution)/shard_map/pass/ppermute | solution.py:50
  58.5 2.7 %collective-permute-done.19 = bf16[1,16,1280]{2,1,0:T(8,128)(2,1)S(1)} collective-permute-done((bf16[1,16,1280]{2,1,0:T(8,128)(2,1)S(1)}, bf16[1,16,1280]{2,1,0:T(8,128)(2,1)S(1)}, u32[]{:S(2)}, u32[]{:S(2)}) %collective-permute-start.19) | collective-permute-done | bytes 40992 | tf_op jit(solution)/shard_map/pass/ppermute | solution.py:50
  61.3 0.8 collective-permute-done.18
  62.2 2.7 %collective-permute-done.22.got = bf16[128,3712]{1,0:T(8,128)(2,1)S(1)} collective-permute-done((bf16[128,3712]{1,0:T(8,128)(2,1)S(1)}, bf16[128,3712]{1,0:T(8,128)(2,1)S(1)}, u32[]{:S(2)}, u32[]{:S(2)}) %collective-permute-start.22) | collective-permute-done | bytes 950304 | tf_op jit(solution)/shard_map/swap_off_back/ppermute | solution.py:84
  64.9 2.2 %backward.1 = (f32[64,1280]{1,0:T(8,128)S(1)}, bf16[64,1280]{1,0:T(8,128)(2,1)S(1)}, bf16[128,1792]{1,0:T(8,128)(2,1)S(1)}, bf16[128,1792]{1,0:T(8,128)(2,1)S(1)}) custom-call(bf16[128,3712]{1,0:T(8,128)(2,1)S(1)} %products_and_act_grads.1.refs_0_.own, bf16[128,3712]{1,0:T(8,128)(2,1)S(1)} %collective-permute-done.22.got, ...), custom_call_target="tpu_custom_call" | custom-call | flops 1 | bytes 1 | tf_op jit(solution)/shard_map/off_back/backward/pallas_call | solution.py:96
  67.2 1.8 %enter.3 = (bf16[128,1920]{1,0:T(8,128)(2,1)S(1)}, bf16[128,1280]{1,0:T(8,128)(2,1)S(1)}) custom-call(s32[1]{0:T(128)} %bitcast.flag, bf16[64,1280]{1,0:T(8,128)(2,1)S(1)} %pad_maximum_fusion.6.low, bf16[64,1280]{1,0:T(8,128)(2,1)S(1)} %collective-permute-done.21.high, bf16[64,1280]{1,0:T(8,128)(2,1)S(1)} %pad_maximum_fusion.1.low.other_low, ...), custom_call_target="tpu_custom_call" | custom-call | flops 1 | bytes 1 | tf_op jit(solution)/shard_map/enter/pallas_call | solution.py:96
  68.9 1.6 %collective-permute-start.29 = (bf16[128,1920]{1,0:T(8,128)(2,1)S(1)}, bf16[128,1920]{1,0:T(8,128)(2,1)S(1)}, u32[]{:S(2)}, u32[]{:S(2)}) collective-permute-start(bf16[128,1920]{1,0:T(8,128)(2,1)S(1)} %get-tuple-element.83.refs_0_.own), channel_id=1, source_target_pairs={{0,1},{1,0},{2,3},{3,2},{4,5},{5,4},{6,7},{7,6},{8,9},{9,8},{10,11... | collective-permute-start | bytes 1474568 | tf_op jit(solution)/shard_map/swap_chain1/ppermute | solution.py:84
  70.5 4.9 %collective-permute-done.24.got = bf16[128,1920]{1,0:T(8,128)(2,1)S(1)} collective-permute-done((bf16[128,1920]{1,0:T(8,128)(2,1)S(1)}, bf16[128,1920]{1,0:T(8,128)(2,1)S(1)}, u32[]{:S(2)}, u32[]{:S(2)}) %collective-permute-start.24) | collective-permute-done | bytes 491552 | tf_op jit(solution)/shard_map/swap_off_forward/ppermute | solution.py:84
  75.4 1.0 forward.1
  76.6 1.3 %collective-permute-done.25 = bf16[64,1280]{1,0:T(8,128)(2,1)S(1)} collective-permute-done((bf16[64,1280]{1,0:T(8,128)(2,1)S(1)}, bf16[64,1280]{1,0:T(8,128)(2,1)S(1)}, u32[]{:S(2)}, u32[]{:S(2)}) %collective-permute-start.25) | collective-permute-done | bytes 163872 | tf_op jit(solution)/shard_map/off_forward/ppermute | solution.py:27
  78.1 3.0 %collective-permute-start.26 = (bf16[2,16,1280]{2,1,0:T(8,128)(2,1)S(1)}, bf16[2,16,1280]{2,1,0:T(8,128)(2,1)S(1)}, u32[]{:S(2)}, u32[]{:S(2)}) collective-permute-start(bf16[2,16,1280]{2,1,0:T(8,128)(2,1)S(1)} %get-tuple-element.113), channel_id=1, source_target_pairs={{0,12},{2,14},{4,0},{6,2},{8,4},{10,6},{12,8},{14,10},{1,13},{3,15... | collective-permute-start | bytes 245768 | tf_op jit(solution)/shard_map/off_forward/ppermute | solution.py:32
  81.7 3.8 %collective-permute-done.29.got = bf16[128,1920]{1,0:T(8,128)(2,1)S(1)} collective-permute-done((bf16[128,1920]{1,0:T(8,128)(2,1)S(1)}, bf16[128,1920]{1,0:T(8,128)(2,1)S(1)}, u32[]{:S(2)}, u32[]{:S(2)}) %collective-permute-start.29) | collective-permute-done | bytes 491552 | tf_op jit(solution)/shard_map/swap_chain1/ppermute | solution.py:84
  85.5 2.1 %leave.3 = (f32[64,1280]{1,0:T(8,128)S(1)}, bf16[64,1280]{1,0:T(8,128)(2,1)S(1)}, bf16[128,1792]{1,0:T(8,128)(2,1)S(1)}, bf16[128,1792]{1,0:T(8,128)(2,1)S(1)}) custom-call(s32[1]{0:T(128)} %bitcast.flag, bf16[128,1920]{1,0:T(8,128)(2,1)S(1)} %get-tuple-element.83.refs_0_.own, ...), custom_call_target="tpu_custom_call", output_to_operand_aliasing={{2}: (10, {}), {3}: (11, {})} | custom-call | flops 1 | bytes 1 | tf_op jit(solution)/shard_map/chain1/leave/pallas_call | solution.py:404
  87.7 1.6 %collective-permute-done.27.refs_2_ = bf16[2,16,1280]{2,1,0:T(8,128)(2,1)S(1)} collective-permute-done((bf16[2,16,1280]{2,1,0:T(8,128)(2,1)S(1)}, bf16[2,16,1280]{2,1,0:T(8,128)(2,1)S(1)}, u32[]{:S(2)}, u32[]{:S(2)}) %collective-permute-start.27) | collective-permute-done | bytes 81952 | tf_op jit(solution)/shard_map/off_forward/ppermute | solution.py:32
  89.3 2.1 %block_grads.1 = bf16[8,128,128]{2,1,0:T(8,128)(2,1)S(1)} custom-call(s32[8,14]{1,0:T(8,128)S(1)} %pad_add_fusion.refs_1_.plan, bf16[1,1280]{1,0:T(2,128)(2,1)S(1)} %copy-done, bf16[64,1280]{1,0:T(8,128)(2,1)S(1)} %pad_maximum_fusion.2.low.refs_0_, bf16[64,1280]{1,0:T(8,128)(2,1)S(1)} %collective-permute-done.4.high.refs_1_, ...), custom_call_target="tpu_custom_call" | custom-call | flops 1 | bytes 1 | tf_op jit(solution)/shard_map/block_exchange/block_grads/pallas_call | solution.py:96
  91.7 2.0 %collective-permute-start.31 = (bf16[16,1280]{1,0:T(8,128)(2,1)S(1)}, bf16[16,1280]{1,0:T(8,128)(2,1)S(1)}, u32[]{:S(2)}, u32[]{:S(2)}) collective-permute-start(bf16[16,1280]{1,0:T(8,128)(2,1)S(1)} %get-tuple-element.119), channel_id=1, source_target_pairs={{0,12},{2,14},{4,0},{6,2},{8,4},{10,6},{12,8},{14,10},{1,13},{3,15... | collective-permute-start | bytes 122888 | tf_op jit(solution)/shard_map/chain1/ppermute | solution.py:32
  93.8 1.9 %collective-permute-start.33 = (bf16[16,1280]{1,0:T(8,128)(2,1)S(1)}, bf16[16,1280]{1,0:T(8,128)(2,1)S(1)}, u32[]{:S(2)}, u32[]{:S(2)}) collective-permute-start(bf16[16,1280]{1,0:T(8,128)(2,1)S(1)} %get-tuple-element.117), channel_id=1, source_target_pairs={{0,4},{2,6},{4,8},{6,10},{8,12},{10,14},{12,0},{14,2},{1,5},{3,7},... | collective-permute-start | bytes 122888 | tf_op jit(solution)/shard_map/chain1/ppermute | solution.py:32
  95.8 1.9 %collective-permute-start.35 = (bf16[256,128]{1,0:T(8,128)(2,1)S(1)}, bf16[256,128]{1,0:T(8,128)(2,1)S(1)}, u32[]{:S(2)}, u32[]{:S(2)}) collective-permute-start(bf16[256,128]{1,0:T(8,128)(2,1)S(1)} %pad_maximum_fusion.8), channel_id=1, source_target_pairs={{0,12},{2,14},{4,0},{6,2},{8,4},{10,6},{12,8},{14,10},{1,13},{3,15... | collective-permute-start | bytes 196616 | tf_op jit(solution)/shard_map/block_exchange/ppermute | solution.py:32
  97.7 1.0 collective-permute-start.36
  98.9 1.2 %collective-permute-done.32.refs_6_ = bf16[16,1280]{1,0:T(8,128)(2,1)S(1)} collective-permute-done((bf16[16,1280]{1,0:T(8,128)(2,1)S(1)}, bf16[16,1280]{1,0:T(8,128)(2,1)S(1)}, u32[]{:S(2)}, u32[]{:S(2)}) %collective-permute-start.32) | collective-permute-done | bytes 40992 | tf_op jit(solution)/shard_map/chain1/ppermute | solution.py:32
  100.9 4.2 %collective-permute-done.36.refs_1_ = bf16[256,128]{1,0:T(8,128)(2,1)S(1)} collective-permute-done((bf16[256,128]{1,0:T(8,128)(2,1)S(1)}, bf16[256,128]{1,0:T(8,128)(2,1)S(1)}, u32[]{:S(2)}, u32[]{:S(2)}) %collective-permute-start.36) | collective-permute-done | bytes 65568 | tf_op jit(solution)/shard_map/block_exchange/ppermute | solution.py:32
  105.1 2.1 %adam_step.1 = (f32[6,128,128]{2,1,0:T(8,128)}, f32[6,128,128]{2,1,0:T(8,128)}, f32[6,128,128]{2,1,0:T(8,128)}) custom-call(s32[8,14]{1,0:T(8,128)S(1)} %pad_add_fusion.refs_1_.plan, bf16[4,128,128]{2,1,0:T(8,128)(2,1)S(1)} %collective-permute-done.34.relayed, bf16[256,128]{1,0:T(8,128)(2,1)S(1)} %collective-permute-done.35.refs_0_, ...), custom_call_target="tpu_custom_call" | custom-call | tf_op jit(solution)/shard_map/adam_step/pallas_call | solution.py:546
  (102 shorter events, 9.0 us)
Async XLA Ops:
  1.5 11.7 %collective-permute-start = (bf16[2,16,1280]{2,1,0:T(8,128)(2,1)S(1)}, bf16[2,16,1280]{2,1,0:T(8,128)(2,1)S(1)}, u32[]{:S(2)}, u32[]{:S(2)}) collective-permute-start(bf16[2,16,1280]{2,1,0:T(8,128)(2,1)S(1)} %first_rows.1.refs_0_), channel_id=1, source_target_pairs={{0,4},{2,6},{4,8},{6,10},{8,12},{10,14},{12,0},{14,2},{1,5},{3,7},... | collective-permute-start | bytes 245768 | tf_op jit(solution)/shard_map/gather_first/ppermute | solution.py:32
  4.5 8.6 %collective-permute-start.1 = (bf16[2,16,1280]{2,1,0:T(8,128)(2,1)S(1)}, bf16[2,16,1280]{2,1,0:T(8,128)(2,1)S(1)}, u32[]{:S(2)}, u32[]{:S(2)}) collective-permute-start(bf16[2,16,1280]{2,1,0:T(8,128)(2,1)S(1)} %first_rows.1.refs_0_), channel_id=1, source_target_pairs={{0,8},{2,10},{4,12},{6,14},{8,0},{10,2},{12,4},{14,6},{1,9},{3,11}... | collective-permute-start | bytes 245768 | tf_op jit(solution)/shard_map/gather_first/ppermute | solution.py:32
  7.1 6.1 %collective-permute-start.2 = (bf16[2,16,1280]{2,1,0:T(8,128)(2,1)S(1)}, bf16[2,16,1280]{2,1,0:T(8,128)(2,1)S(1)}, u32[]{:S(2)}, u32[]{:S(2)}) collective-permute-start(bf16[2,16,1280]{2,1,0:T(8,128)(2,1)S(1)} %first_rows.1.refs_0_), channel_id=1, source_target_pairs={{0,12},{2,14},{4,0},{6,2},{8,4},{10,6},{12,8},{14,10},{1,13},{3,15... | collective-permute-start | bytes 245768 | tf_op jit(solution)/shard_map/gather_first/ppermute | solution.py:32
  10.8 3.1 %copy-start.5 = (bf16[1,2,16,1280]{3,2,1,0:T(8,128)(2,1)S(1)}, bf16[1,2,16,1280]{3,2,1,0:T(8,128)(2,1)}, u32[]{:S(2)}) copy-start(bf16[1,2,16,1280]{3,2,1,0:T(8,128)(2,1)} %param.19) | copy-start | bytes 245764
  10.8 4.2 %copy-start = (bf16[1,1280]{1,0:T(2,128)(2,1)S(1)}, bf16[1,1280]{1,0:T(2,128)(2,1)}, u32[]{:S(2)}) copy-start(bf16[1,1280]{1,0:T(2,128)(2,1)} %gain.17) | copy-start | bytes 7684
  13.3 4.1 %collective-permute-start.3 = (bf16[64,1280]{1,0:T(8,128)(2,1)S(1)}, bf16[64,1280]{1,0:T(8,128)(2,1)S(1)}, u32[]{:S(2)}, u32[]{:S(2)}) collective-permute-start(bf16[64,1280]{1,0:T(8,128)(2,1)S(1)} %pad_maximum_fusion.1.low.other_low), channel_id=1, source_target_pairs={{0,2},{2,0},{4,6},{6,4},{8,10},{10,8},{12,14},{14,12},{1,3},{3,1},... | collective-permute-start | bytes 491528 | tf_op jit(solution)/shard_map/gather_first/ppermute | solution.py:27
  13.4 1.6 %collective-permute-start.4 = (bf16[64,1280]{1,0:T(8,128)(2,1)S(1)}, bf16[64,1280]{1,0:T(8,128)(2,1)S(1)}, u32[]{:S(2)}, u32[]{:S(2)}) collective-permute-start(bf16[64,1280]{1,0:T(8,128)(2,1)S(1)} %pad_maximum_fusion.2.low.refs_0_), channel_id=1, source_target_pairs={{0,2},{2,0},{4,6},{6,4},{8,10},{10,8},{12,14},{14,12},{1,3},{3,1},... | collective-permute-start | bytes 491528 | tf_op jit(solution)/shard_map/gather_first/ppermute | solution.py:27
  15.8 18.1 %collective-permute-start.6 = (bf16[128,1920]{1,0:T(8,128)(2,1)S(1)}, bf16[128,1920]{1,0:T(8,128)(2,1)S(1)}, u32[]{:S(2)}, u32[]{:S(2)}) collective-permute-start(bf16[128,1920]{1,0:T(8,128)(2,1)S(1)} %products.2.refs_0_.back_own), channel_id=1, source_target_pairs={{0,1},{1,0},{2,3},{3,2},{4,5},{5,4},{6,7},{7,6},{8,9},{9,8},{10,11... | collective-permute-start | bytes 1474568 | tf_op jit(solution)/shard_map/swap_back/ppermute | solution.py:84
  19.7 1.6 %copy-start.3 = (bf16[1,16,1280]{2,1,0:T(8,128)(2,1)S(1)}, bf16[1,16,1280]{2,1,0:T(8,128)(2,1)}, u32[]{:S(2)}) copy-start(bf16[1,16,1280]{2,1,0:T(8,128)(2,1)} %param.14) | copy-start | bytes 122884
  19.7 1.6 %copy-start.4 = (bf16[1,16,1280]{2,1,0:T(8,128)(2,1)S(1)}, bf16[1,16,1280]{2,1,0:T(8,128)(2,1)}, u32[]{:S(2)}) copy-start(bf16[1,16,1280]{2,1,0:T(8,128)(2,1)} %param.16) | copy-start | bytes 122884
  19.7 1.6 %copy-start.6 = (bf16[1,16,1280]{2,1,0:T(8,128)(2,1)S(1)}, bf16[1,16,1280]{2,1,0:T(8,128)(2,1)}, u32[]{:S(2)}) copy-start(bf16[1,16,1280]{2,1,0:T(8,128)(2,1)} %param.17) | copy-start | bytes 122884
  19.7 1.5 %copy-start.7 = (bf16[1,16,1280]{2,1,0:T(8,128)(2,1)S(1)}, bf16[1,16,1280]{2,1,0:T(8,128)(2,1)}, u32[]{:S(2)}) copy-start(bf16[1,16,1280]{2,1,0:T(8,128)(2,1)} %param.15) | copy-start | bytes 122884
  21.3 8.1 %collective-permute-start.7 = (bf16[3,16,1280]{2,1,0:T(8,128)(2,1)S(1)}, bf16[3,16,1280]{2,1,0:T(8,128)(2,1)S(1)}, u32[]{:S(2)}, u32[]{:S(2)}) collective-permute-start(bf16[3,16,1280]{2,1,0:T(8,128)(2,1)S(1)} %pad_maximum_fusion.7), channel_id=1, source_target_pairs={{0,4},{2,6},{4,8},{6,10},{8,12},{10,14},{12,0},{14,2},{1,5},{3,7},... | collective-permute-start | bytes 368648 | tf_op jit(solution)/shard_map/gather_others/ppermute | solution.py:32
  23.0 10.8 %collective-permute-start.8 = (bf16[3,16,1280]{2,1,0:T(8,128)(2,1)S(1)}, bf16[3,16,1280]{2,1,0:T(8,128)(2,1)S(1)}, u32[]{:S(2)}, u32[]{:S(2)}) collective-permute-start(bf16[3,16,1280]{2,1,0:T(8,128)(2,1)S(1)} %pad_maximum_fusion.7), channel_id=1, source_target_pairs={{0,8},{2,10},{4,12},{6,14},{8,0},{10,2},{12,4},{14,6},{1,9},{3,11}... | collective-permute-start | bytes 368648 | tf_op jit(solution)/shard_map/gather_others/ppermute | solution.py:32
  24.9 9.0 %collective-permute-start.9 = (bf16[3,16,1280]{2,1,0:T(8,128)(2,1)S(1)}, bf16[3,16,1280]{2,1,0:T(8,128)(2,1)S(1)}, u32[]{:S(2)}, u32[]{:S(2)}) collective-permute-start(bf16[3,16,1280]{2,1,0:T(8,128)(2,1)S(1)} %pad_maximum_fusion.7), channel_id=1, source_target_pairs={{0,12},{2,14},{4,0},{6,2},{8,4},{10,6},{12,8},{14,10},{1,13},{3,15... | collective-permute-start | bytes 368648 | tf_op jit(solution)/shard_map/gather_others/ppermute | solution.py:32
  25.5 14.4 %collective-permute-start.5 = (bf16[128,1920]{1,0:T(8,128)(2,1)S(1)}, bf16[128,1920]{1,0:T(8,128)(2,1)S(1)}, u32[]{:S(2)}, u32[]{:S(2)}) collective-permute-start(bf16[128,1920]{1,0:T(8,128)(2,1)S(1)} %get-tuple-element.65.own), channel_id=1, source_target_pairs={{0,1},{1,0},{2,3},{3,2},{4,5},{5,4},{6,7},{7,6},{8,9},{9,8},{10,11... | collective-permute-start | bytes 1474568 | tf_op jit(solution)/shard_map/swap_chain0/ppermute | solution.py:84
  33.9 1.5 %collective-permute-start.10 = (bf16[64,1280]{1,0:T(8,128)(2,1)S(1)}, bf16[64,1280]{1,0:T(8,128)(2,1)S(1)}, u32[]{:S(2)}, u32[]{:S(2)}) collective-permute-start(bf16[64,1280]{1,0:T(8,128)(2,1)S(1)} %pad_maximum_fusion.3.low.refs_5_), channel_id=1, source_target_pairs={{0,2},{2,0},{4,6},{6,4},{8,10},{10,8},{12,14},{14,12},{1,3},{3,1},... | collective-permute-start | bytes 491528 | tf_op jit(solution)/shard_map/gather_others/ppermute | solution.py:27
  34.0 1.6 %collective-permute-start.11 = (bf16[64,1280]{1,0:T(8,128)(2,1)S(1)}, bf16[64,1280]{1,0:T(8,128)(2,1)S(1)}, u32[]{:S(2)}, u32[]{:S(2)}) collective-permute-start(bf16[64,1280]{1,0:T(8,128)(2,1)S(1)} %pad_maximum_fusion.4.grad_low.refs_9_), channel_id=1, source_target_pairs={{0,2},{2,0},{4,6},{6,4},{8,10},{10,8},{12,14},{14,12},{1,3},{3,1},... | collective-permute-start | bytes 491528 | tf_op jit(solution)/shard_map/gather_others/ppermute | solution.py:27
  34.6 3.0 %collective-permute-start.12 = (bf16[64,1280]{1,0:T(8,128)(2,1)S(1)}, bf16[64,1280]{1,0:T(8,128)(2,1)S(1)}, u32[]{:S(2)}, u32[]{:S(2)}) collective-permute-start(bf16[64,1280]{1,0:T(8,128)(2,1)S(1)} %pad_maximum_fusion.5.low), channel_id=1, source_target_pairs={{0,2},{2,0},{4,6},{6,4},{8,10},{10,8},{12,14},{14,12},{1,3},{3,1},... | collective-permute-start | bytes 491528 | tf_op jit(solution)/shard_map/gather_others/ppermute | solution.py:27
  40.9 1.6 %collective-permute-start.13 = (bf16[64,1280]{1,0:T(8,128)(2,1)S(1)}, bf16[64,1280]{1,0:T(8,128)(2,1)S(1)}, u32[]{:S(2)}, u32[]{:S(2)}) collective-permute-start(bf16[64,1280]{1,0:T(8,128)(2,1)S(1)} %get-tuple-element.78), channel_id=1, source_target_pairs={{0,2},{2,0},{4,6},{6,4},{8,10},{10,8},{12,14},{14,12},{1,3},{3,1},... | collective-permute-start | bytes 491528 | tf_op jit(solution)/shard_map/chain0/ppermute | solution.py:27
  41.0 23.9 %collective-permute-start.22 = (bf16[128,3712]{1,0:T(8,128)(2,1)S(1)}, bf16[128,3712]{1,0:T(8,128)(2,1)S(1)}, u32[]{:S(2)}, u32[]{:S(2)}) collective-permute-start(bf16[128,3712]{1,0:T(8,128)(2,1)S(1)} %products_and_act_grads.1.refs_0_.own), channel_id=1, source_target_pairs={{0,1},{1,0},{2,3},{3,2},{4,5},{5,4},{6,7},{7,6},{8,9},{9,8},{10,11... | collective-permute-start | bytes 2850824 | tf_op jit(solution)/shard_map/swap_off_back/ppermute | solution.py:84
  42.6 6.0 %collective-permute-start.16 = (bf16[16,1280]{1,0:T(8,128)(2,1)S(1)}, bf16[16,1280]{1,0:T(8,128)(2,1)S(1)}, u32[]{:S(2)}, u32[]{:S(2)}) collective-permute-start(bf16[16,1280]{1,0:T(8,128)(2,1)S(1)} %get-tuple-element.121), channel_id=1, source_target_pairs={{0,4},{2,6},{4,8},{6,10},{8,12},{10,14},{12,0},{14,2},{1,5},{3,7},... | collective-permute-start | bytes 122888 | tf_op jit(solution)/shard_map/chain0/ppermute | solution.py:32
  44.3 5.7 %collective-permute-start.15 = (bf16[16,1280]{1,0:T(8,128)(2,1)S(1)}, bf16[16,1280]{1,0:T(8,128)(2,1)S(1)}, u32[]{:S(2)}, u32[]{:S(2)}) collective-permute-start(bf16[16,1280]{1,0:T(8,128)(2,1)S(1)} %get-tuple-element.122), channel_id=1, source_target_pairs={{0,8},{2,10},{4,12},{6,14},{8,0},{10,2},{12,4},{14,6},{1,9},{3,11}... | collective-permute-start | bytes 122888 | tf_op jit(solution)/shard_map/chain0/ppermute | solution.py:32
  46.1 4.1 %collective-permute-start.14 = (bf16[16,1280]{1,0:T(8,128)(2,1)S(1)}, bf16[16,1280]{1,0:T(8,128)(2,1)S(1)}, u32[]{:S(2)}, u32[]{:S(2)}) collective-permute-start(bf16[16,1280]{1,0:T(8,128)(2,1)S(1)} %get-tuple-element.120), channel_id=1, source_target_pairs={{0,12},{2,14},{4,0},{6,2},{8,4},{10,6},{12,8},{14,10},{1,13},{3,15... | collective-permute-start | bytes 122888 | tf_op jit(solution)/shard_map/chain0/ppermute | solution.py:32
  46.7 28.7 %collective-permute-start.24 = (bf16[128,1920]{1,0:T(8,128)(2,1)S(1)}, bf16[128,1920]{1,0:T(8,128)(2,1)S(1)}, u32[]{:S(2)}, u32[]{:S(2)}) collective-permute-start(bf16[128,1920]{1,0:T(8,128)(2,1)S(1)} %products.3.refs_1_.own), channel_id=1, source_target_pairs={{0,1},{1,0},{2,3},{3,2},{4,5},{5,4},{6,7},{7,6},{8,9},{9,8},{10,11... | collective-permute-start | bytes 1474568 | tf_op jit(solution)/shard_map/swap_off_forward/ppermute | solution.py:84
  50.3 6.7 %collective-permute-start.20 = (bf16[1,16,1280]{2,1,0:T(8,128)(2,1)S(1)}, bf16[1,16,1280]{2,1,0:T(8,128)(2,1)S(1)}, u32[]{:S(2)}, u32[]{:S(2)}) collective-permute-start(bf16[1,16,1280]{2,1,0:T(8,128)(2,1)S(1)} %bitcast.105), channel_id=1, source_target_pairs={{0,28},{2,30},{4,16},{6,18},{8,20},{10,22},{12,24},{14,26},{16,12}... | collective-permute-start | bytes 122888 | tf_op jit(solution)/shard_map/pass/ppermute | solution.py:50
  55.4 5.9 %collective-permute-start.19 = (bf16[1,16,1280]{2,1,0:T(8,128)(2,1)S(1)}, bf16[1,16,1280]{2,1,0:T(8,128)(2,1)S(1)}, u32[]{:S(2)}, u32[]{:S(2)}) collective-permute-start(bf16[1,16,1280]{2,1,0:T(8,128)(2,1)S(1)} %bitcast.106), channel_id=1, source_target_pairs={{0,24},{2,26},{4,28},{6,30},{8,16},{10,18},{12,20},{14,22},{16,8},... | collective-permute-start | bytes 122888 | tf_op jit(solution)/shard_map/pass/ppermute | solution.py:50
  55.4 6.7 %collective-permute-start.18 = (bf16[1,16,1280]{2,1,0:T(8,128)(2,1)S(1)}, bf16[1,16,1280]{2,1,0:T(8,128)(2,1)S(1)}, u32[]{:S(2)}, u32[]{:S(2)}) collective-permute-start(bf16[1,16,1280]{2,1,0:T(8,128)(2,1)S(1)} %bitcast.107), channel_id=1, source_target_pairs={{0,20},{2,22},{4,24},{6,26},{8,28},{10,30},{12,16},{14,18},{16,4},... | collective-permute-start | bytes 122888 | tf_op jit(solution)/shard_map/pass/ppermute | solution.py:50
  57.0 5.0 %collective-permute-start.17 = (bf16[1,16,1280]{2,1,0:T(8,128)(2,1)S(1)}, bf16[1,16,1280]{2,1,0:T(8,128)(2,1)S(1)}, u32[]{:S(2)}, u32[]{:S(2)}) collective-permute-start(bf16[1,16,1280]{2,1,0:T(8,128)(2,1)S(1)} %bitcast.108), channel_id=1, source_target_pairs={{0,16},{2,18},{4,20},{6,22},{8,24},{10,26},{12,28},{14,30},{16,0},... | collective-permute-start | bytes 122888 | tf_op jit(solution)/shard_map/pass/ppermute | solution.py:50
  62.1 5.1 %collective-permute-start.21 = (bf16[64,1280]{1,0:T(8,128)(2,1)S(1)}, bf16[64,1280]{1,0:T(8,128)(2,1)S(1)}, u32[]{:S(2)}, u32[]{:S(2)}) collective-permute-start(bf16[64,1280]{1,0:T(8,128)(2,1)S(1)} %pad_maximum_fusion.6.low), channel_id=1, source_target_pairs={{0,2},{2,0},{4,6},{6,4},{8,10},{10,8},{12,14},{14,12},{1,3},{3,1},... | collective-permute-start | bytes 491528 | tf_op jit(solution)/shard_map/pass/ppermute | solution.py:27
  67.1 9.5 %collective-permute-start.23 = (bf16[64,1280]{1,0:T(8,128)(2,1)S(1)}, bf16[64,1280]{1,0:T(8,128)(2,1)S(1)}, u32[]{:S(2)}, u32[]{:S(2)}) collective-permute-start(bf16[64,1280]{1,0:T(8,128)(2,1)S(1)} %get-tuple-element.81), channel_id=1, source_target_pairs={{0,2},{2,0},{4,6},{6,4},{8,10},{10,8},{12,14},{14,12},{1,3},{3,1},... | collective-permute-start | bytes 491528 | tf_op jit(solution)/shard_map/off_back/ppermute | solution.py:27
  68.9 16.6 %collective-permute-start.29 = (bf16[128,1920]{1,0:T(8,128)(2,1)S(1)}, bf16[128,1920]{1,0:T(8,128)(2,1)S(1)}, u32[]{:S(2)}, u32[]{:S(2)}) collective-permute-start(bf16[128,1920]{1,0:T(8,128)(2,1)S(1)} %get-tuple-element.83.refs_0_.own), channel_id=1, source_target_pairs={{0,1},{1,0},{2,3},{3,2},{4,5},{5,4},{6,7},{7,6},{8,9},{9,8},{10,11... | collective-permute-start | bytes 1474568 | tf_op jit(solution)/shard_map/swap_chain1/ppermute | solution.py:84
  76.5 1.5 %collective-permute-start.25 = (bf16[64,1280]{1,0:T(8,128)(2,1)S(1)}, bf16[64,1280]{1,0:T(8,128)(2,1)S(1)}, u32[]{:S(2)}, u32[]{:S(2)}) collective-permute-start(bf16[64,1280]{1,0:T(8,128)(2,1)S(1)} %get-tuple-element.85), channel_id=1, source_target_pairs={{0,2},{2,0},{4,6},{6,4},{8,10},{10,8},{12,14},{14,12},{1,3},{3,1},... | collective-permute-start | bytes 491528 | tf_op jit(solution)/shard_map/off_forward/ppermute | solution.py:27
  78.1 9.6 %collective-permute-start.26 = (bf16[2,16,1280]{2,1,0:T(8,128)(2,1)S(1)}, bf16[2,16,1280]{2,1,0:T(8,128)(2,1)S(1)}, u32[]{:S(2)}, u32[]{:S(2)}) collective-permute-start(bf16[2,16,1280]{2,1,0:T(8,128)(2,1)S(1)} %get-tuple-element.113), channel_id=1, source_target_pairs={{0,12},{2,14},{4,0},{6,2},{8,4},{10,6},{12,8},{14,10},{1,13},{3,15... | collective-permute-start | bytes 245768 | tf_op jit(solution)/shard_map/off_forward/ppermute | solution.py:32
  81.0 8.3 %collective-permute-start.27 = (bf16[2,16,1280]{2,1,0:T(8,128)(2,1)S(1)}, bf16[2,16,1280]{2,1,0:T(8,128)(2,1)S(1)}, u32[]{:S(2)}, u32[]{:S(2)}) collective-permute-start(bf16[2,16,1280]{2,1,0:T(8,128)(2,1)S(1)} %get-tuple-element.112), channel_id=1, source_target_pairs={{0,8},{2,10},{4,12},{6,14},{8,0},{10,2},{12,4},{14,6},{1,9},{3,11}... | collective-permute-start | bytes 245768 | tf_op jit(solution)/shard_map/off_forward/ppermute | solution.py:32
  81.6 7.7 %collective-permute-start.28 = (bf16[2,16,1280]{2,1,0:T(8,128)(2,1)S(1)}, bf16[2,16,1280]{2,1,0:T(8,128)(2,1)S(1)}, u32[]{:S(2)}, u32[]{:S(2)}) collective-permute-start(bf16[2,16,1280]{2,1,0:T(8,128)(2,1)S(1)} %get-tuple-element.111), channel_id=1, source_target_pairs={{0,4},{2,6},{4,8},{6,10},{8,12},{10,14},{12,0},{14,2},{1,5},{3,7},... | collective-permute-start | bytes 245768 | tf_op jit(solution)/shard_map/off_forward/ppermute | solution.py:32
  87.7 17.5 %copy-start.1 = (f32[1,1,1,6,128,128]{5,4,3,2,1,0:T(8,128)S(1)}, f32[1,1,1,6,128,128]{5,4,3,2,1,0:T(8,128)}, u32[]{:S(2)}) copy-start(f32[1,1,1,6,128,128]{5,4,3,2,1,0:T(8,128)} %param.26) | copy-start | bytes 1179652
  87.7 17.5 %copy-start.2 = (f32[1,1,1,6,128,128]{5,4,3,2,1,0:T(8,128)S(1)}, f32[1,1,1,6,128,128]{5,4,3,2,1,0:T(8,128)}, u32[]{:S(2)}) copy-start(f32[1,1,1,6,128,128]{5,4,3,2,1,0:T(8,128)} %param.27) | copy-start | bytes 1179652
  89.3 2.3 %collective-permute-start.30 = (bf16[64,1280]{1,0:T(8,128)(2,1)S(1)}, bf16[64,1280]{1,0:T(8,128)(2,1)S(1)}, u32[]{:S(2)}, u32[]{:S(2)}) collective-permute-start(bf16[64,1280]{1,0:T(8,128)(2,1)S(1)} %get-tuple-element.93), channel_id=1, source_target_pairs={{0,2},{2,0},{4,6},{6,4},{8,10},{10,8},{12,14},{14,12},{1,3},{3,1},... | collective-permute-start | bytes 491528 | tf_op jit(solution)/shard_map/chain1/ppermute | solution.py:27
  91.5 4.3 %collective-permute-start.34 = (bf16[4,128,128]{2,1,0:T(8,128)(2,1)S(1)}, bf16[4,128,128]{2,1,0:T(8,128)(2,1)S(1)}, u32[]{:S(2)}, u32[]{:S(2)}) collective-permute-start(bf16[4,128,128]{2,1,0:T(8,128)(2,1)S(1)} %slice.206), channel_id=1, source_target_pairs={{0,2},{2,0},{4,6},{6,4},{8,10},{10,8},{12,14},{14,12},{1,3},{3,1},... | collective-permute-start | bytes 393224 | tf_op jit(solution)/shard_map/block_exchange/ppermute | solution.py:27
  91.7 7.0 %collective-permute-start.31 = (bf16[16,1280]{1,0:T(8,128)(2,1)S(1)}, bf16[16,1280]{1,0:T(8,128)(2,1)S(1)}, u32[]{:S(2)}, u32[]{:S(2)}) collective-permute-start(bf16[16,1280]{1,0:T(8,128)(2,1)S(1)} %get-tuple-element.119), channel_id=1, source_target_pairs={{0,12},{2,14},{4,0},{6,2},{8,4},{10,6},{12,8},{14,10},{1,13},{3,15... | collective-permute-start | bytes 122888 | tf_op jit(solution)/shard_map/chain1/ppermute | solution.py:32
  93.6 6.5 %collective-permute-start.32 = (bf16[16,1280]{1,0:T(8,128)(2,1)S(1)}, bf16[16,1280]{1,0:T(8,128)(2,1)S(1)}, u32[]{:S(2)}, u32[]{:S(2)}) collective-permute-start(bf16[16,1280]{1,0:T(8,128)(2,1)S(1)} %get-tuple-element.118), channel_id=1, source_target_pairs={{0,8},{2,10},{4,12},{6,14},{8,0},{10,2},{12,4},{14,6},{1,9},{3,11}... | collective-permute-start | bytes 122888 | tf_op jit(solution)/shard_map/chain1/ppermute | solution.py:32
  93.8 6.4 %collective-permute-start.33 = (bf16[16,1280]{1,0:T(8,128)(2,1)S(1)}, bf16[16,1280]{1,0:T(8,128)(2,1)S(1)}, u32[]{:S(2)}, u32[]{:S(2)}) collective-permute-start(bf16[16,1280]{1,0:T(8,128)(2,1)S(1)} %get-tuple-element.117), channel_id=1, source_target_pairs={{0,4},{2,6},{4,8},{6,10},{8,12},{10,14},{12,0},{14,2},{1,5},{3,7},... | collective-permute-start | bytes 122888 | tf_op jit(solution)/shard_map/chain1/ppermute | solution.py:32
  95.8 5.1 %collective-permute-start.35 = (bf16[256,128]{1,0:T(8,128)(2,1)S(1)}, bf16[256,128]{1,0:T(8,128)(2,1)S(1)}, u32[]{:S(2)}, u32[]{:S(2)}) collective-permute-start(bf16[256,128]{1,0:T(8,128)(2,1)S(1)} %pad_maximum_fusion.8), channel_id=1, source_target_pairs={{0,12},{2,14},{4,0},{6,2},{8,4},{10,6},{12,8},{14,10},{1,13},{3,15... | collective-permute-start | bytes 196616 | tf_op jit(solution)/shard_map/block_exchange/ppermute | solution.py:32
  97.7 7.4 %collective-permute-start.36 = (bf16[256,128]{1,0:T(8,128)(2,1)S(1)}, bf16[256,128]{1,0:T(8,128)(2,1)S(1)}, u32[]{:S(2)}, u32[]{:S(2)}) collective-permute-start(bf16[256,128]{1,0:T(8,128)(2,1)S(1)} %pad_maximum_fusion.9), channel_id=1, source_target_pairs={{0,8},{2,10},{4,12},{6,14},{8,0},{10,2},{12,4},{14,6},{1,9},{3,11}... | collective-permute-start | bytes 196616 | tf_op jit(solution)/shard_map/block_exchange/ppermute | solution.py:32
  98.7 6.4 %collective-permute-start.37 = (bf16[256,128]{1,0:T(8,128)(2,1)S(1)}, bf16[256,128]{1,0:T(8,128)(2,1)S(1)}, u32[]{:S(2)}, u32[]{:S(2)}) collective-permute-start(bf16[256,128]{1,0:T(8,128)(2,1)S(1)} %pad_maximum_fusion.10), channel_id=1, source_target_pairs={{0,4},{2,6},{4,8},{6,10},{8,12},{10,14},{12,0},{14,2},{1,5},{3,7},... | collective-permute-start | bytes 196616 | tf_op jit(solution)/shard_map/block_exchange/ppermute | solution.py:32

commit v4 on v3

--- a/solution.py
+++ b/solution.py
@@ -676,12 +676,11 @@
         )
         got = sibling(sent)
         chain_sums = scatter_parts(summed_pairs(kept, got))
-        off_sums = later(off_sums, kept)
     tables = [
         (*back_halves, scaled, activated, grads),
         (*off_halves, off_scaled, off_activated, *off_grad_halves),
     ]
-    relayed, from_others = exchange(later(plan, off_sums), tables, got)
+    relayed, from_others, off_sums = exchange(plan, tables, got, off_sums)
     section_outputs, input_grads, done = finish_pair(
         flag, chained, off_grads, off_rows, chain_in, off_sums, chain_sums
     )
@@ -798,13 +797,14 @@
     dp_index = lax.axis_index("dp")
     plan = jnp.concatenate([jnp.full((dp_count, 1), dp_index, jnp.int32), counts[:, None], owners, blocks], axis=1)
 
-    def exchange(plan, tables, before):
+    def exchange(plan, tables, before, beside):
         with jax.named_scope("block_exchange"):
             outgoing = outgoing_blocks(plan, capacity, norm_gain, tables, channels // BLK, hidden // BLK)
             outgoing = outgoing.reshape((2, dp_count // 2, BLK, BLK))
-            relayed = later(sibling(outgoing[1]), before)
+            beside = later(beside, outgoing)
+            relayed = later(sibling(outgoing[1]), before, beside)
             pairs = [jnp.concatenate([outgoing[0, k], relayed[k]]) for k in range(1, dp_count // 2)]
-            return relayed, [shifted(pair, -k - 1) for k, pair in enumerate(pairs)]
+            return relayed, [shifted(pair, -k - 1) for k, pair in enumerate(pairs)], beside
 
     if section_count == 2 and turn_count == 2:
         section_outputs, input_grads, plan, relayed, others, after = relay_pair(
@@ -818,7 +818,7 @@
             is_first, is_last, masked, entering, section_inputs, grad_outputs, stashed_inputs, norm_gain,
             up_weight[0], down_weight[0], width,
         )
-        relayed, others = exchange(plan, tables, None)
+        relayed, others, _ = exchange(plan, tables, None, None)
         after = []
     first_out, second_out, direction_out = adam(
         plan, relayed, others, first_moment[0, 0, 0], second_moment[0, 0, 0], after

time: 108 us -> 108 us (level)
  starting transfers between devices: 42.4 us -> 43.5 us
  waiting for transfers between devices: 36.3 us -> 35.2 us
    ppermute x18, waiting for transfers between devices: 17.2 us -> 15.2 us  [shifted(): lax.ppermute(value, 'dp', [(d, (d + 2 * steps) % count) for d in range(co...]
where the time goes in v4:
time: 108 us; the launch traced here: 107 us
  starting transfers between devices  43.5 us (40%)
  waiting for transfers between devices  35.2 us (33%)
  Pallas kernels  23.7 us (22%)
  local copies, waits for them, and re-layouts  2.44 us (2%)
  between operations  1.95 us (2%)
    ppermute x18, starting transfers between devices, shifted(): lax.ppermute(value, 'dp', [(d, (d + 2 * steps) % count) for d in range(co...  26.7 us
    ppermute x18, waiting for transfers between devices, shifted(): lax.ppermute(value, 'dp', [(d, (d + 2 * steps) % count) for d in range(co...  15.2 us
    pallas_call x9, Pallas kernels, call(): pl.pallas_call(kernel, out_shape=outs, in_specs=specs, out_specs=[VMEM] *...  12.9 us
    ppermute x5, waiting for transfers between devices, tensor_parts(): got = lax.ppermute(value, 'tensor', [(t, t ^ step) for t in range(count)])  12.9 us
    ppermute x4, starting transfers between devices, moved(): return lax.ppermute(local, ('section', 'dp'), pairs)  8.15 us
    ppermute x5, starting transfers between devices, tensor_parts(): got = lax.ppermute(value, 'tensor', [(t, t ^ step) for t in range(count)])  6.54 us
    pallas_call x2, Pallas kernels, load_one(): pl.pallas_call(load_one_kernel, out_shape=pltpu.VMEM(weight.shape, BF16),...  4.65 us
    ppermute x4, waiting for transfers between devices, moved(): return lax.ppermute(local, ('section', 'dp'), pairs)  3.6 us
  transfers between devices with their start and end apart: 38, of which 19 were waited for; matrix products, arithmetic and copies ran while one was open for 3% of the time, Pallas kernels for 18%

profile of v4, /device:TPU:0, one launch (start us, length us, event | category | flops | bytes accessed | tf_op | source)
XLA Modules:
  0.0 107.4 jit_solution(15876174632511429944)
XLA Ops:
  0.6 0.8 first_rows.1.refs_0_
  1.5 3.1 %collective-permute-start = (bf16[2,16,1280]{2,1,0:T(8,128)(2,1)S(1)}, bf16[2,16,1280]{2,1,0:T(8,128)(2,1)S(1)}, u32[]{:S(2)}, u32[]{:S(2)}) collective-permute-start(bf16[2,16,1280]{2,1,0:T(8,128)(2,1)S(1)} %first_rows.1.refs_0_), channel_id=1, source_target_pairs={{0,4},{2,6},{4,8},{6,10},{8,12},{10,14},{12,0},{14,2},{1,5},{3,7},... | collective-permute-start | bytes 245768 | tf_op jit(solution)/shard_map/gather_first/ppermute | solution.py:32
  4.5 2.6 %collective-permute-start.1 = (bf16[2,16,1280]{2,1,0:T(8,128)(2,1)S(1)}, bf16[2,16,1280]{2,1,0:T(8,128)(2,1)S(1)}, u32[]{:S(2)}, u32[]{:S(2)}) collective-permute-start(bf16[2,16,1280]{2,1,0:T(8,128)(2,1)S(1)} %first_rows.1.refs_0_), channel_id=1, source_target_pairs={{0,8},{2,10},{4,12},{6,14},{8,0},{10,2},{12,4},{14,6},{1,9},{3,11}... | collective-permute-start | bytes 245768 | tf_op jit(solution)/shard_map/gather_first/ppermute | solution.py:32
  7.1 1.3 %collective-permute-start.2 = (bf16[2,16,1280]{2,1,0:T(8,128)(2,1)S(1)}, bf16[2,16,1280]{2,1,0:T(8,128)(2,1)S(1)}, u32[]{:S(2)}, u32[]{:S(2)}) collective-permute-start(bf16[2,16,1280]{2,1,0:T(8,128)(2,1)S(1)} %first_rows.1.refs_0_), channel_id=1, source_target_pairs={{0,12},{2,14},{4,0},{6,2},{8,4},{10,6},{12,8},{14,10},{1,13},{3,15... | collective-permute-start | bytes 245768 | tf_op jit(solution)/shard_map/gather_first/ppermute | solution.py:32
  8.5 0.8 copy.22
  9.2 0.8 copy.21
  10.8 2.3 %load_weight.2.up._ = bf16[1280,1792]{1,0:T(8,128)(2,1)S(1)} custom-call(bf16[1280,1792]{1,0:T(8,128)(2,1)} %bitcast.115, bf16[2,16,1280]{2,1,0:T(8,128)(2,1)S(1)} %first_rows.1.refs_0_, s32[8,14]{1,0:T(8,128)S(1)} %pad_add_fusion.refs_1_.plan), custom_call_target="tpu_custom_call" | custom-call | tf_op jit(solution)/shard_map/load_weight/pallas_call | solution.py:132
  15.0 0.8 products.2.refs_0_.back_own
  15.8 1.6 %collective-permute-start.6 = (bf16[128,1920]{1,0:T(8,128)(2,1)S(1)}, bf16[128,1920]{1,0:T(8,128)(2,1)S(1)}, u32[]{:S(2)}, u32[]{:S(2)}) collective-permute-start(bf16[128,1920]{1,0:T(8,128)(2,1)S(1)} %products.2.refs_0_.back_own), channel_id=1, source_target_pairs={{0,1},{1,0},{2,3},{3,2},{4,5},{5,4},{6,7},{7,6},{8,9},{9,8},{10,11... | collective-permute-start | bytes 1474568 | tf_op jit(solution)/shard_map/swap_back/ppermute | solution.py:84
  17.3 2.3 %load_weight.3.down.refs_0_._ = bf16[1792,1280]{1,0:T(8,128)(2,1)S(1)} custom-call(bf16[1792,1280]{1,0:T(8,128)(2,1)} %bitcast.116, bf16[128,1920]{1,0:T(8,128)(2,1)S(1)} %products.2.refs_0_.back_own), custom_call_target="tpu_custom_call" | custom-call | tf_op jit(solution)/shard_map/load_weight/pallas_call | solution.py:132
  19.7 1.5 %enter.2 = (bf16[128,1920]{1,0:T(8,128)(2,1)S(1)}, bf16[128,1280]{1,0:T(8,128)(2,1)}) custom-call(s32[1]{0:T(128)} %bitcast.flag, bf16[64,1280]{1,0:T(8,128)(2,1)S(1)} %pad_maximum_fusion.1.low.other_low, bf16[64,1280]{1,0:T(8,128)(2,1)S(1)} %collective-permute-done.3.high.other_high, bf16[64,1280]{1,0:T(8,128)(2,1)S(1)} %pad_maximum_fusion.1.low.other_low, ...), custom_call_target="tpu_custom_call" | custom-call | flops 1 | bytes 1 | tf_op jit(solution)/shard_map/enter/pallas_call | solution.py:96
  21.3 1.7 %collective-permute-start.7 = (bf16[3,16,1280]{2,1,0:T(8,128)(2,1)S(1)}, bf16[3,16,1280]{2,1,0:T(8,128)(2,1)S(1)}, u32[]{:S(2)}, u32[]{:S(2)}) collective-permute-start(bf16[3,16,1280]{2,1,0:T(8,128)(2,1)S(1)} %pad_maximum_fusion.7), channel_id=1, source_target_pairs={{0,4},{2,6},{4,8},{6,10},{8,12},{10,14},{12,0},{14,2},{1,5},{3,7},... | collective-permute-start | bytes 368648 | tf_op jit(solution)/shard_map/gather_others/ppermute | solution.py:32
  23.0 1.9 %collective-permute-start.8 = (bf16[3,16,1280]{2,1,0:T(8,128)(2,1)S(1)}, bf16[3,16,1280]{2,1,0:T(8,128)(2,1)S(1)}, u32[]{:S(2)}, u32[]{:S(2)}) collective-permute-start(bf16[3,16,1280]{2,1,0:T(8,128)(2,1)S(1)} %pad_maximum_fusion.7), channel_id=1, source_target_pairs={{0,8},{2,10},{4,12},{6,14},{8,0},{10,2},{12,4},{14,6},{1,9},{3,11}... | collective-permute-start | bytes 368648 | tf_op jit(solution)/shard_map/gather_others/ppermute | solution.py:32
  26.0 3.5 %collective-permute-done.7 = bf16[3,16,1280]{2,1,0:T(8,128)(2,1)S(1)} collective-permute-done((bf16[3,16,1280]{2,1,0:T(8,128)(2,1)S(1)}, bf16[3,16,1280]{2,1,0:T(8,128)(2,1)S(1)}, u32[]{:S(2)}, u32[]{:S(2)}) %collective-permute-start.7) | collective-permute-done | bytes 122912 | tf_op jit(solution)/shard_map/gather_others/ppermute | solution.py:32
  29.5 4.4 %collective-permute-done.8 = bf16[3,16,1280]{2,1,0:T(8,128)(2,1)S(1)} collective-permute-done((bf16[3,16,1280]{2,1,0:T(8,128)(2,1)S(1)}, bf16[3,16,1280]{2,1,0:T(8,128)(2,1)S(1)}, u32[]{:S(2)}, u32[]{:S(2)}) %collective-permute-start.8) | collective-permute-done | bytes 122912 | tf_op jit(solution)/shard_map/gather_others/ppermute | solution.py:32
  35.6 2.0 %products_and_act_grads.1.refs_0_.own = bf16[128,3712]{1,0:T(8,128)(2,1)S(1)} custom-call(bf16[64,1280]{1,0:T(8,128)(2,1)S(1)} %pad_maximum_fusion.3.low.refs_5_, bf16[64,1280]{1,0:T(8,128)(2,1)S(1)} %collective-permute-done.10.high.refs_6_, bf16[64,1280]{1,0:T(8,128)(2,1)S(1)} %pad_maximum_fusion.4.grad_low.refs_9_, ...), custom_call_target="tpu_custom_call" | custom-call | flops 1 | bytes 1 | tf_op jit(solution)/shard_map/products_and_act_grads/pallas_call | solution.py:96
  37.6 0.8 products.3.refs_1_.own
  38.4 1.4 %collective-permute-done.5.got = bf16[128,1920]{1,0:T(8,128)(2,1)S(1)} collective-permute-done((bf16[128,1920]{1,0:T(8,128)(2,1)S(1)}, bf16[128,1920]{1,0:T(8,128)(2,1)S(1)}, u32[]{:S(2)}, u32[]{:S(2)}) %collective-permute-start.5) | collective-permute-done | bytes 491552 | tf_op jit(solution)/shard_map/swap_chain0/ppermute | solution.py:84
  39.8 1.1 leave.2
  41.0 1.6 %collective-permute-start.22 = (bf16[128,3712]{1,0:T(8,128)(2,1)S(1)}, bf16[128,3712]{1,0:T(8,128)(2,1)S(1)}, u32[]{:S(2)}, u32[]{:S(2)}) collective-permute-start(bf16[128,3712]{1,0:T(8,128)(2,1)S(1)} %products_and_act_grads.1.refs_0_.own), channel_id=1, source_target_pairs={{0,1},{1,0},{2,3},{3,2},{4,5},{5,4},{6,7},{7,6},{8,9},{9,8},{10,11... | collective-permute-start | bytes 2850824 | tf_op jit(solution)/shard_map/swap_off_back/ppermute | solution.py:84
  42.6 1.7 %collective-permute-start.16 = (bf16[16,1280]{1,0:T(8,128)(2,1)S(1)}, bf16[16,1280]{1,0:T(8,128)(2,1)S(1)}, u32[]{:S(2)}, u32[]{:S(2)}) collective-permute-start(bf16[16,1280]{1,0:T(8,128)(2,1)S(1)} %get-tuple-element.119), channel_id=1, source_target_pairs={{0,4},{2,6},{4,8},{6,10},{8,12},{10,14},{12,0},{14,2},{1,5},{3,7},... | collective-permute-start | bytes 122888 | tf_op jit(solution)/shard_map/chain0/ppermute | solution.py:32
  44.3 1.9 %collective-permute-start.15 = (bf16[16,1280]{1,0:T(8,128)(2,1)S(1)}, bf16[16,1280]{1,0:T(8,128)(2,1)S(1)}, u32[]{:S(2)}, u32[]{:S(2)}) collective-permute-start(bf16[16,1280]{1,0:T(8,128)(2,1)S(1)} %get-tuple-element.120), channel_id=1, source_target_pairs={{0,8},{2,10},{4,12},{6,14},{8,0},{10,2},{12,4},{14,6},{1,9},{3,11}... | collective-permute-start | bytes 122888 | tf_op jit(solution)/shard_map/chain0/ppermute | solution.py:32
  46.7 1.3 %collective-permute-start.24 = (bf16[128,1920]{1,0:T(8,128)(2,1)S(1)}, bf16[128,1920]{1,0:T(8,128)(2,1)S(1)}, u32[]{:S(2)}, u32[]{:S(2)}) collective-permute-start(bf16[128,1920]{1,0:T(8,128)(2,1)S(1)} %products.3.refs_1_.own), channel_id=1, source_target_pairs={{0,1},{1,0},{2,3},{3,2},{4,5},{5,4},{6,7},{7,6},{8,9},{9,8},{10,11... | collective-permute-start | bytes 1474568 | tf_op jit(solution)/shard_map/swap_off_forward/ppermute | solution.py:84
  48.6 1.3 %collective-permute-done.15 = bf16[16,1280]{1,0:T(8,128)(2,1)S(1)} collective-permute-done((bf16[16,1280]{1,0:T(8,128)(2,1)S(1)}, bf16[16,1280]{1,0:T(8,128)(2,1)S(1)}, u32[]{:S(2)}, u32[]{:S(2)}) %collective-permute-start.15) | collective-permute-done | bytes 40992 | tf_op jit(solution)/shard_map/chain0/ppermute | solution.py:32
  50.3 5.1 %collective-permute-start.20 = (bf16[1,16,1280]{2,1,0:T(8,128)(2,1)S(1)}, bf16[1,16,1280]{2,1,0:T(8,128)(2,1)S(1)}, u32[]{:S(2)}, u32[]{:S(2)}) collective-permute-start(bf16[1,16,1280]{2,1,0:T(8,128)(2,1)S(1)} %bitcast.105), channel_id=1, source_target_pairs={{0,28},{2,30},{4,16},{6,18},{8,20},{10,22},{12,24},{14,26},{16,12}... | collective-permute-start | bytes 122888 | tf_op jit(solution)/shard_map/pass/ppermute | solution.py:50
  55.4 1.6 %collective-permute-start.18 = (bf16[1,16,1280]{2,1,0:T(8,128)(2,1)S(1)}, bf16[1,16,1280]{2,1,0:T(8,128)(2,1)S(1)}, u32[]{:S(2)}, u32[]{:S(2)}) collective-permute-start(bf16[1,16,1280]{2,1,0:T(8,128)(2,1)S(1)} %bitcast.107), channel_id=1, source_target_pairs={{0,20},{2,22},{4,24},{6,26},{8,28},{10,30},{12,16},{14,18},{16,4},... | collective-permute-start | bytes 122888 | tf_op jit(solution)/shard_map/pass/ppermute | solution.py:50
  57.0 1.5 %collective-permute-start.17 = (bf16[1,16,1280]{2,1,0:T(8,128)(2,1)S(1)}, bf16[1,16,1280]{2,1,0:T(8,128)(2,1)S(1)}, u32[]{:S(2)}, u32[]{:S(2)}) collective-permute-start(bf16[1,16,1280]{2,1,0:T(8,128)(2,1)S(1)} %bitcast.108), channel_id=1, source_target_pairs={{0,16},{2,18},{4,20},{6,22},{8,24},{10,26},{12,28},{14,30},{16,0},... | collective-permute-start | bytes 122888 | tf_op jit(solution)/shard_map/pass/ppermute | solution.py:50
  58.5 2.7 %collective-permute-done.19 = bf16[1,16,1280]{2,1,0:T(8,128)(2,1)S(1)} collective-permute-done((bf16[1,16,1280]{2,1,0:T(8,128)(2,1)S(1)}, bf16[1,16,1280]{2,1,0:T(8,128)(2,1)S(1)}, u32[]{:S(2)}, u32[]{:S(2)}) %collective-permute-start.19) | collective-permute-done | bytes 40992 | tf_op jit(solution)/shard_map/pass/ppermute | solution.py:50
  61.3 0.8 collective-permute-done.18
  62.2 2.7 %collective-permute-done.22.got = bf16[128,3712]{1,0:T(8,128)(2,1)S(1)} collective-permute-done((bf16[128,3712]{1,0:T(8,128)(2,1)S(1)}, bf16[128,3712]{1,0:T(8,128)(2,1)S(1)}, u32[]{:S(2)}, u32[]{:S(2)}) %collective-permute-start.22) | collective-permute-done | bytes 950304 | tf_op jit(solution)/shard_map/swap_off_back/ppermute | solution.py:84
  64.9 2.2 %backward.1 = (f32[64,1280]{1,0:T(8,128)S(1)}, bf16[64,1280]{1,0:T(8,128)(2,1)S(1)}, bf16[128,1792]{1,0:T(8,128)(2,1)S(1)}, bf16[128,1792]{1,0:T(8,128)(2,1)S(1)}) custom-call(bf16[128,3712]{1,0:T(8,128)(2,1)S(1)} %products_and_act_grads.1.refs_0_.own, bf16[128,3712]{1,0:T(8,128)(2,1)S(1)} %collective-permute-done.22.got, ...), custom_call_target="tpu_custom_call" | custom-call | flops 1 | bytes 1 | tf_op jit(solution)/shard_map/off_back/backward/pallas_call | solution.py:96
  67.2 1.8 %enter.3 = (bf16[128,1920]{1,0:T(8,128)(2,1)S(1)}, bf16[128,1280]{1,0:T(8,128)(2,1)S(1)}) custom-call(s32[1]{0:T(128)} %bitcast.flag, bf16[64,1280]{1,0:T(8,128)(2,1)S(1)} %pad_maximum_fusion.6.low, bf16[64,1280]{1,0:T(8,128)(2,1)S(1)} %collective-permute-done.21.high, bf16[64,1280]{1,0:T(8,128)(2,1)S(1)} %pad_maximum_fusion.1.low.other_low, ...), custom_call_target="tpu_custom_call" | custom-call | flops 1 | bytes 1 | tf_op jit(solution)/shard_map/enter/pallas_call | solution.py:96
  68.9 1.6 %collective-permute-start.29 = (bf16[128,1920]{1,0:T(8,128)(2,1)S(1)}, bf16[128,1920]{1,0:T(8,128)(2,1)S(1)}, u32[]{:S(2)}, u32[]{:S(2)}) collective-permute-start(bf16[128,1920]{1,0:T(8,128)(2,1)S(1)} %get-tuple-element.82.refs_0_.own), channel_id=1, source_target_pairs={{0,1},{1,0},{2,3},{3,2},{4,5},{5,4},{6,7},{7,6},{8,9},{9,8},{10,11... | collective-permute-start | bytes 1474568 | tf_op jit(solution)/shard_map/swap_chain1/ppermute | solution.py:84
  70.5 4.9 %collective-permute-done.24.got = bf16[128,1920]{1,0:T(8,128)(2,1)S(1)} collective-permute-done((bf16[128,1920]{1,0:T(8,128)(2,1)S(1)}, bf16[128,1920]{1,0:T(8,128)(2,1)S(1)}, u32[]{:S(2)}, u32[]{:S(2)}) %collective-permute-start.24) | collective-permute-done | bytes 491552 | tf_op jit(solution)/shard_map/swap_off_forward/ppermute | solution.py:84
  75.4 1.0 forward.1
  76.6 1.3 %collective-permute-done.25 = bf16[64,1280]{1,0:T(8,128)(2,1)S(1)} collective-permute-done((bf16[64,1280]{1,0:T(8,128)(2,1)S(1)}, bf16[64,1280]{1,0:T(8,128)(2,1)S(1)}, u32[]{:S(2)}, u32[]{:S(2)}) %collective-permute-start.25) | collective-permute-done | bytes 163872 | tf_op jit(solution)/shard_map/off_forward/ppermute | solution.py:27
  78.1 3.0 %collective-permute-start.26 = (bf16[2,16,1280]{2,1,0:T(8,128)(2,1)S(1)}, bf16[2,16,1280]{2,1,0:T(8,128)(2,1)S(1)}, u32[]{:S(2)}, u32[]{:S(2)}) collective-permute-start(bf16[2,16,1280]{2,1,0:T(8,128)(2,1)S(1)} %get-tuple-element.111), channel_id=1, source_target_pairs={{0,12},{2,14},{4,0},{6,2},{8,4},{10,6},{12,8},{14,10},{1,13},{3,15... | collective-permute-start | bytes 245768 | tf_op jit(solution)/shard_map/off_forward/ppermute | solution.py:32
  81.7 3.8 %collective-permute-done.29.got = bf16[128,1920]{1,0:T(8,128)(2,1)S(1)} collective-permute-done((bf16[128,1920]{1,0:T(8,128)(2,1)S(1)}, bf16[128,1920]{1,0:T(8,128)(2,1)S(1)}, u32[]{:S(2)}, u32[]{:S(2)}) %collective-permute-start.29) | collective-permute-done | bytes 491552 | tf_op jit(solution)/shard_map/swap_chain1/ppermute | solution.py:84
  85.5 2.1 %leave.3 = (f32[64,1280]{1,0:T(8,128)S(1)}, bf16[64,1280]{1,0:T(8,128)(2,1)S(1)}, bf16[128,1792]{1,0:T(8,128)(2,1)S(1)}, bf16[128,1792]{1,0:T(8,128)(2,1)S(1)}) custom-call(s32[1]{0:T(128)} %bitcast.flag, bf16[128,1920]{1,0:T(8,128)(2,1)S(1)} %get-tuple-element.82.refs_0_.own, ...), custom_call_target="tpu_custom_call", output_to_operand_aliasing={{2}: (10, {}), {3}: (11, {})} | custom-call | flops 1 | bytes 1 | tf_op jit(solution)/shard_map/chain1/leave/pallas_call | solution.py:404
  87.7 2.1 %block_grads.1 = bf16[8,128,128]{2,1,0:T(8,128)(2,1)S(1)} custom-call(s32[8,14]{1,0:T(8,128)S(1)} %pad_add_fusion.refs_1_.plan, bf16[1,1280]{1,0:T(2,128)(2,1)S(1)} %copy-done, bf16[64,1280]{1,0:T(8,128)(2,1)S(1)} %pad_maximum_fusion.2.low.refs_0_, bf16[64,1280]{1,0:T(8,128)(2,1)S(1)} %collective-permute-done.4.high.refs_1_, ...), custom_call_target="tpu_custom_call" | custom-call | flops 1 | bytes 1 | tf_op jit(solution)/shard_map/block_exchange/block_grads/pallas_call | solution.py:96
  90.4 0.9 collective-permute-done.30
  91.4 2.3 %collective-permute-start.31 = (bf16[16,1280]{1,0:T(8,128)(2,1)S(1)}, bf16[16,1280]{1,0:T(8,128)(2,1)S(1)}, u32[]{:S(2)}, u32[]{:S(2)}) collective-permute-start(bf16[16,1280]{1,0:T(8,128)(2,1)S(1)} %get-tuple-element.117), channel_id=1, source_target_pairs={{0,12},{2,14},{4,0},{6,2},{8,4},{10,6},{12,8},{14,10},{1,13},{3,15... | collective-permute-start | bytes 122888 | tf_op jit(solution)/shard_map/chain1/ppermute | solution.py:32
  93.7 0.9 collective-permute-start.32
  94.6 3.9 %collective-permute-start.35 = (bf16[256,128]{1,0:T(8,128)(2,1)S(1)}, bf16[256,128]{1,0:T(8,128)(2,1)S(1)}, u32[]{:S(2)}, u32[]{:S(2)}) collective-permute-start(bf16[256,128]{1,0:T(8,128)(2,1)S(1)} %pad_maximum_fusion.8), channel_id=1, source_target_pairs={{0,12},{2,14},{4,0},{6,2},{8,4},{10,6},{12,8},{14,10},{1,13},{3,15... | collective-permute-start | bytes 196616 | tf_op jit(solution)/shard_map/block_exchange/ppermute | solution.py:32
  99.3 1.6 %collective-permute-done.33.refs_7_ = bf16[16,1280]{1,0:T(8,128)(2,1)S(1)} collective-permute-done((bf16[16,1280]{1,0:T(8,128)(2,1)S(1)}, bf16[16,1280]{1,0:T(8,128)(2,1)S(1)}, u32[]{:S(2)}, u32[]{:S(2)}) %collective-permute-start.33) | collective-permute-done | bytes 40992 | tf_op jit(solution)/shard_map/chain1/ppermute | solution.py:32
  100.9 0.7 finish_pair.1
  101.6 3.5 %collective-permute-done.36.refs_1_ = bf16[256,128]{1,0:T(8,128)(2,1)S(1)} collective-permute-done((bf16[256,128]{1,0:T(8,128)(2,1)S(1)}, bf16[256,128]{1,0:T(8,128)(2,1)S(1)}, u32[]{:S(2)}, u32[]{:S(2)}) %collective-permute-start.36) | collective-permute-done | bytes 65568 | tf_op jit(solution)/shard_map/block_exchange/ppermute | solution.py:32
  105.1 2.1 %adam_step.1 = (f32[6,128,128]{2,1,0:T(8,128)}, f32[6,128,128]{2,1,0:T(8,128)}, f32[6,128,128]{2,1,0:T(8,128)}) custom-call(s32[8,14]{1,0:T(8,128)S(1)} %pad_add_fusion.refs_1_.plan, bf16[4,128,128]{2,1,0:T(8,128)(2,1)S(1)} %collective-permute-done.34.relayed, bf16[256,128]{1,0:T(8,128)(2,1)S(1)} %collective-permute-done.35.refs_0_, ...), custom_call_target="tpu_custom_call" | custom-call | tf_op jit(solution)/shard_map/adam_step/pallas_call | solution.py:546
  (102 shorter events, 9.2 us)
Async XLA Ops:
  1.5 11.7 %collective-permute-start = (bf16[2,16,1280]{2,1,0:T(8,128)(2,1)S(1)}, bf16[2,16,1280]{2,1,0:T(8,128)(2,1)S(1)}, u32[]{:S(2)}, u32[]{:S(2)}) collective-permute-start(bf16[2,16,1280]{2,1,0:T(8,128)(2,1)S(1)} %first_rows.1.refs_0_), channel_id=1, source_target_pairs={{0,4},{2,6},{4,8},{6,10},{8,12},{10,14},{12,0},{14,2},{1,5},{3,7},... | collective-permute-start | bytes 245768 | tf_op jit(solution)/shard_map/gather_first/ppermute | solution.py:32
  4.5 8.6 %collective-permute-start.1 = (bf16[2,16,1280]{2,1,0:T(8,128)(2,1)S(1)}, bf16[2,16,1280]{2,1,0:T(8,128)(2,1)S(1)}, u32[]{:S(2)}, u32[]{:S(2)}) collective-permute-start(bf16[2,16,1280]{2,1,0:T(8,128)(2,1)S(1)} %first_rows.1.refs_0_), channel_id=1, source_target_pairs={{0,8},{2,10},{4,12},{6,14},{8,0},{10,2},{12,4},{14,6},{1,9},{3,11}... | collective-permute-start | bytes 245768 | tf_op jit(solution)/shard_map/gather_first/ppermute | solution.py:32
  7.1 6.1 %collective-permute-start.2 = (bf16[2,16,1280]{2,1,0:T(8,128)(2,1)S(1)}, bf16[2,16,1280]{2,1,0:T(8,128)(2,1)S(1)}, u32[]{:S(2)}, u32[]{:S(2)}) collective-permute-start(bf16[2,16,1280]{2,1,0:T(8,128)(2,1)S(1)} %first_rows.1.refs_0_), channel_id=1, source_target_pairs={{0,12},{2,14},{4,0},{6,2},{8,4},{10,6},{12,8},{14,10},{1,13},{3,15... | collective-permute-start | bytes 245768 | tf_op jit(solution)/shard_map/gather_first/ppermute | solution.py:32
  10.8 3.1 %copy-start.5 = (bf16[1,2,16,1280]{3,2,1,0:T(8,128)(2,1)S(1)}, bf16[1,2,16,1280]{3,2,1,0:T(8,128)(2,1)}, u32[]{:S(2)}) copy-start(bf16[1,2,16,1280]{3,2,1,0:T(8,128)(2,1)} %param.19) | copy-start | bytes 245764
  10.8 4.2 %copy-start = (bf16[1,1280]{1,0:T(2,128)(2,1)S(1)}, bf16[1,1280]{1,0:T(2,128)(2,1)}, u32[]{:S(2)}) copy-start(bf16[1,1280]{1,0:T(2,128)(2,1)} %gain.17) | copy-start | bytes 7684
  13.3 4.1 %collective-permute-start.3 = (bf16[64,1280]{1,0:T(8,128)(2,1)S(1)}, bf16[64,1280]{1,0:T(8,128)(2,1)S(1)}, u32[]{:S(2)}, u32[]{:S(2)}) collective-permute-start(bf16[64,1280]{1,0:T(8,128)(2,1)S(1)} %pad_maximum_fusion.1.low.other_low), channel_id=1, source_target_pairs={{0,2},{2,0},{4,6},{6,4},{8,10},{10,8},{12,14},{14,12},{1,3},{3,1},... | collective-permute-start | bytes 491528 | tf_op jit(solution)/shard_map/gather_first/ppermute | solution.py:27
  13.4 1.6 %collective-permute-start.4 = (bf16[64,1280]{1,0:T(8,128)(2,1)S(1)}, bf16[64,1280]{1,0:T(8,128)(2,1)S(1)}, u32[]{:S(2)}, u32[]{:S(2)}) collective-permute-start(bf16[64,1280]{1,0:T(8,128)(2,1)S(1)} %pad_maximum_fusion.2.low.refs_0_), channel_id=1, source_target_pairs={{0,2},{2,0},{4,6},{6,4},{8,10},{10,8},{12,14},{14,12},{1,3},{3,1},... | collective-permute-start | bytes 491528 | tf_op jit(solution)/shard_map/gather_first/ppermute | solution.py:27
  15.8 18.1 %collective-permute-start.6 = (bf16[128,1920]{1,0:T(8,128)(2,1)S(1)}, bf16[128,1920]{1,0:T(8,128)(2,1)S(1)}, u32[]{:S(2)}, u32[]{:S(2)}) collective-permute-start(bf16[128,1920]{1,0:T(8,128)(2,1)S(1)} %products.2.refs_0_.back_own), channel_id=1, source_target_pairs={{0,1},{1,0},{2,3},{3,2},{4,5},{5,4},{6,7},{7,6},{8,9},{9,8},{10,11... | collective-permute-start | bytes 1474568 | tf_op jit(solution)/shard_map/swap_back/ppermute | solution.py:84
  19.7 1.6 %copy-start.3 = (bf16[1,16,1280]{2,1,0:T(8,128)(2,1)S(1)}, bf16[1,16,1280]{2,1,0:T(8,128)(2,1)}, u32[]{:S(2)}) copy-start(bf16[1,16,1280]{2,1,0:T(8,128)(2,1)} %param.14) | copy-start | bytes 122884
  19.7 1.6 %copy-start.4 = (bf16[1,16,1280]{2,1,0:T(8,128)(2,1)S(1)}, bf16[1,16,1280]{2,1,0:T(8,128)(2,1)}, u32[]{:S(2)}) copy-start(bf16[1,16,1280]{2,1,0:T(8,128)(2,1)} %param.16) | copy-start | bytes 122884
  19.7 1.6 %copy-start.6 = (bf16[1,16,1280]{2,1,0:T(8,128)(2,1)S(1)}, bf16[1,16,1280]{2,1,0:T(8,128)(2,1)}, u32[]{:S(2)}) copy-start(bf16[1,16,1280]{2,1,0:T(8,128)(2,1)} %param.17) | copy-start | bytes 122884
  19.7 1.5 %copy-start.7 = (bf16[1,16,1280]{2,1,0:T(8,128)(2,1)S(1)}, bf16[1,16,1280]{2,1,0:T(8,128)(2,1)}, u32[]{:S(2)}) copy-start(bf16[1,16,1280]{2,1,0:T(8,128)(2,1)} %param.15) | copy-start | bytes 122884
  21.3 8.1 %collective-permute-start.7 = (bf16[3,16,1280]{2,1,0:T(8,128)(2,1)S(1)}, bf16[3,16,1280]{2,1,0:T(8,128)(2,1)S(1)}, u32[]{:S(2)}, u32[]{:S(2)}) collective-permute-start(bf16[3,16,1280]{2,1,0:T(8,128)(2,1)S(1)} %pad_maximum_fusion.7), channel_id=1, source_target_pairs={{0,4},{2,6},{4,8},{6,10},{8,12},{10,14},{12,0},{14,2},{1,5},{3,7},... | collective-permute-start | bytes 368648 | tf_op jit(solution)/shard_map/gather_others/ppermute | solution.py:32
  23.0 10.8 %collective-permute-start.8 = (bf16[3,16,1280]{2,1,0:T(8,128)(2,1)S(1)}, bf16[3,16,1280]{2,1,0:T(8,128)(2,1)S(1)}, u32[]{:S(2)}, u32[]{:S(2)}) collective-permute-start(bf16[3,16,1280]{2,1,0:T(8,128)(2,1)S(1)} %pad_maximum_fusion.7), channel_id=1, source_target_pairs={{0,8},{2,10},{4,12},{6,14},{8,0},{10,2},{12,4},{14,6},{1,9},{3,11}... | collective-permute-start | bytes 368648 | tf_op jit(solution)/shard_map/gather_others/ppermute | solution.py:32
  24.9 9.0 %collective-permute-start.9 = (bf16[3,16,1280]{2,1,0:T(8,128)(2,1)S(1)}, bf16[3,16,1280]{2,1,0:T(8,128)(2,1)S(1)}, u32[]{:S(2)}, u32[]{:S(2)}) collective-permute-start(bf16[3,16,1280]{2,1,0:T(8,128)(2,1)S(1)} %pad_maximum_fusion.7), channel_id=1, source_target_pairs={{0,12},{2,14},{4,0},{6,2},{8,4},{10,6},{12,8},{14,10},{1,13},{3,15... | collective-permute-start | bytes 368648 | tf_op jit(solution)/shard_map/gather_others/ppermute | solution.py:32
  25.5 14.4 %collective-permute-start.5 = (bf16[128,1920]{1,0:T(8,128)(2,1)S(1)}, bf16[128,1920]{1,0:T(8,128)(2,1)S(1)}, u32[]{:S(2)}, u32[]{:S(2)}) collective-permute-start(bf16[128,1920]{1,0:T(8,128)(2,1)S(1)} %get-tuple-element.64.own), channel_id=1, source_target_pairs={{0,1},{1,0},{2,3},{3,2},{4,5},{5,4},{6,7},{7,6},{8,9},{9,8},{10,11... | collective-permute-start | bytes 1474568 | tf_op jit(solution)/shard_map/swap_chain0/ppermute | solution.py:84
  33.9 1.5 %collective-permute-start.10 = (bf16[64,1280]{1,0:T(8,128)(2,1)S(1)}, bf16[64,1280]{1,0:T(8,128)(2,1)S(1)}, u32[]{:S(2)}, u32[]{:S(2)}) collective-permute-start(bf16[64,1280]{1,0:T(8,128)(2,1)S(1)} %pad_maximum_fusion.3.low.refs_5_), channel_id=1, source_target_pairs={{0,2},{2,0},{4,6},{6,4},{8,10},{10,8},{12,14},{14,12},{1,3},{3,1},... | collective-permute-start | bytes 491528 | tf_op jit(solution)/shard_map/gather_others/ppermute | solution.py:27
  34.0 1.6 %collective-permute-start.11 = (bf16[64,1280]{1,0:T(8,128)(2,1)S(1)}, bf16[64,1280]{1,0:T(8,128)(2,1)S(1)}, u32[]{:S(2)}, u32[]{:S(2)}) collective-permute-start(bf16[64,1280]{1,0:T(8,128)(2,1)S(1)} %pad_maximum_fusion.4.grad_low.refs_9_), channel_id=1, source_target_pairs={{0,2},{2,0},{4,6},{6,4},{8,10},{10,8},{12,14},{14,12},{1,3},{3,1},... | collective-permute-start | bytes 491528 | tf_op jit(solution)/shard_map/gather_others/ppermute | solution.py:27
  34.6 3.0 %collective-permute-start.12 = (bf16[64,1280]{1,0:T(8,128)(2,1)S(1)}, bf16[64,1280]{1,0:T(8,128)(2,1)S(1)}, u32[]{:S(2)}, u32[]{:S(2)}) collective-permute-start(bf16[64,1280]{1,0:T(8,128)(2,1)S(1)} %pad_maximum_fusion.5.low), channel_id=1, source_target_pairs={{0,2},{2,0},{4,6},{6,4},{8,10},{10,8},{12,14},{14,12},{1,3},{3,1},... | collective-permute-start | bytes 491528 | tf_op jit(solution)/shard_map/gather_others/ppermute | solution.py:27
  40.9 1.6 %collective-permute-start.13 = (bf16[64,1280]{1,0:T(8,128)(2,1)S(1)}, bf16[64,1280]{1,0:T(8,128)(2,1)S(1)}, u32[]{:S(2)}, u32[]{:S(2)}) collective-permute-start(bf16[64,1280]{1,0:T(8,128)(2,1)S(1)} %get-tuple-element.77), channel_id=1, source_target_pairs={{0,2},{2,0},{4,6},{6,4},{8,10},{10,8},{12,14},{14,12},{1,3},{3,1},... | collective-permute-start | bytes 491528 | tf_op jit(solution)/shard_map/chain0/ppermute | solution.py:27
  41.0 23.9 %collective-permute-start.22 = (bf16[128,3712]{1,0:T(8,128)(2,1)S(1)}, bf16[128,3712]{1,0:T(8,128)(2,1)S(1)}, u32[]{:S(2)}, u32[]{:S(2)}) collective-permute-start(bf16[128,3712]{1,0:T(8,128)(2,1)S(1)} %products_and_act_grads.1.refs_0_.own), channel_id=1, source_target_pairs={{0,1},{1,0},{2,3},{3,2},{4,5},{5,4},{6,7},{7,6},{8,9},{9,8},{10,11... | collective-permute-start | bytes 2850824 | tf_op jit(solution)/shard_map/swap_off_back/ppermute | solution.py:84
  42.6 6.0 %collective-permute-start.16 = (bf16[16,1280]{1,0:T(8,128)(2,1)S(1)}, bf16[16,1280]{1,0:T(8,128)(2,1)S(1)}, u32[]{:S(2)}, u32[]{:S(2)}) collective-permute-start(bf16[16,1280]{1,0:T(8,128)(2,1)S(1)} %get-tuple-element.119), channel_id=1, source_target_pairs={{0,4},{2,6},{4,8},{6,10},{8,12},{10,14},{12,0},{14,2},{1,5},{3,7},... | collective-permute-start | bytes 122888 | tf_op jit(solution)/shard_map/chain0/ppermute | solution.py:32
  44.3 5.7 %collective-permute-start.15 = (bf16[16,1280]{1,0:T(8,128)(2,1)S(1)}, bf16[16,1280]{1,0:T(8,128)(2,1)S(1)}, u32[]{:S(2)}, u32[]{:S(2)}) collective-permute-start(bf16[16,1280]{1,0:T(8,128)(2,1)S(1)} %get-tuple-element.120), channel_id=1, source_target_pairs={{0,8},{2,10},{4,12},{6,14},{8,0},{10,2},{12,4},{14,6},{1,9},{3,11}... | collective-permute-start | bytes 122888 | tf_op jit(solution)/shard_map/chain0/ppermute | solution.py:32
  46.1 4.1 %collective-permute-start.14 = (bf16[16,1280]{1,0:T(8,128)(2,1)S(1)}, bf16[16,1280]{1,0:T(8,128)(2,1)S(1)}, u32[]{:S(2)}, u32[]{:S(2)}) collective-permute-start(bf16[16,1280]{1,0:T(8,128)(2,1)S(1)} %get-tuple-element.118), channel_id=1, source_target_pairs={{0,12},{2,14},{4,0},{6,2},{8,4},{10,6},{12,8},{14,10},{1,13},{3,15... | collective-permute-start | bytes 122888 | tf_op jit(solution)/shard_map/chain0/ppermute | solution.py:32
  46.7 28.7 %collective-permute-start.24 = (bf16[128,1920]{1,0:T(8,128)(2,1)S(1)}, bf16[128,1920]{1,0:T(8,128)(2,1)S(1)}, u32[]{:S(2)}, u32[]{:S(2)}) collective-permute-start(bf16[128,1920]{1,0:T(8,128)(2,1)S(1)} %products.3.refs_1_.own), channel_id=1, source_target_pairs={{0,1},{1,0},{2,3},{3,2},{4,5},{5,4},{6,7},{7,6},{8,9},{9,8},{10,11... | collective-permute-start | bytes 1474568 | tf_op jit(solution)/shard_map/swap_off_forward/ppermute | solution.py:84
  50.3 6.7 %collective-permute-start.20 = (bf16[1,16,1280]{2,1,0:T(8,128)(2,1)S(1)}, bf16[1,16,1280]{2,1,0:T(8,128)(2,1)S(1)}, u32[]{:S(2)}, u32[]{:S(2)}) collective-permute-start(bf16[1,16,1280]{2,1,0:T(8,128)(2,1)S(1)} %bitcast.105), channel_id=1, source_target_pairs={{0,28},{2,30},{4,16},{6,18},{8,20},{10,22},{12,24},{14,26},{16,12}... | collective-permute-start | bytes 122888 | tf_op jit(solution)/shard_map/pass/ppermute | solution.py:50
  55.4 5.9 %collective-permute-start.19 = (bf16[1,16,1280]{2,1,0:T(8,128)(2,1)S(1)}, bf16[1,16,1280]{2,1,0:T(8,128)(2,1)S(1)}, u32[]{:S(2)}, u32[]{:S(2)}) collective-permute-start(bf16[1,16,1280]{2,1,0:T(8,128)(2,1)S(1)} %bitcast.106), channel_id=1, source_target_pairs={{0,24},{2,26},{4,28},{6,30},{8,16},{10,18},{12,20},{14,22},{16,8},... | collective-permute-start | bytes 122888 | tf_op jit(solution)/shard_map/pass/ppermute | solution.py:50
  55.4 6.7 %collective-permute-start.18 = (bf16[1,16,1280]{2,1,0:T(8,128)(2,1)S(1)}, bf16[1,16,1280]{2,1,0:T(8,128)(2,1)S(1)}, u32[]{:S(2)}, u32[]{:S(2)}) collective-permute-start(bf16[1,16,1280]{2,1,0:T(8,128)(2,1)S(1)} %bitcast.107), channel_id=1, source_target_pairs={{0,20},{2,22},{4,24},{6,26},{8,28},{10,30},{12,16},{14,18},{16,4},... | collective-permute-start | bytes 122888 | tf_op jit(solution)/shard_map/pass/ppermute | solution.py:50
  57.0 5.0 %collective-permute-start.17 = (bf16[1,16,1280]{2,1,0:T(8,128)(2,1)S(1)}, bf16[1,16,1280]{2,1,0:T(8,128)(2,1)S(1)}, u32[]{:S(2)}, u32[]{:S(2)}) collective-permute-start(bf16[1,16,1280]{2,1,0:T(8,128)(2,1)S(1)} %bitcast.108), channel_id=1, source_target_pairs={{0,16},{2,18},{4,20},{6,22},{8,24},{10,26},{12,28},{14,30},{16,0},... | collective-permute-start | bytes 122888 | tf_op jit(solution)/shard_map/pass/ppermute | solution.py:50
  62.1 5.1 %collective-permute-start.21 = (bf16[64,1280]{1,0:T(8,128)(2,1)S(1)}, bf16[64,1280]{1,0:T(8,128)(2,1)S(1)}, u32[]{:S(2)}, u32[]{:S(2)}) collective-permute-start(bf16[64,1280]{1,0:T(8,128)(2,1)S(1)} %pad_maximum_fusion.6.low), channel_id=1, source_target_pairs={{0,2},{2,0},{4,6},{6,4},{8,10},{10,8},{12,14},{14,12},{1,3},{3,1},... | collective-permute-start | bytes 491528 | tf_op jit(solution)/shard_map/pass/ppermute | solution.py:27
  67.1 9.5 %collective-permute-start.23 = (bf16[64,1280]{1,0:T(8,128)(2,1)S(1)}, bf16[64,1280]{1,0:T(8,128)(2,1)S(1)}, u32[]{:S(2)}, u32[]{:S(2)}) collective-permute-start(bf16[64,1280]{1,0:T(8,128)(2,1)S(1)} %get-tuple-element.80), channel_id=1, source_target_pairs={{0,2},{2,0},{4,6},{6,4},{8,10},{10,8},{12,14},{14,12},{1,3},{3,1},... | collective-permute-start | bytes 491528 | tf_op jit(solution)/shard_map/off_back/ppermute | solution.py:27
  68.9 16.6 %collective-permute-start.29 = (bf16[128,1920]{1,0:T(8,128)(2,1)S(1)}, bf16[128,1920]{1,0:T(8,128)(2,1)S(1)}, u32[]{:S(2)}, u32[]{:S(2)}) collective-permute-start(bf16[128,1920]{1,0:T(8,128)(2,1)S(1)} %get-tuple-element.82.refs_0_.own), channel_id=1, source_target_pairs={{0,1},{1,0},{2,3},{3,2},{4,5},{5,4},{6,7},{7,6},{8,9},{9,8},{10,11... | collective-permute-start | bytes 1474568 | tf_op jit(solution)/shard_map/swap_chain1/ppermute | solution.py:84
  76.5 1.5 %collective-permute-start.25 = (bf16[64,1280]{1,0:T(8,128)(2,1)S(1)}, bf16[64,1280]{1,0:T(8,128)(2,1)S(1)}, u32[]{:S(2)}, u32[]{:S(2)}) collective-permute-start(bf16[64,1280]{1,0:T(8,128)(2,1)S(1)} %get-tuple-element.84), channel_id=1, source_target_pairs={{0,2},{2,0},{4,6},{6,4},{8,10},{10,8},{12,14},{14,12},{1,3},{3,1},... | collective-permute-start | bytes 491528 | tf_op jit(solution)/shard_map/off_forward/ppermute | solution.py:27
  78.1 11.8 %collective-permute-start.26 = (bf16[2,16,1280]{2,1,0:T(8,128)(2,1)S(1)}, bf16[2,16,1280]{2,1,0:T(8,128)(2,1)S(1)}, u32[]{:S(2)}, u32[]{:S(2)}) collective-permute-start(bf16[2,16,1280]{2,1,0:T(8,128)(2,1)S(1)} %get-tuple-element.111), channel_id=1, source_target_pairs={{0,12},{2,14},{4,0},{6,2},{8,4},{10,6},{12,8},{14,10},{1,13},{3,15... | collective-permute-start | bytes 245768 | tf_op jit(solution)/shard_map/off_forward/ppermute | solution.py:32
  81.0 8.8 %collective-permute-start.27 = (bf16[2,16,1280]{2,1,0:T(8,128)(2,1)S(1)}, bf16[2,16,1280]{2,1,0:T(8,128)(2,1)S(1)}, u32[]{:S(2)}, u32[]{:S(2)}) collective-permute-start(bf16[2,16,1280]{2,1,0:T(8,128)(2,1)S(1)} %get-tuple-element.110), channel_id=1, source_target_pairs={{0,8},{2,10},{4,12},{6,14},{8,0},{10,2},{12,4},{14,6},{1,9},{3,11}... | collective-permute-start | bytes 245768 | tf_op jit(solution)/shard_map/off_forward/ppermute | solution.py:32
  81.6 8.2 %collective-permute-start.28 = (bf16[2,16,1280]{2,1,0:T(8,128)(2,1)S(1)}, bf16[2,16,1280]{2,1,0:T(8,128)(2,1)S(1)}, u32[]{:S(2)}, u32[]{:S(2)}) collective-permute-start(bf16[2,16,1280]{2,1,0:T(8,128)(2,1)S(1)} %get-tuple-element.109), channel_id=1, source_target_pairs={{0,4},{2,6},{4,8},{6,10},{8,12},{10,14},{12,0},{14,2},{1,5},{3,7},... | collective-permute-start | bytes 245768 | tf_op jit(solution)/shard_map/off_forward/ppermute | solution.py:32
  87.7 17.5 %copy-start.1 = (f32[1,1,1,6,128,128]{5,4,3,2,1,0:T(8,128)S(1)}, f32[1,1,1,6,128,128]{5,4,3,2,1,0:T(8,128)}, u32[]{:S(2)}) copy-start(f32[1,1,1,6,128,128]{5,4,3,2,1,0:T(8,128)} %param.26) | copy-start | bytes 1179652
  87.7 17.5 %copy-start.2 = (f32[1,1,1,6,128,128]{5,4,3,2,1,0:T(8,128)S(1)}, f32[1,1,1,6,128,128]{5,4,3,2,1,0:T(8,128)}, u32[]{:S(2)}) copy-start(f32[1,1,1,6,128,128]{5,4,3,2,1,0:T(8,128)} %param.27) | copy-start | bytes 1179652
  89.8 1.5 %collective-permute-start.30 = (bf16[64,1280]{1,0:T(8,128)(2,1)S(1)}, bf16[64,1280]{1,0:T(8,128)(2,1)S(1)}, u32[]{:S(2)}, u32[]{:S(2)}) collective-permute-start(bf16[64,1280]{1,0:T(8,128)(2,1)S(1)} %get-tuple-element.97), channel_id=1, source_target_pairs={{0,2},{2,0},{4,6},{6,4},{8,10},{10,8},{12,14},{14,12},{1,3},{3,1},... | collective-permute-start | bytes 491528 | tf_op jit(solution)/shard_map/chain1/ppermute | solution.py:27
  89.9 4.7 %collective-permute-start.34 = (bf16[4,128,128]{2,1,0:T(8,128)(2,1)S(1)}, bf16[4,128,128]{2,1,0:T(8,128)(2,1)S(1)}, u32[]{:S(2)}, u32[]{:S(2)}) collective-permute-start(bf16[4,128,128]{2,1,0:T(8,128)(2,1)S(1)} %slice.206), channel_id=1, source_target_pairs={{0,2},{2,0},{4,6},{6,4},{8,10},{10,8},{12,14},{14,12},{1,3},{3,1},... | collective-permute-start | bytes 393224 | tf_op jit(solution)/shard_map/block_exchange/ppermute | solution.py:27
  91.4 7.3 %collective-permute-start.31 = (bf16[16,1280]{1,0:T(8,128)(2,1)S(1)}, bf16[16,1280]{1,0:T(8,128)(2,1)S(1)}, u32[]{:S(2)}, u32[]{:S(2)}) collective-permute-start(bf16[16,1280]{1,0:T(8,128)(2,1)S(1)} %get-tuple-element.117), channel_id=1, source_target_pairs={{0,12},{2,14},{4,0},{6,2},{8,4},{10,6},{12,8},{14,10},{1,13},{3,15... | collective-permute-start | bytes 122888 | tf_op jit(solution)/shard_map/chain1/ppermute | solution.py:32
  93.7 5.7 %collective-permute-start.32 = (bf16[16,1280]{1,0:T(8,128)(2,1)S(1)}, bf16[16,1280]{1,0:T(8,128)(2,1)S(1)}, u32[]{:S(2)}, u32[]{:S(2)}) collective-permute-start(bf16[16,1280]{1,0:T(8,128)(2,1)S(1)} %get-tuple-element.116), channel_id=1, source_target_pairs={{0,8},{2,10},{4,12},{6,14},{8,0},{10,2},{12,4},{14,6},{1,9},{3,11}... | collective-permute-start | bytes 122888 | tf_op jit(solution)/shard_map/chain1/ppermute | solution.py:32
  94.6 6.3 %collective-permute-start.33 = (bf16[16,1280]{1,0:T(8,128)(2,1)S(1)}, bf16[16,1280]{1,0:T(8,128)(2,1)S(1)}, u32[]{:S(2)}, u32[]{:S(2)}) collective-permute-start(bf16[16,1280]{1,0:T(8,128)(2,1)S(1)} %get-tuple-element.115), channel_id=1, source_target_pairs={{0,4},{2,6},{4,8},{6,10},{8,12},{10,14},{12,0},{14,2},{1,5},{3,7},... | collective-permute-start | bytes 122888 | tf_op jit(solution)/shard_map/chain1/ppermute | solution.py:32
  94.6 7.0 %collective-permute-start.35 = (bf16[256,128]{1,0:T(8,128)(2,1)S(1)}, bf16[256,128]{1,0:T(8,128)(2,1)S(1)}, u32[]{:S(2)}, u32[]{:S(2)}) collective-permute-start(bf16[256,128]{1,0:T(8,128)(2,1)S(1)} %pad_maximum_fusion.8), channel_id=1, source_target_pairs={{0,12},{2,14},{4,0},{6,2},{8,4},{10,6},{12,8},{14,10},{1,13},{3,15... | collective-permute-start | bytes 196616 | tf_op jit(solution)/shard_map/block_exchange/ppermute | solution.py:32
  98.5 6.6 %collective-permute-start.36 = (bf16[256,128]{1,0:T(8,128)(2,1)S(1)}, bf16[256,128]{1,0:T(8,128)(2,1)S(1)}, u32[]{:S(2)}, u32[]{:S(2)}) collective-permute-start(bf16[256,128]{1,0:T(8,128)(2,1)S(1)} %pad_maximum_fusion.9), channel_id=1, source_target_pairs={{0,8},{2,10},{4,12},{6,14},{8,0},{10,2},{12,4},{14,6},{1,9},{3,11}... | collective-permute-start | bytes 196616 | tf_op jit(solution)/shard_map/block_exchange/ppermute | solution.py:32
  98.7 6.4 %collective-permute-start.37 = (bf16[256,128]{1,0:T(8,128)(2,1)S(1)}, bf16[256,128]{1,0:T(8,128)(2,1)S(1)}, u32[]{:S(2)}, u32[]{:S(2)}) collective-permute-start(bf16[256,128]{1,0:T(8,128)(2,1)S(1)} %pad_maximum_fusion.10), channel_id=1, source_target_pairs={{0,4},{2,6},{4,8},{6,10},{8,12},{10,14},{12,0},{14,2},{1,5},{3,7},... | collective-permute-start | bytes 196616 | tf_op jit(solution)/shard_map/block_exchange/ppermute | solution.py:32

commit v5 on v3

--- a/solution.py
+++ b/solution.py
@@ -654,7 +654,7 @@
 
     with jax.named_scope("chain0"):
         kept, sent, scaled, activated = leave(
-            width, 1, flag, parts, back_parts, back_halves, gain, up, down, [], [off_product, off_forward]
+            width, 1, flag, parts, back_parts, back_halves, gain, up, down, [], [off_product]
         )
         chained = added(first[1], scatter_parts(scatter_pairs(kept, sent)))
     with jax.named_scope("off_back"):

time: 108 us -> 108 us (level)
    ppermute x5, waiting for transfers between devices: 12.9 us -> 14 us  [tensor_parts(): got = lax.ppermute(value, 'tensor', [(t, t ^ step) for t in range(count)])]
where the time goes in v5:
time: 108 us
  starting transfers between devices  42.2 us (39%)
  waiting for transfers between devices  37 us (34%)
  Pallas kernels  23.7 us (22%)
  local copies, waits for them, and re-layouts  2.44 us (2%)
  between operations  1.93 us (2%)
    ppermute x18, starting transfers between devices, shifted(): lax.ppermute(value, 'dp', [(d, (d + 2 * steps) % count) for d in range(co...  26 us
    ppermute x18, waiting for transfers between devices, shifted(): lax.ppermute(value, 'dp', [(d, (d + 2 * steps) % count) for d in range(co...  16.7 us
    ppermute x5, waiting for transfers between devices, tensor_parts(): got = lax.ppermute(value, 'tensor', [(t, t ^ step) for t in range(count)])  14 us
    pallas_call x9, Pallas kernels, call(): pl.pallas_call(kernel, out_shape=outs, in_specs=specs, out_specs=[VMEM] *...  12.9 us
    ppermute x4, starting transfers between devices, moved(): return lax.ppermute(local, ('section', 'dp'), pairs)  7.48 us
    ppermute x5, starting transfers between devices, tensor_parts(): got = lax.ppermute(value, 'tensor', [(t, t ^ step) for t in range(count)])  6.03 us
    pallas_call x2, Pallas kernels, load_one(): pl.pallas_call(load_one_kernel, out_shape=pltpu.VMEM(weight.shape, BF16),...  4.65 us
    ppermute x4, waiting for transfers between devices, moved(): return lax.ppermute(local, ('section', 'dp'), pairs)  3.54 us
  transfers between devices with their start and end apart: 38, of which 19 were waited for; matrix products, arithmetic and copies ran while one was open for 3% of the time, Pallas kernels for 18%

profile of v5, /device:TPU:0, one launch (start us, length us, event | category | flops | bytes accessed | tf_op | source)
XLA Modules:
  0.0 107.8 jit_solution(15631438352433023688)
XLA Ops:
  0.6 0.8 first_rows.1.refs_0_
  1.5 3.1 %collective-permute-start = (bf16[2,16,1280]{2,1,0:T(8,128)(2,1)S(1)}, bf16[2,16,1280]{2,1,0:T(8,128)(2,1)S(1)}, u32[]{:S(2)}, u32[]{:S(2)}) collective-permute-start(bf16[2,16,1280]{2,1,0:T(8,128)(2,1)S(1)} %first_rows.1.refs_0_), channel_id=1, source_target_pairs={{0,4},{2,6},{4,8},{6,10},{8,12},{10,14},{12,0},{14,2},{1,5},{3,7},... | collective-permute-start | bytes 245768 | tf_op jit(solution)/shard_map/gather_first/ppermute | solution.py:32
  4.5 2.6 %collective-permute-start.1 = (bf16[2,16,1280]{2,1,0:T(8,128)(2,1)S(1)}, bf16[2,16,1280]{2,1,0:T(8,128)(2,1)S(1)}, u32[]{:S(2)}, u32[]{:S(2)}) collective-permute-start(bf16[2,16,1280]{2,1,0:T(8,128)(2,1)S(1)} %first_rows.1.refs_0_), channel_id=1, source_target_pairs={{0,8},{2,10},{4,12},{6,14},{8,0},{10,2},{12,4},{14,6},{1,9},{3,11}... | collective-permute-start | bytes 245768 | tf_op jit(solution)/shard_map/gather_first/ppermute | solution.py:32
  7.1 1.3 %collective-permute-start.2 = (bf16[2,16,1280]{2,1,0:T(8,128)(2,1)S(1)}, bf16[2,16,1280]{2,1,0:T(8,128)(2,1)S(1)}, u32[]{:S(2)}, u32[]{:S(2)}) collective-permute-start(bf16[2,16,1280]{2,1,0:T(8,128)(2,1)S(1)} %first_rows.1.refs_0_), channel_id=1, source_target_pairs={{0,12},{2,14},{4,0},{6,2},{8,4},{10,6},{12,8},{14,10},{1,13},{3,15... | collective-permute-start | bytes 245768 | tf_op jit(solution)/shard_map/gather_first/ppermute | solution.py:32
  8.5 0.8 copy.22
  10.8 2.3 %load_weight.2.up._ = bf16[1280,1792]{1,0:T(8,128)(2,1)S(1)} custom-call(bf16[1280,1792]{1,0:T(8,128)(2,1)} %bitcast.115, bf16[2,16,1280]{2,1,0:T(8,128)(2,1)S(1)} %first_rows.1.refs_0_, s32[8,14]{1,0:T(8,128)S(1)} %pad_add_fusion.refs_1_.plan), custom_call_target="tpu_custom_call" | custom-call | tf_op jit(solution)/shard_map/load_weight/pallas_call | solution.py:132
  15.0 0.8 products.2.refs_0_.back_own
  15.8 1.6 %collective-permute-start.6 = (bf16[128,1920]{1,0:T(8,128)(2,1)S(1)}, bf16[128,1920]{1,0:T(8,128)(2,1)S(1)}, u32[]{:S(2)}, u32[]{:S(2)}) collective-permute-start(bf16[128,1920]{1,0:T(8,128)(2,1)S(1)} %products.2.refs_0_.back_own), channel_id=1, source_target_pairs={{0,1},{1,0},{2,3},{3,2},{4,5},{5,4},{6,7},{7,6},{8,9},{9,8},{10,11... | collective-permute-start | bytes 1474568 | tf_op jit(solution)/shard_map/swap_back/ppermute | solution.py:84
  17.3 2.3 %load_weight.3.down._.refs_0_ = bf16[1792,1280]{1,0:T(8,128)(2,1)S(1)} custom-call(bf16[1792,1280]{1,0:T(8,128)(2,1)} %bitcast.116, bf16[128,1920]{1,0:T(8,128)(2,1)S(1)} %products.2.refs_0_.back_own), custom_call_target="tpu_custom_call" | custom-call | tf_op jit(solution)/shard_map/load_weight/pallas_call | solution.py:132
  19.7 1.5 %enter.2 = (bf16[128,1920]{1,0:T(8,128)(2,1)S(1)}, bf16[128,1280]{1,0:T(8,128)(2,1)}) custom-call(s32[1]{0:T(128)} %bitcast.flag, bf16[64,1280]{1,0:T(8,128)(2,1)S(1)} %pad_maximum_fusion.1.low.other_low, bf16[64,1280]{1,0:T(8,128)(2,1)S(1)} %collective-permute-done.3.high.other_high, bf16[64,1280]{1,0:T(8,128)(2,1)S(1)} %pad_maximum_fusion.1.low.other_low, ...), custom_call_target="tpu_custom_call" | custom-call | flops 1 | bytes 1 | tf_op jit(solution)/shard_map/enter/pallas_call | solution.py:96
  21.3 1.7 %collective-permute-start.7 = (bf16[3,16,1280]{2,1,0:T(8,128)(2,1)S(1)}, bf16[3,16,1280]{2,1,0:T(8,128)(2,1)S(1)}, u32[]{:S(2)}, u32[]{:S(2)}) collective-permute-start(bf16[3,16,1280]{2,1,0:T(8,128)(2,1)S(1)} %pad_maximum_fusion.7), channel_id=1, source_target_pairs={{0,4},{2,6},{4,8},{6,10},{8,12},{10,14},{12,0},{14,2},{1,5},{3,7},... | collective-permute-start | bytes 368648 | tf_op jit(solution)/shard_map/gather_others/ppermute | solution.py:32
  23.0 1.9 %collective-permute-start.8 = (bf16[3,16,1280]{2,1,0:T(8,128)(2,1)S(1)}, bf16[3,16,1280]{2,1,0:T(8,128)(2,1)S(1)}, u32[]{:S(2)}, u32[]{:S(2)}) collective-permute-start(bf16[3,16,1280]{2,1,0:T(8,128)(2,1)S(1)} %pad_maximum_fusion.7), channel_id=1, source_target_pairs={{0,8},{2,10},{4,12},{6,14},{8,0},{10,2},{12,4},{14,6},{1,9},{3,11}... | collective-permute-start | bytes 368648 | tf_op jit(solution)/shard_map/gather_others/ppermute | solution.py:32
  26.0 3.5 %collective-permute-done.7 = bf16[3,16,1280]{2,1,0:T(8,128)(2,1)S(1)} collective-permute-done((bf16[3,16,1280]{2,1,0:T(8,128)(2,1)S(1)}, bf16[3,16,1280]{2,1,0:T(8,128)(2,1)S(1)}, u32[]{:S(2)}, u32[]{:S(2)}) %collective-permute-start.7) | collective-permute-done | bytes 122912 | tf_op jit(solution)/shard_map/gather_others/ppermute | solution.py:32
  29.5 4.4 %collective-permute-done.8 = bf16[3,16,1280]{2,1,0:T(8,128)(2,1)S(1)} collective-permute-done((bf16[3,16,1280]{2,1,0:T(8,128)(2,1)S(1)}, bf16[3,16,1280]{2,1,0:T(8,128)(2,1)S(1)}, u32[]{:S(2)}, u32[]{:S(2)}) %collective-permute-start.8) | collective-permute-done | bytes 122912 | tf_op jit(solution)/shard_map/gather_others/ppermute | solution.py:32
  34.6 0.8 collective-permute-done.10.high.refs_6_
  35.6 2.0 %products_and_act_grads.1.refs_0_.own = bf16[128,3712]{1,0:T(8,128)(2,1)S(1)} custom-call(bf16[64,1280]{1,0:T(8,128)(2,1)S(1)} %pad_maximum_fusion.3.low.refs_5_, bf16[64,1280]{1,0:T(8,128)(2,1)S(1)} %collective-permute-done.10.high.refs_6_, bf16[64,1280]{1,0:T(8,128)(2,1)S(1)} %pad_maximum_fusion.4.grad_low.refs_9_, ...), custom_call_target="tpu_custom_call" | custom-call | flops 1 | bytes 1 | tf_op jit(solution)/shard_map/products_and_act_grads/pallas_call | solution.py:96
  37.6 2.2 %collective-permute-done.5.got = bf16[128,1920]{1,0:T(8,128)(2,1)S(1)} collective-permute-done((bf16[128,1920]{1,0:T(8,128)(2,1)S(1)}, bf16[128,1920]{1,0:T(8,128)(2,1)S(1)}, u32[]{:S(2)}, u32[]{:S(2)}) %collective-permute-start.5) | collective-permute-done | bytes 491552 | tf_op jit(solution)/shard_map/swap_chain0/ppermute | solution.py:84
  39.8 1.1 leave.2
  41.6 1.5 %collective-permute-start.21 = (bf16[128,3712]{1,0:T(8,128)(2,1)S(1)}, bf16[128,3712]{1,0:T(8,128)(2,1)S(1)}, u32[]{:S(2)}, u32[]{:S(2)}) collective-permute-start(bf16[128,3712]{1,0:T(8,128)(2,1)S(1)} %products_and_act_grads.1.refs_0_.own), channel_id=1, source_target_pairs={{0,1},{1,0},{2,3},{3,2},{4,5},{5,4},{6,7},{7,6},{8,9},{9,8},{10,11... | collective-permute-start | bytes 2850824 | tf_op jit(solution)/shard_map/swap_off_back/ppermute | solution.py:84
  43.1 1.7 %collective-permute-start.15 = (bf16[16,1280]{1,0:T(8,128)(2,1)S(1)}, bf16[16,1280]{1,0:T(8,128)(2,1)S(1)}, u32[]{:S(2)}, u32[]{:S(2)}) collective-permute-start(bf16[16,1280]{1,0:T(8,128)(2,1)S(1)} %get-tuple-element.121), channel_id=1, source_target_pairs={{0,4},{2,6},{4,8},{6,10},{8,12},{10,14},{12,0},{14,2},{1,5},{3,7},... | collective-permute-start | bytes 122888 | tf_op jit(solution)/shard_map/chain0/ppermute | solution.py:32
  44.8 1.9 %collective-permute-start.14 = (bf16[16,1280]{1,0:T(8,128)(2,1)S(1)}, bf16[16,1280]{1,0:T(8,128)(2,1)S(1)}, u32[]{:S(2)}, u32[]{:S(2)}) collective-permute-start(bf16[16,1280]{1,0:T(8,128)(2,1)S(1)} %get-tuple-element.122), channel_id=1, source_target_pairs={{0,8},{2,10},{4,12},{6,14},{8,0},{10,2},{12,4},{14,6},{1,9},{3,11}... | collective-permute-start | bytes 122888 | tf_op jit(solution)/shard_map/chain0/ppermute | solution.py:32
  47.2 0.8 products.3.own
  48.0 0.9 collective-permute-start.24
  49.0 1.4 %collective-permute-done.14 = bf16[16,1280]{1,0:T(8,128)(2,1)S(1)} collective-permute-done((bf16[16,1280]{1,0:T(8,128)(2,1)S(1)}, bf16[16,1280]{1,0:T(8,128)(2,1)S(1)}, u32[]{:S(2)}, u32[]{:S(2)}) %collective-permute-start.14) | collective-permute-done | bytes 40992 | tf_op jit(solution)/shard_map/chain0/ppermute | solution.py:32
  50.8 4.3 %collective-permute-start.19 = (bf16[1,16,1280]{2,1,0:T(8,128)(2,1)S(1)}, bf16[1,16,1280]{2,1,0:T(8,128)(2,1)S(1)}, u32[]{:S(2)}, u32[]{:S(2)}) collective-permute-start(bf16[1,16,1280]{2,1,0:T(8,128)(2,1)S(1)} %bitcast.105), channel_id=1, source_target_pairs={{0,28},{2,30},{4,16},{6,18},{8,20},{10,22},{12,24},{14,26},{16,12}... | collective-permute-start | bytes 122888 | tf_op jit(solution)/shard_map/pass/ppermute | solution.py:50
  55.2 1.6 %collective-permute-start.17 = (bf16[1,16,1280]{2,1,0:T(8,128)(2,1)S(1)}, bf16[1,16,1280]{2,1,0:T(8,128)(2,1)S(1)}, u32[]{:S(2)}, u32[]{:S(2)}) collective-permute-start(bf16[1,16,1280]{2,1,0:T(8,128)(2,1)S(1)} %bitcast.107), channel_id=1, source_target_pairs={{0,20},{2,22},{4,24},{6,26},{8,28},{10,30},{12,16},{14,18},{16,4},... | collective-permute-start | bytes 122888 | tf_op jit(solution)/shard_map/pass/ppermute | solution.py:50
  56.8 1.5 %collective-permute-start.16 = (bf16[1,16,1280]{2,1,0:T(8,128)(2,1)S(1)}, bf16[1,16,1280]{2,1,0:T(8,128)(2,1)S(1)}, u32[]{:S(2)}, u32[]{:S(2)}) collective-permute-start(bf16[1,16,1280]{2,1,0:T(8,128)(2,1)S(1)} %bitcast.108), channel_id=1, source_target_pairs={{0,16},{2,18},{4,20},{6,22},{8,24},{10,26},{12,28},{14,30},{16,0},... | collective-permute-start | bytes 122888 | tf_op jit(solution)/shard_map/pass/ppermute | solution.py:50
  58.4 2.7 %collective-permute-done.18 = bf16[1,16,1280]{2,1,0:T(8,128)(2,1)S(1)} collective-permute-done((bf16[1,16,1280]{2,1,0:T(8,128)(2,1)S(1)}, bf16[1,16,1280]{2,1,0:T(8,128)(2,1)S(1)}, u32[]{:S(2)}, u32[]{:S(2)}) %collective-permute-start.18) | collective-permute-done | bytes 40992 | tf_op jit(solution)/shard_map/pass/ppermute | solution.py:50
  61.1 0.8 collective-permute-done.17
  62.0 3.5 %collective-permute-done.21.got = bf16[128,3712]{1,0:T(8,128)(2,1)S(1)} collective-permute-done((bf16[128,3712]{1,0:T(8,128)(2,1)S(1)}, bf16[128,3712]{1,0:T(8,128)(2,1)S(1)}, u32[]{:S(2)}, u32[]{:S(2)}) %collective-permute-start.21) | collective-permute-done | bytes 950304 | tf_op jit(solution)/shard_map/swap_off_back/ppermute | solution.py:84
  65.5 2.2 %backward.1 = (f32[64,1280]{1,0:T(8,128)S(1)}, bf16[64,1280]{1,0:T(8,128)(2,1)S(1)}, bf16[128,1792]{1,0:T(8,128)(2,1)S(1)}, bf16[128,1792]{1,0:T(8,128)(2,1)S(1)}) custom-call(bf16[128,3712]{1,0:T(8,128)(2,1)S(1)} %products_and_act_grads.1.refs_0_.own, bf16[128,3712]{1,0:T(8,128)(2,1)S(1)} %collective-permute-done.21.got, ...), custom_call_target="tpu_custom_call" | custom-call | flops 1 | bytes 1 | tf_op jit(solution)/shard_map/off_back/backward/pallas_call | solution.py:96
  67.7 1.8 %enter.3 = (bf16[128,1920]{1,0:T(8,128)(2,1)S(1)}, bf16[128,1280]{1,0:T(8,128)(2,1)S(1)}) custom-call(s32[1]{0:T(128)} %bitcast.flag, bf16[64,1280]{1,0:T(8,128)(2,1)S(1)} %pad_maximum_fusion.5.low, bf16[64,1280]{1,0:T(8,128)(2,1)S(1)} %collective-permute-done.20.high, bf16[64,1280]{1,0:T(8,128)(2,1)S(1)} %pad_maximum_fusion.1.low.other_low, ...), custom_call_target="tpu_custom_call" | custom-call | flops 1 | bytes 1 | tf_op jit(solution)/shard_map/enter/pallas_call | solution.py:96
  69.5 1.6 %collective-permute-start.29 = (bf16[128,1920]{1,0:T(8,128)(2,1)S(1)}, bf16[128,1920]{1,0:T(8,128)(2,1)S(1)}, u32[]{:S(2)}, u32[]{:S(2)}) collective-permute-start(bf16[128,1920]{1,0:T(8,128)(2,1)S(1)} %get-tuple-element.83.refs_0_.own), channel_id=1, source_target_pairs={{0,1},{1,0},{2,3},{3,2},{4,5},{5,4},{6,7},{7,6},{8,9},{9,8},{10,11... | collective-permute-start | bytes 1474568 | tf_op jit(solution)/shard_map/swap_chain1/ppermute | solution.py:84
  71.1 4.9 %collective-permute-done.24.got = bf16[128,1920]{1,0:T(8,128)(2,1)S(1)} collective-permute-done((bf16[128,1920]{1,0:T(8,128)(2,1)S(1)}, bf16[128,1920]{1,0:T(8,128)(2,1)S(1)}, u32[]{:S(2)}, u32[]{:S(2)}) %collective-permute-start.24) | collective-permute-done | bytes 491552 | tf_op jit(solution)/shard_map/swap_off_forward/ppermute | solution.py:84
  76.0 1.1 forward.1
  77.2 1.3 %collective-permute-done.25 = bf16[64,1280]{1,0:T(8,128)(2,1)S(1)} collective-permute-done((bf16[64,1280]{1,0:T(8,128)(2,1)S(1)}, bf16[64,1280]{1,0:T(8,128)(2,1)S(1)}, u32[]{:S(2)}, u32[]{:S(2)}) %collective-permute-start.25) | collective-permute-done | bytes 163872 | tf_op jit(solution)/shard_map/off_forward/ppermute | solution.py:27
  78.6 3.0 %collective-permute-start.26 = (bf16[2,16,1280]{2,1,0:T(8,128)(2,1)S(1)}, bf16[2,16,1280]{2,1,0:T(8,128)(2,1)S(1)}, u32[]{:S(2)}, u32[]{:S(2)}) collective-permute-start(bf16[2,16,1280]{2,1,0:T(8,128)(2,1)S(1)} %get-tuple-element.113), channel_id=1, source_target_pairs={{0,12},{2,14},{4,0},{6,2},{8,4},{10,6},{12,8},{14,10},{1,13},{3,15... | collective-permute-start | bytes 245768 | tf_op jit(solution)/shard_map/off_forward/ppermute | solution.py:32
  82.3 3.3 %collective-permute-done.29.got = bf16[128,1920]{1,0:T(8,128)(2,1)S(1)} collective-permute-done((bf16[128,1920]{1,0:T(8,128)(2,1)S(1)}, bf16[128,1920]{1,0:T(8,128)(2,1)S(1)}, u32[]{:S(2)}, u32[]{:S(2)}) %collective-permute-start.29) | collective-permute-done | bytes 491552 | tf_op jit(solution)/shard_map/swap_chain1/ppermute | solution.py:84
  85.7 2.1 %leave.3 = (f32[64,1280]{1,0:T(8,128)S(1)}, bf16[64,1280]{1,0:T(8,128)(2,1)S(1)}, bf16[128,1792]{1,0:T(8,128)(2,1)S(1)}, bf16[128,1792]{1,0:T(8,128)(2,1)S(1)}) custom-call(s32[1]{0:T(128)} %bitcast.flag, bf16[128,1920]{1,0:T(8,128)(2,1)S(1)} %get-tuple-element.83.refs_0_.own, ...), custom_call_target="tpu_custom_call", output_to_operand_aliasing={{2}: (10, {}), {3}: (11, {})} | custom-call | flops 1 | bytes 1 | tf_op jit(solution)/shard_map/chain1/leave/pallas_call | solution.py:404
  87.8 1.8 %collective-permute-done.27.refs_2_ = bf16[2,16,1280]{2,1,0:T(8,128)(2,1)S(1)} collective-permute-done((bf16[2,16,1280]{2,1,0:T(8,128)(2,1)S(1)}, bf16[2,16,1280]{2,1,0:T(8,128)(2,1)S(1)}, u32[]{:S(2)}, u32[]{:S(2)}) %collective-permute-start.27) | collective-permute-done | bytes 81952 | tf_op jit(solution)/shard_map/off_forward/ppermute | solution.py:32
  89.6 2.1 %block_grads.1 = bf16[8,128,128]{2,1,0:T(8,128)(2,1)S(1)} custom-call(s32[8,14]{1,0:T(8,128)S(1)} %pad_add_fusion.refs_1_.plan, bf16[1,1280]{1,0:T(2,128)(2,1)S(1)} %copy-done, bf16[64,1280]{1,0:T(8,128)(2,1)S(1)} %pad_maximum_fusion.2.low.refs_0_, bf16[64,1280]{1,0:T(8,128)(2,1)S(1)} %collective-permute-done.4.high.refs_1_, ...), custom_call_target="tpu_custom_call" | custom-call | flops 1 | bytes 1 | tf_op jit(solution)/shard_map/block_exchange/block_grads/pallas_call | solution.py:96
  92.4 1.3 %collective-permute-start.31 = (bf16[16,1280]{1,0:T(8,128)(2,1)S(1)}, bf16[16,1280]{1,0:T(8,128)(2,1)S(1)}, u32[]{:S(2)}, u32[]{:S(2)}) collective-permute-start(bf16[16,1280]{1,0:T(8,128)(2,1)S(1)} %get-tuple-element.119), channel_id=1, source_target_pairs={{0,12},{2,14},{4,0},{6,2},{8,4},{10,6},{12,8},{14,10},{1,13},{3,15... | collective-permute-start | bytes 122888 | tf_op jit(solution)/shard_map/chain1/ppermute | solution.py:32
  94.4 1.9 %collective-permute-start.33 = (bf16[16,1280]{1,0:T(8,128)(2,1)S(1)}, bf16[16,1280]{1,0:T(8,128)(2,1)S(1)}, u32[]{:S(2)}, u32[]{:S(2)}) collective-permute-start(bf16[16,1280]{1,0:T(8,128)(2,1)S(1)} %get-tuple-element.117), channel_id=1, source_target_pairs={{0,4},{2,6},{4,8},{6,10},{8,12},{10,14},{12,0},{14,2},{1,5},{3,7},... | collective-permute-start | bytes 122888 | tf_op jit(solution)/shard_map/chain1/ppermute | solution.py:32
  96.3 1.9 %collective-permute-start.35 = (bf16[256,128]{1,0:T(8,128)(2,1)S(1)}, bf16[256,128]{1,0:T(8,128)(2,1)S(1)}, u32[]{:S(2)}, u32[]{:S(2)}) collective-permute-start(bf16[256,128]{1,0:T(8,128)(2,1)S(1)} %pad_maximum_fusion.8), channel_id=1, source_target_pairs={{0,12},{2,14},{4,0},{6,2},{8,4},{10,6},{12,8},{14,10},{1,13},{3,15... | collective-permute-start | bytes 196616 | tf_op jit(solution)/shard_map/block_exchange/ppermute | solution.py:32
  98.8 0.8 collective-permute-start.37
  99.7 0.9 collective-permute-done.33.refs_7_
  101.4 4.2 %collective-permute-done.36.refs_1_ = bf16[256,128]{1,0:T(8,128)(2,1)S(1)} collective-permute-done((bf16[256,128]{1,0:T(8,128)(2,1)S(1)}, bf16[256,128]{1,0:T(8,128)(2,1)S(1)}, u32[]{:S(2)}, u32[]{:S(2)}) %collective-permute-start.36) | collective-permute-done | bytes 65568 | tf_op jit(solution)/shard_map/block_exchange/ppermute | solution.py:32
  105.6 2.1 %adam_step.1 = (f32[6,128,128]{2,1,0:T(8,128)}, f32[6,128,128]{2,1,0:T(8,128)}, f32[6,128,128]{2,1,0:T(8,128)}) custom-call(s32[8,14]{1,0:T(8,128)S(1)} %pad_add_fusion.refs_1_.plan, bf16[4,128,128]{2,1,0:T(8,128)(2,1)S(1)} %collective-permute-done.34.relayed, bf16[256,128]{1,0:T(8,128)(2,1)S(1)} %collective-permute-done.35.refs_0_, ...), custom_call_target="tpu_custom_call" | custom-call | tf_op jit(solution)/shard_map/adam_step/pallas_call | solution.py:546
  (102 shorter events, 10.4 us)
Async XLA Ops:
  1.5 11.7 %collective-permute-start = (bf16[2,16,1280]{2,1,0:T(8,128)(2,1)S(1)}, bf16[2,16,1280]{2,1,0:T(8,128)(2,1)S(1)}, u32[]{:S(2)}, u32[]{:S(2)}) collective-permute-start(bf16[2,16,1280]{2,1,0:T(8,128)(2,1)S(1)} %first_rows.1.refs_0_), channel_id=1, source_target_pairs={{0,4},{2,6},{4,8},{6,10},{8,12},{10,14},{12,0},{14,2},{1,5},{3,7},... | collective-permute-start | bytes 245768 | tf_op jit(solution)/shard_map/gather_first/ppermute | solution.py:32
  4.5 8.6 %collective-permute-start.1 = (bf16[2,16,1280]{2,1,0:T(8,128)(2,1)S(1)}, bf16[2,16,1280]{2,1,0:T(8,128)(2,1)S(1)}, u32[]{:S(2)}, u32[]{:S(2)}) collective-permute-start(bf16[2,16,1280]{2,1,0:T(8,128)(2,1)S(1)} %first_rows.1.refs_0_), channel_id=1, source_target_pairs={{0,8},{2,10},{4,12},{6,14},{8,0},{10,2},{12,4},{14,6},{1,9},{3,11}... | collective-permute-start | bytes 245768 | tf_op jit(solution)/shard_map/gather_first/ppermute | solution.py:32
  7.1 6.1 %collective-permute-start.2 = (bf16[2,16,1280]{2,1,0:T(8,128)(2,1)S(1)}, bf16[2,16,1280]{2,1,0:T(8,128)(2,1)S(1)}, u32[]{:S(2)}, u32[]{:S(2)}) collective-permute-start(bf16[2,16,1280]{2,1,0:T(8,128)(2,1)S(1)} %first_rows.1.refs_0_), channel_id=1, source_target_pairs={{0,12},{2,14},{4,0},{6,2},{8,4},{10,6},{12,8},{14,10},{1,13},{3,15... | collective-permute-start | bytes 245768 | tf_op jit(solution)/shard_map/gather_first/ppermute | solution.py:32
  10.8 3.1 %copy-start.5 = (bf16[1,2,16,1280]{3,2,1,0:T(8,128)(2,1)S(1)}, bf16[1,2,16,1280]{3,2,1,0:T(8,128)(2,1)}, u32[]{:S(2)}) copy-start(bf16[1,2,16,1280]{3,2,1,0:T(8,128)(2,1)} %param.19) | copy-start | bytes 245764
  10.8 4.2 %copy-start = (bf16[1,1280]{1,0:T(2,128)(2,1)S(1)}, bf16[1,1280]{1,0:T(2,128)(2,1)}, u32[]{:S(2)}) copy-start(bf16[1,1280]{1,0:T(2,128)(2,1)} %gain.17) | copy-start | bytes 7684
  13.3 4.1 %collective-permute-start.3 = (bf16[64,1280]{1,0:T(8,128)(2,1)S(1)}, bf16[64,1280]{1,0:T(8,128)(2,1)S(1)}, u32[]{:S(2)}, u32[]{:S(2)}) collective-permute-start(bf16[64,1280]{1,0:T(8,128)(2,1)S(1)} %pad_maximum_fusion.1.low.other_low), channel_id=1, source_target_pairs={{0,2},{2,0},{4,6},{6,4},{8,10},{10,8},{12,14},{14,12},{1,3},{3,1},... | collective-permute-start | bytes 491528 | tf_op jit(solution)/shard_map/gather_first/ppermute | solution.py:27
  13.4 1.6 %collective-permute-start.4 = (bf16[64,1280]{1,0:T(8,128)(2,1)S(1)}, bf16[64,1280]{1,0:T(8,128)(2,1)S(1)}, u32[]{:S(2)}, u32[]{:S(2)}) collective-permute-start(bf16[64,1280]{1,0:T(8,128)(2,1)S(1)} %pad_maximum_fusion.2.low.refs_0_), channel_id=1, source_target_pairs={{0,2},{2,0},{4,6},{6,4},{8,10},{10,8},{12,14},{14,12},{1,3},{3,1},... | collective-permute-start | bytes 491528 | tf_op jit(solution)/shard_map/gather_first/ppermute | solution.py:27
  15.8 18.1 %collective-permute-start.6 = (bf16[128,1920]{1,0:T(8,128)(2,1)S(1)}, bf16[128,1920]{1,0:T(8,128)(2,1)S(1)}, u32[]{:S(2)}, u32[]{:S(2)}) collective-permute-start(bf16[128,1920]{1,0:T(8,128)(2,1)S(1)} %products.2.refs_0_.back_own), channel_id=1, source_target_pairs={{0,1},{1,0},{2,3},{3,2},{4,5},{5,4},{6,7},{7,6},{8,9},{9,8},{10,11... | collective-permute-start | bytes 1474568 | tf_op jit(solution)/shard_map/swap_back/ppermute | solution.py:84
  19.7 1.6 %copy-start.3 = (bf16[1,16,1280]{2,1,0:T(8,128)(2,1)S(1)}, bf16[1,16,1280]{2,1,0:T(8,128)(2,1)}, u32[]{:S(2)}) copy-start(bf16[1,16,1280]{2,1,0:T(8,128)(2,1)} %param.14) | copy-start | bytes 122884
  19.7 1.6 %copy-start.4 = (bf16[1,16,1280]{2,1,0:T(8,128)(2,1)S(1)}, bf16[1,16,1280]{2,1,0:T(8,128)(2,1)}, u32[]{:S(2)}) copy-start(bf16[1,16,1280]{2,1,0:T(8,128)(2,1)} %param.16) | copy-start | bytes 122884
  19.7 1.6 %copy-start.6 = (bf16[1,16,1280]{2,1,0:T(8,128)(2,1)S(1)}, bf16[1,16,1280]{2,1,0:T(8,128)(2,1)}, u32[]{:S(2)}) copy-start(bf16[1,16,1280]{2,1,0:T(8,128)(2,1)} %param.17) | copy-start | bytes 122884
  19.7 1.5 %copy-start.7 = (bf16[1,16,1280]{2,1,0:T(8,128)(2,1)S(1)}, bf16[1,16,1280]{2,1,0:T(8,128)(2,1)}, u32[]{:S(2)}) copy-start(bf16[1,16,1280]{2,1,0:T(8,128)(2,1)} %param.15) | copy-start | bytes 122884
  21.3 8.1 %collective-permute-start.7 = (bf16[3,16,1280]{2,1,0:T(8,128)(2,1)S(1)}, bf16[3,16,1280]{2,1,0:T(8,128)(2,1)S(1)}, u32[]{:S(2)}, u32[]{:S(2)}) collective-permute-start(bf16[3,16,1280]{2,1,0:T(8,128)(2,1)S(1)} %pad_maximum_fusion.7), channel_id=1, source_target_pairs={{0,4},{2,6},{4,8},{6,10},{8,12},{10,14},{12,0},{14,2},{1,5},{3,7},... | collective-permute-start | bytes 368648 | tf_op jit(solution)/shard_map/gather_others/ppermute | solution.py:32
  23.0 10.8 %collective-permute-start.8 = (bf16[3,16,1280]{2,1,0:T(8,128)(2,1)S(1)}, bf16[3,16,1280]{2,1,0:T(8,128)(2,1)S(1)}, u32[]{:S(2)}, u32[]{:S(2)}) collective-permute-start(bf16[3,16,1280]{2,1,0:T(8,128)(2,1)S(1)} %pad_maximum_fusion.7), channel_id=1, source_target_pairs={{0,8},{2,10},{4,12},{6,14},{8,0},{10,2},{12,4},{14,6},{1,9},{3,11}... | collective-permute-start | bytes 368648 | tf_op jit(solution)/shard_map/gather_others/ppermute | solution.py:32
  24.9 9.0 %collective-permute-start.9 = (bf16[3,16,1280]{2,1,0:T(8,128)(2,1)S(1)}, bf16[3,16,1280]{2,1,0:T(8,128)(2,1)S(1)}, u32[]{:S(2)}, u32[]{:S(2)}) collective-permute-start(bf16[3,16,1280]{2,1,0:T(8,128)(2,1)S(1)} %pad_maximum_fusion.7), channel_id=1, source_target_pairs={{0,12},{2,14},{4,0},{6,2},{8,4},{10,6},{12,8},{14,10},{1,13},{3,15... | collective-permute-start | bytes 368648 | tf_op jit(solution)/shard_map/gather_others/ppermute | solution.py:32
  25.5 14.4 %collective-permute-start.5 = (bf16[128,1920]{1,0:T(8,128)(2,1)S(1)}, bf16[128,1920]{1,0:T(8,128)(2,1)S(1)}, u32[]{:S(2)}, u32[]{:S(2)}) collective-permute-start(bf16[128,1920]{1,0:T(8,128)(2,1)S(1)} %get-tuple-element.65.own), channel_id=1, source_target_pairs={{0,1},{1,0},{2,3},{3,2},{4,5},{5,4},{6,7},{7,6},{8,9},{9,8},{10,11... | collective-permute-start | bytes 1474568 | tf_op jit(solution)/shard_map/swap_chain0/ppermute | solution.py:84
  33.9 1.5 %collective-permute-start.10 = (bf16[64,1280]{1,0:T(8,128)(2,1)S(1)}, bf16[64,1280]{1,0:T(8,128)(2,1)S(1)}, u32[]{:S(2)}, u32[]{:S(2)}) collective-permute-start(bf16[64,1280]{1,0:T(8,128)(2,1)S(1)} %pad_maximum_fusion.3.low.refs_5_), channel_id=1, source_target_pairs={{0,2},{2,0},{4,6},{6,4},{8,10},{10,8},{12,14},{14,12},{1,3},{3,1},... | collective-permute-start | bytes 491528 | tf_op jit(solution)/shard_map/gather_others/ppermute | solution.py:27
  34.0 1.6 %collective-permute-start.11 = (bf16[64,1280]{1,0:T(8,128)(2,1)S(1)}, bf16[64,1280]{1,0:T(8,128)(2,1)S(1)}, u32[]{:S(2)}, u32[]{:S(2)}) collective-permute-start(bf16[64,1280]{1,0:T(8,128)(2,1)S(1)} %pad_maximum_fusion.4.grad_low.refs_9_), channel_id=1, source_target_pairs={{0,2},{2,0},{4,6},{6,4},{8,10},{10,8},{12,14},{14,12},{1,3},{3,1},... | collective-permute-start | bytes 491528 | tf_op jit(solution)/shard_map/gather_others/ppermute | solution.py:27
  40.9 2.2 %collective-permute-start.12 = (bf16[64,1280]{1,0:T(8,128)(2,1)S(1)}, bf16[64,1280]{1,0:T(8,128)(2,1)S(1)}, u32[]{:S(2)}, u32[]{:S(2)}) collective-permute-start(bf16[64,1280]{1,0:T(8,128)(2,1)S(1)} %get-tuple-element.76), channel_id=1, source_target_pairs={{0,2},{2,0},{4,6},{6,4},{8,10},{10,8},{12,14},{14,12},{1,3},{3,1},... | collective-permute-start | bytes 491528 | tf_op jit(solution)/shard_map/chain0/ppermute | solution.py:27
  41.0 6.2 %collective-permute-start.23 = (bf16[64,1280]{1,0:T(8,128)(2,1)S(1)}, bf16[64,1280]{1,0:T(8,128)(2,1)S(1)}, u32[]{:S(2)}, u32[]{:S(2)}) collective-permute-start(bf16[64,1280]{1,0:T(8,128)(2,1)S(1)} %pad_maximum_fusion.6.low), channel_id=1, source_target_pairs={{0,2},{2,0},{4,6},{6,4},{8,10},{10,8},{12,14},{14,12},{1,3},{3,1},... | collective-permute-start | bytes 491528 | tf_op jit(solution)/shard_map/gather_others/ppermute | solution.py:27
  41.6 23.9 %collective-permute-start.21 = (bf16[128,3712]{1,0:T(8,128)(2,1)S(1)}, bf16[128,3712]{1,0:T(8,128)(2,1)S(1)}, u32[]{:S(2)}, u32[]{:S(2)}) collective-permute-start(bf16[128,3712]{1,0:T(8,128)(2,1)S(1)} %products_and_act_grads.1.refs_0_.own), channel_id=1, source_target_pairs={{0,1},{1,0},{2,3},{3,2},{4,5},{5,4},{6,7},{7,6},{8,9},{9,8},{10,11... | collective-permute-start | bytes 2850824 | tf_op jit(solution)/shard_map/swap_off_back/ppermute | solution.py:84
  43.1 5.9 %collective-permute-start.15 = (bf16[16,1280]{1,0:T(8,128)(2,1)S(1)}, bf16[16,1280]{1,0:T(8,128)(2,1)S(1)}, u32[]{:S(2)}, u32[]{:S(2)}) collective-permute-start(bf16[16,1280]{1,0:T(8,128)(2,1)S(1)} %get-tuple-element.121), channel_id=1, source_target_pairs={{0,4},{2,6},{4,8},{6,10},{8,12},{10,14},{12,0},{14,2},{1,5},{3,7},... | collective-permute-start | bytes 122888 | tf_op jit(solution)/shard_map/chain0/ppermute | solution.py:32
  44.8 5.6 %collective-permute-start.14 = (bf16[16,1280]{1,0:T(8,128)(2,1)S(1)}, bf16[16,1280]{1,0:T(8,128)(2,1)S(1)}, u32[]{:S(2)}, u32[]{:S(2)}) collective-permute-start(bf16[16,1280]{1,0:T(8,128)(2,1)S(1)} %get-tuple-element.122), channel_id=1, source_target_pairs={{0,8},{2,10},{4,12},{6,14},{8,0},{10,2},{12,4},{14,6},{1,9},{3,11}... | collective-permute-start | bytes 122888 | tf_op jit(solution)/shard_map/chain0/ppermute | solution.py:32
  46.7 4.2 %collective-permute-start.13 = (bf16[16,1280]{1,0:T(8,128)(2,1)S(1)}, bf16[16,1280]{1,0:T(8,128)(2,1)S(1)}, u32[]{:S(2)}, u32[]{:S(2)}) collective-permute-start(bf16[16,1280]{1,0:T(8,128)(2,1)S(1)} %get-tuple-element.120), channel_id=1, source_target_pairs={{0,12},{2,14},{4,0},{6,2},{8,4},{10,6},{12,8},{14,10},{1,13},{3,15... | collective-permute-start | bytes 122888 | tf_op jit(solution)/shard_map/chain0/ppermute | solution.py:32
  48.0 28.0 %collective-permute-start.24 = (bf16[128,1920]{1,0:T(8,128)(2,1)S(1)}, bf16[128,1920]{1,0:T(8,128)(2,1)S(1)}, u32[]{:S(2)}, u32[]{:S(2)}) collective-permute-start(bf16[128,1920]{1,0:T(8,128)(2,1)S(1)} %products.3.own), channel_id=1, source_target_pairs={{0,1},{1,0},{2,3},{3,2},{4,5},{5,4},{6,7},{7,6},{8,9},{9,8},{10,11... | collective-permute-start | bytes 1474568 | tf_op jit(solution)/shard_map/swap_off_forward/ppermute | solution.py:84
  50.8 6.0 %collective-permute-start.19 = (bf16[1,16,1280]{2,1,0:T(8,128)(2,1)S(1)}, bf16[1,16,1280]{2,1,0:T(8,128)(2,1)S(1)}, u32[]{:S(2)}, u32[]{:S(2)}) collective-permute-start(bf16[1,16,1280]{2,1,0:T(8,128)(2,1)S(1)} %bitcast.105), channel_id=1, source_target_pairs={{0,28},{2,30},{4,16},{6,18},{8,20},{10,22},{12,24},{14,26},{16,12}... | collective-permute-start | bytes 122888 | tf_op jit(solution)/shard_map/pass/ppermute | solution.py:50
  55.2 5.9 %collective-permute-start.18 = (bf16[1,16,1280]{2,1,0:T(8,128)(2,1)S(1)}, bf16[1,16,1280]{2,1,0:T(8,128)(2,1)S(1)}, u32[]{:S(2)}, u32[]{:S(2)}) collective-permute-start(bf16[1,16,1280]{2,1,0:T(8,128)(2,1)S(1)} %bitcast.106), channel_id=1, source_target_pairs={{0,24},{2,26},{4,28},{6,30},{8,16},{10,18},{12,20},{14,22},{16,8},... | collective-permute-start | bytes 122888 | tf_op jit(solution)/shard_map/pass/ppermute | solution.py:50
  55.2 6.7 %collective-permute-start.17 = (bf16[1,16,1280]{2,1,0:T(8,128)(2,1)S(1)}, bf16[1,16,1280]{2,1,0:T(8,128)(2,1)S(1)}, u32[]{:S(2)}, u32[]{:S(2)}) collective-permute-start(bf16[1,16,1280]{2,1,0:T(8,128)(2,1)S(1)} %bitcast.107), channel_id=1, source_target_pairs={{0,20},{2,22},{4,24},{6,26},{8,28},{10,30},{12,16},{14,18},{16,4},... | collective-permute-start | bytes 122888 | tf_op jit(solution)/shard_map/pass/ppermute | solution.py:50
  56.8 5.0 %collective-permute-start.16 = (bf16[1,16,1280]{2,1,0:T(8,128)(2,1)S(1)}, bf16[1,16,1280]{2,1,0:T(8,128)(2,1)S(1)}, u32[]{:S(2)}, u32[]{:S(2)}) collective-permute-start(bf16[1,16,1280]{2,1,0:T(8,128)(2,1)S(1)} %bitcast.108), channel_id=1, source_target_pairs={{0,16},{2,18},{4,20},{6,22},{8,24},{10,26},{12,28},{14,30},{16,0},... | collective-permute-start | bytes 122888 | tf_op jit(solution)/shard_map/pass/ppermute | solution.py:50
  61.9 5.8 %collective-permute-start.20 = (bf16[64,1280]{1,0:T(8,128)(2,1)S(1)}, bf16[64,1280]{1,0:T(8,128)(2,1)S(1)}, u32[]{:S(2)}, u32[]{:S(2)}) collective-permute-start(bf16[64,1280]{1,0:T(8,128)(2,1)S(1)} %pad_maximum_fusion.5.low), channel_id=1, source_target_pairs={{0,2},{2,0},{4,6},{6,4},{8,10},{10,8},{12,14},{14,12},{1,3},{3,1},... | collective-permute-start | bytes 491528 | tf_op jit(solution)/shard_map/pass/ppermute | solution.py:27
  67.6 9.5 %collective-permute-start.22 = (bf16[64,1280]{1,0:T(8,128)(2,1)S(1)}, bf16[64,1280]{1,0:T(8,128)(2,1)S(1)}, u32[]{:S(2)}, u32[]{:S(2)}) collective-permute-start(bf16[64,1280]{1,0:T(8,128)(2,1)S(1)} %get-tuple-element.79), channel_id=1, source_target_pairs={{0,2},{2,0},{4,6},{6,4},{8,10},{10,8},{12,14},{14,12},{1,3},{3,1},... | collective-permute-start | bytes 491528 | tf_op jit(solution)/shard_map/off_back/ppermute | solution.py:27
  69.5 16.2 %collective-permute-start.29 = (bf16[128,1920]{1,0:T(8,128)(2,1)S(1)}, bf16[128,1920]{1,0:T(8,128)(2,1)S(1)}, u32[]{:S(2)}, u32[]{:S(2)}) collective-permute-start(bf16[128,1920]{1,0:T(8,128)(2,1)S(1)} %get-tuple-element.83.refs_0_.own), channel_id=1, source_target_pairs={{0,1},{1,0},{2,3},{3,2},{4,5},{5,4},{6,7},{7,6},{8,9},{9,8},{10,11... | collective-permute-start | bytes 1474568 | tf_op jit(solution)/shard_map/swap_chain1/ppermute | solution.py:84
  77.1 1.5 %collective-permute-start.25 = (bf16[64,1280]{1,0:T(8,128)(2,1)S(1)}, bf16[64,1280]{1,0:T(8,128)(2,1)S(1)}, u32[]{:S(2)}, u32[]{:S(2)}) collective-permute-start(bf16[64,1280]{1,0:T(8,128)(2,1)S(1)} %get-tuple-element.85), channel_id=1, source_target_pairs={{0,2},{2,0},{4,6},{6,4},{8,10},{10,8},{12,14},{14,12},{1,3},{3,1},... | collective-permute-start | bytes 491528 | tf_op jit(solution)/shard_map/off_forward/ppermute | solution.py:27
  78.6 9.2 %collective-permute-start.26 = (bf16[2,16,1280]{2,1,0:T(8,128)(2,1)S(1)}, bf16[2,16,1280]{2,1,0:T(8,128)(2,1)S(1)}, u32[]{:S(2)}, u32[]{:S(2)}) collective-permute-start(bf16[2,16,1280]{2,1,0:T(8,128)(2,1)S(1)} %get-tuple-element.113), channel_id=1, source_target_pairs={{0,12},{2,14},{4,0},{6,2},{8,4},{10,6},{12,8},{14,10},{1,13},{3,15... | collective-permute-start | bytes 245768 | tf_op jit(solution)/shard_map/off_forward/ppermute | solution.py:32
  81.6 8.0 %collective-permute-start.27 = (bf16[2,16,1280]{2,1,0:T(8,128)(2,1)S(1)}, bf16[2,16,1280]{2,1,0:T(8,128)(2,1)S(1)}, u32[]{:S(2)}, u32[]{:S(2)}) collective-permute-start(bf16[2,16,1280]{2,1,0:T(8,128)(2,1)S(1)} %get-tuple-element.112), channel_id=1, source_target_pairs={{0,8},{2,10},{4,12},{6,14},{8,0},{10,2},{12,4},{14,6},{1,9},{3,11}... | collective-permute-start | bytes 245768 | tf_op jit(solution)/shard_map/off_forward/ppermute | solution.py:32
  81.8 7.8 %collective-permute-start.28 = (bf16[2,16,1280]{2,1,0:T(8,128)(2,1)S(1)}, bf16[2,16,1280]{2,1,0:T(8,128)(2,1)S(1)}, u32[]{:S(2)}, u32[]{:S(2)}) collective-permute-start(bf16[2,16,1280]{2,1,0:T(8,128)(2,1)S(1)} %get-tuple-element.111), channel_id=1, source_target_pairs={{0,4},{2,6},{4,8},{6,10},{8,12},{10,14},{12,0},{14,2},{1,5},{3,7},... | collective-permute-start | bytes 245768 | tf_op jit(solution)/shard_map/off_forward/ppermute | solution.py:32
  87.8 17.8 %copy-start.1 = (f32[1,1,1,6,128,128]{5,4,3,2,1,0:T(8,128)S(1)}, f32[1,1,1,6,128,128]{5,4,3,2,1,0:T(8,128)}, u32[]{:S(2)}) copy-start(f32[1,1,1,6,128,128]{5,4,3,2,1,0:T(8,128)} %param.26) | copy-start | bytes 1179652
  87.8 17.8 %copy-start.2 = (f32[1,1,1,6,128,128]{5,4,3,2,1,0:T(8,128)S(1)}, f32[1,1,1,6,128,128]{5,4,3,2,1,0:T(8,128)}, u32[]{:S(2)}) copy-start(f32[1,1,1,6,128,128]{5,4,3,2,1,0:T(8,128)} %param.27) | copy-start | bytes 1179652
  89.6 2.7 %collective-permute-start.30 = (bf16[64,1280]{1,0:T(8,128)(2,1)S(1)}, bf16[64,1280]{1,0:T(8,128)(2,1)S(1)}, u32[]{:S(2)}, u32[]{:S(2)}) collective-permute-start(bf16[64,1280]{1,0:T(8,128)(2,1)S(1)} %get-tuple-element.93), channel_id=1, source_target_pairs={{0,2},{2,0},{4,6},{6,4},{8,10},{10,8},{12,14},{14,12},{1,3},{3,1},... | collective-permute-start | bytes 491528 | tf_op jit(solution)/shard_map/chain1/ppermute | solution.py:27
  91.8 4.5 %collective-permute-start.34 = (bf16[4,128,128]{2,1,0:T(8,128)(2,1)S(1)}, bf16[4,128,128]{2,1,0:T(8,128)(2,1)S(1)}, u32[]{:S(2)}, u32[]{:S(2)}) collective-permute-start(bf16[4,128,128]{2,1,0:T(8,128)(2,1)S(1)} %slice.206), channel_id=1, source_target_pairs={{0,2},{2,0},{4,6},{6,4},{8,10},{10,8},{12,14},{14,12},{1,3},{3,1},... | collective-permute-start | bytes 393224 | tf_op jit(solution)/shard_map/block_exchange/ppermute | solution.py:27
  92.4 6.4 %collective-permute-start.31 = (bf16[16,1280]{1,0:T(8,128)(2,1)S(1)}, bf16[16,1280]{1,0:T(8,128)(2,1)S(1)}, u32[]{:S(2)}, u32[]{:S(2)}) collective-permute-start(bf16[16,1280]{1,0:T(8,128)(2,1)S(1)} %get-tuple-element.119), channel_id=1, source_target_pairs={{0,12},{2,14},{4,0},{6,2},{8,4},{10,6},{12,8},{14,10},{1,13},{3,15... | collective-permute-start | bytes 122888 | tf_op jit(solution)/shard_map/chain1/ppermute | solution.py:32
  93.7 6.0 %collective-permute-start.32 = (bf16[16,1280]{1,0:T(8,128)(2,1)S(1)}, bf16[16,1280]{1,0:T(8,128)(2,1)S(1)}, u32[]{:S(2)}, u32[]{:S(2)}) collective-permute-start(bf16[16,1280]{1,0:T(8,128)(2,1)S(1)} %get-tuple-element.118), channel_id=1, source_target_pairs={{0,8},{2,10},{4,12},{6,14},{8,0},{10,2},{12,4},{14,6},{1,9},{3,11}... | collective-permute-start | bytes 122888 | tf_op jit(solution)/shard_map/chain1/ppermute | solution.py:32
  94.4 6.3 %collective-permute-start.33 = (bf16[16,1280]{1,0:T(8,128)(2,1)S(1)}, bf16[16,1280]{1,0:T(8,128)(2,1)S(1)}, u32[]{:S(2)}, u32[]{:S(2)}) collective-permute-start(bf16[16,1280]{1,0:T(8,128)(2,1)S(1)} %get-tuple-element.117), channel_id=1, source_target_pairs={{0,4},{2,6},{4,8},{6,10},{8,12},{10,14},{12,0},{14,2},{1,5},{3,7},... | collective-permute-start | bytes 122888 | tf_op jit(solution)/shard_map/chain1/ppermute | solution.py:32
  96.3 5.0 %collective-permute-start.35 = (bf16[256,128]{1,0:T(8,128)(2,1)S(1)}, bf16[256,128]{1,0:T(8,128)(2,1)S(1)}, u32[]{:S(2)}, u32[]{:S(2)}) collective-permute-start(bf16[256,128]{1,0:T(8,128)(2,1)S(1)} %pad_maximum_fusion.8), channel_id=1, source_target_pairs={{0,12},{2,14},{4,0},{6,2},{8,4},{10,6},{12,8},{14,10},{1,13},{3,15... | collective-permute-start | bytes 196616 | tf_op jit(solution)/shard_map/block_exchange/ppermute | solution.py:32
  98.3 7.3 %collective-permute-start.36 = (bf16[256,128]{1,0:T(8,128)(2,1)S(1)}, bf16[256,128]{1,0:T(8,128)(2,1)S(1)}, u32[]{:S(2)}, u32[]{:S(2)}) collective-permute-start(bf16[256,128]{1,0:T(8,128)(2,1)S(1)} %pad_maximum_fusion.9), channel_id=1, source_target_pairs={{0,8},{2,10},{4,12},{6,14},{8,0},{10,2},{12,4},{14,6},{1,9},{3,11}... | collective-permute-start | bytes 196616 | tf_op jit(solution)/shard_map/block_exchange/ppermute | solution.py:32
  98.8 6.8 %collective-permute-start.37 = (bf16[256,128]{1,0:T(8,128)(2,1)S(1)}, bf16[256,128]{1,0:T(8,128)(2,1)S(1)}, u32[]{:S(2)}, u32[]{:S(2)}) collective-permute-start(bf16[256,128]{1,0:T(8,128)(2,1)S(1)} %pad_maximum_fusion.10), channel_id=1, source_target_pairs={{0,4},{2,6},{4,8},{6,10},{8,12},{10,14},{12,0},{14,2},{1,5},{3,7},... | collective-permute-start | bytes 196616 | tf_op jit(solution)/shard_map/block_exchange/ppermute | solution.py:32
